TPU v7x, 32 devices: a whole 2x2x4 slice. The times are simulated.
32 devices in a mesh: seq: 8 (over z, y), head: 4 (over x, core).
Axes of the slice: x: 2, y: 2, z: 4, core: 2. Of those that a mesh axis runs over, the one named last changes fastest.
Arguments:
- tokens: bfloat16 [2, 16384, 768], P(None, 'seq'), may hold values from -6 to 6
- doc_starts: int32 [2, 8], replicated, may hold values from 0 to 16383, as said below
- norm_gain: float32 [768], replicated, may hold values from 0.5 to 1.5
- gate_x_weight: bfloat16 [768, 2, 1536], P(None, None, 'head'), may hold values from -0.21875 to 0.21875
- bc_weight: bfloat16 [768, 256], replicated, may hold values from -0.21875 to 0.21875
- dt_weight: bfloat16 [768, 24], P(None, 'head'), may hold values from -0.21875 to 0.21875
- conv_x_weight: float32 [4, 1536], P(None, 'head'), may hold values from -3 to 3
- conv_x_bias: float32 [1536], P('head'), may hold values from -0.5 to 0.5
- conv_bc_weight: float32 [4, 256], replicated, may hold values from -3 to 3
- conv_bc_bias: float32 [256], replicated, may hold values from -0.5 to 0.5
- dt_bias: float32 [24], P('head'), may hold values from -6 to -4.5
- a_log: float32 [24], P('head'), may hold values from -8 to 3
- d_skip: float32 [24], P('head'), may hold values from 0.5 to 2
- gate_gain: float32 [1536], P('head'), may hold values from 0.5 to 1.5
- out_weight: bfloat16 [1536, 768], P('head'), may hold values from -0.15625 to 0.15625
- cotangent: bfloat16 [2, 16384, 768], P(None, 'seq'), may hold values from -6 to 6
Outputs:
- mixed_out: bfloat16 [2, 16384, 768], P(None, 'seq')
- token_grad: bfloat16 [2, 16384, 768], P(None, 'seq')
- grad_norm_gain: float32 [768], replicated
- grad_gate_x: float32 [768, 2, 1536], P(None, None, 'head')
- grad_bc: float32 [768, 256], P(None, 'head')
- grad_dt: float32 [768, 24], P(None, 'head')
- grad_conv_x: float32 [4, 1536], P(None, 'head')
- grad_conv_x_bias: float32 [1536], P('head')
- grad_conv_bc: float32 [4, 256], replicated
- grad_conv_bc_bias: float32 [256], replicated
- grad_dt_bias: float32 [24], P('head')
- grad_a_log: float32 [24], P('head')
- grad_d_skip: float32 [24], P('head')
- grad_gate_gain: float32 [1536], P('head')
- grad_out: float32 [1536, 768], P('head')
Inputs may be any that keep to these rules, and one draw needn't show every extreme that they name: `doc_starts`: document start positions of each micro-batch, in no order and possibly repeated; an entry 0 starts nothing. In one micro-batch, drawn from the seed, every entry is 0, so that one document covers the whole sequence; another micro-batch has a start at 16383.
All inputs are finite; a program needn't handle non-finite values.
Results may differ from a plain program's by a relative error of at most 0.012.
The roundings to bfloat16 on the way count: a program that leaves them out, or rounds other values in their place, can miss the bound.
Values may be sent and summed in bfloat16 or wider, within the bound.
No kernel may reach another device: no remote copies, remote signals or barrier semaphores. Data moves between devices by JAX's collectives and lax.ppermute only.
A program may use at most 384 MiB of HBM per device.

v0:
```python
from functools import partial

import jax
import jax.numpy as jnp
from jax import lax
from jax.sharding import PartitionSpec as P

GROUP = 256


HIGHEST = lax.Precision.HIGHEST
EPSILON = 1e-05


def from_behind(value, axis, steps):
    count = lax.axis_size(axis)
    leading, last = (max(0, -steps), min(count, count - steps))
    return lax.ppermute(value, axis, [(source, source + steps) for source in range(leading, last)])


def start_counts(doc_starts, places):
    hits = (doc_starts[:, None, :] >= 1) & (doc_starts[:, None, :] <= places[None, :, None])
    return jnp.sum(hits.astype(jnp.int32), axis=2)


def silu_slope(values):
    sigma_v = jax.nn.sigmoid(values)
    return sigma_v * (1.0 + values * (1.0 - sigma_v))


def group_step(states, inputs_x, writes, reads, deltas, decay_rate, counts, before):
    running = jnp.cumsum(deltas * decay_rate[None, :], axis=0)
    positions = jnp.arange(counts.shape[0])
    allowed = (counts[:, None] == counts[None, :]) & (positions[:, None] >= positions[None, :])
    allowed = allowed[:, :, None]
    spread = running[:, None, :] - running[None, :, :]
    weights = jnp.where(allowed, jnp.exp(jnp.where(allowed, spread, 0.0)), 0.0)
    scores = jnp.dot(reads, writes.T, precision=HIGHEST)
    scaled = inputs_x * deltas[:, :, None]
    within = jnp.einsum("tsh,shp->thp", weights * scores[:, :, None], scaled, precision=HIGHEST)
    entry_scale = jnp.exp(running) * (counts == before).astype(running.dtype)[:, None]
    carried = jnp.einsum("tn,hpn->thp", reads, states, precision=HIGHEST) * entry_scale[:, :, None]
    leaving = (
        jnp.exp(running[-1][None, :] - running)
        * (counts == counts[-1]).astype(running.dtype)[:, None]
    )
    newest = jnp.einsum("sh,shp,sn->hpn", leaving, scaled, writes, precision=HIGHEST)
    overall = jnp.exp(running[-1]) * (counts[-1] == before).astype(running.dtype)
    return (states * overall[:, None, None] + newest, within + carried)


def scan_groups(states, inputs_x, writes, reads, deltas, decay_rate, counts, before):
    blocks = inputs_x.shape[0] // GROUP
    befores = jnp.concatenate([jnp.reshape(before, (1,)), counts[GROUP - 1 :: GROUP][:-1]])

    def block_step(carry_states, pieces):
        return group_step(
            carry_states,
            pieces[0],
            pieces[1],
            pieces[2],
            pieces[3],
            decay_rate,
            pieces[4],
            pieces[5],
        )

    pieces = (
        inputs_x.reshape((blocks, GROUP) + inputs_x.shape[1:]),
        writes.reshape(blocks, GROUP, -1),
        reads.reshape(blocks, GROUP, -1),
        deltas.reshape(blocks, GROUP, -1),
        counts.reshape(blocks, GROUP),
        befores,
    )
    last_states, outputs = lax.scan(block_step, states, pieces)
    return (last_states, outputs.reshape((blocks * GROUP,) + outputs.shape[2:]))


def local_part(inputs_x, writes, reads, deltas, decay_rate, counts, before):

    def single(inputs_one, writes_one, reads_one, deltas_one, counts_one, before_one):
        zero_states = jnp.zeros(
            (inputs_one.shape[1], inputs_one.shape[2], writes_one.shape[1]), jnp.float32
        )
        last_states, outputs = scan_groups(
            zero_states,
            inputs_one,
            writes_one,
            reads_one,
            deltas_one,
            decay_rate,
            counts_one,
            before_one,
        )
        overall = jnp.exp(jnp.sum(deltas_one * decay_rate[None, :], axis=0)) * (
            counts_one[-1] == before_one
        ).astype(jnp.float32)
        return (outputs, last_states, overall)

    return jax.vmap(single)(inputs_x, writes, reads, deltas, counts, before)


def carry_part(reads, deltas, decay_rate, carry, counts, before):
    running = jnp.cumsum(deltas * decay_rate[None, None, :], axis=1)
    entry_scale = jnp.exp(running) * (counts == before[:, None]).astype(jnp.float32)[:, :, None]
    return (
        jnp.einsum("mtn,mhpn->mthp", reads, carry, precision=HIGHEST) * entry_scale[:, :, :, None]
    )


def causal_conv(extended, weight, shift_term, tap_masks):
    length = tap_masks[0].shape[1]
    result = jnp.zeros(extended[:, :length].shape, jnp.float32) + shift_term[None, None, :]
    for offset in range(weight.shape[0]):
        result = (
            result
            + weight[offset][None, None, :]
            * extended[:, offset : offset + length]
            * tap_masks[offset][:, :, None]
        )
    return result


def conv_back(extended, weight, tap_masks, grad_pre):
    taps_count = weight.shape[0]
    length = grad_pre.shape[1]
    grad_ext = jnp.zeros_like(extended)
    weight_rows = []
    for offset in range(taps_count):
        masked = grad_pre * tap_masks[offset][:, :, None]
        grad_ext = grad_ext + jnp.pad(
            weight[offset][None, None, :] * masked,
            ((0, 0), (offset, taps_count - 1 - offset), (0, 0)),
        )
        weight_rows.append(jnp.sum(masked * extended[:, offset : offset + length], axis=(0, 1)))
    return (grad_ext, jnp.stack(weight_rows), jnp.sum(grad_pre, axis=(0, 1)))


def norm_input_back(grad_normed, x_float, scale, norm_gain, upstream):
    grad_gain_part = jnp.sum(grad_normed * x_float * scale, axis=0)
    grad_hat = grad_normed * norm_gain
    result = (
        upstream
        + scale * grad_hat
        - x_float * scale**3 * jnp.mean(grad_hat * x_float, axis=1, keepdims=True)
    )
    return (result, grad_gain_part)


def local(
    tokens,
    doc_starts,
    norm_gain,
    gate_x_weight,
    bc_weight,
    dt_weight,
    conv_x_weight,
    conv_x_bias,
    conv_bc_weight,
    conv_bc_bias,
    dt_bias,
    a_log,
    d_skip,
    gate_gain,
    out_weight,
    cotangent,
):
    micro, length, width = tokens.shape
    inner_width = gate_x_weight.shape[2]
    heads = dt_weight.shape[1]
    head_dim = inner_width // heads
    state_dim = bc_weight.shape[1] // 2
    taps_count = conv_x_weight.shape[0]
    rim_rows = taps_count - 1
    full_inner = inner_width * lax.axis_size("head")
    flat_rows = micro * length
    anchor = lax.axis_index("seq") * length
    places = anchor - rim_rows + jnp.arange(length + rim_rows)
    counts_ext = start_counts(doc_starts, places)
    counts = counts_ext[:, rim_rows:]
    before = counts_ext[:, rim_rows - 1]
    tap_masks = [
        (counts_ext[:, offset : offset + length] == counts).astype(jnp.float32)
        for offset in range(taps_count)
    ]
    x_float = tokens.astype(jnp.float32)
    scale = lax.rsqrt(jnp.mean(x_float * x_float, axis=2, keepdims=True) + EPSILON)
    normed = (x_float * scale * norm_gain).astype(jnp.bfloat16)
    gate_x_out = jnp.einsum(
        "mtd,dgc->mtgc", normed, gate_x_weight, preferred_element_type=jnp.float32
    )
    gate_in = gate_x_out[:, :, 0, :]
    x_in = gate_x_out[:, :, 1, :].astype(jnp.bfloat16)
    bc_in = jnp.einsum("mtd,dc->mtc", normed, bc_weight, preferred_element_type=jnp.float32).astype(
        jnp.bfloat16
    )
    dt_in = jnp.einsum("mtd,dh->mth", normed, dt_weight, preferred_element_type=jnp.float32)
    x_rim, bc_rim = from_behind(
        (x_in[:, length - rim_rows :], bc_in[:, length - rim_rows :]), "seq", 1
    )
    x_ext = jnp.concatenate([x_rim, x_in], axis=1).astype(jnp.float32)
    bc_ext = jnp.concatenate([bc_rim, bc_in], axis=1).astype(jnp.float32)
    x_pre = causal_conv(x_ext, conv_x_weight, conv_x_bias, tap_masks)
    bc_pre = causal_conv(bc_ext, conv_bc_weight, conv_bc_bias, tap_masks)
    x_conv = jax.nn.silu(x_pre).astype(jnp.bfloat16).astype(jnp.float32)
    bc_conv = jax.nn.silu(bc_pre).astype(jnp.bfloat16).astype(jnp.float32)
    inputs_x = x_conv.reshape(micro, length, heads, head_dim)
    writes = bc_conv[:, :, :state_dim]
    reads = bc_conv[:, :, state_dim:]
    deltas = jax.nn.softplus(dt_in + dt_bias)
    decay_rate = -jnp.exp(a_log)
    local_fn = partial(local_part, counts=counts, before=before)
    (zero_out, leaving, overall), pull_local = jax.vjp(
        local_fn, inputs_x, writes, reads, deltas, decay_rate
    )

    def relay(index, incoming):
        return from_behind(overall[:, :, None, None] * incoming + leaving, "seq", 1)

    carry = lax.fori_loop(0, lax.axis_size("seq") - 1, relay, jnp.zeros_like(leaving))
    carry_fn = partial(carry_part, counts=counts, before=before)
    carry_out, pull_carry = jax.vjp(carry_fn, reads, deltas, decay_rate, carry)
    ssd_out = (zero_out + carry_out).reshape(micro, length, inner_width)
    skip_scale = jnp.repeat(d_skip, head_dim)
    mixed = ssd_out + x_conv * skip_scale
    gate_act = jax.nn.silu(gate_in)
    gated = mixed * gate_act
    square_sum = lax.psum(jnp.sum(gated * gated, axis=2), "head")
    gate_scale = lax.rsqrt(square_sum[:, :, None] / full_inner + EPSILON)
    branch = (gated * gate_scale * gate_gain).astype(jnp.bfloat16)
    flat_x = x_float.reshape(flat_rows, width)
    branch_part = jnp.einsum("mtc,cd->mtd", branch, out_weight, preferred_element_type=jnp.float32)
    mixed_out = (x_float + lax.psum(branch_part, "head")).astype(jnp.bfloat16)
    grad_branch = jnp.einsum(
        "mtd,cd->mtc", cotangent, out_weight, preferred_element_type=jnp.float32
    )
    grad_out = jnp.einsum("mtc,mtd->cd", branch, cotangent, preferred_element_type=jnp.float32)
    scaled_grad = grad_branch * gate_gain
    grad_gate_gain = jnp.sum(grad_branch * gated * gate_scale, axis=(0, 1))
    inner_sum = lax.psum(jnp.sum(scaled_grad * gated, axis=2), "head")
    grad_gated = (
        gate_scale * scaled_grad - gated * gate_scale**3 * inner_sum[:, :, None] / full_inner
    )
    grad_mixed = grad_gated * gate_act
    grad_gate_in = (grad_gated * mixed * silu_slope(gate_in)).astype(jnp.bfloat16)
    grad_d_skip = jnp.sum(
        (grad_mixed * x_conv).reshape(micro, length, heads, head_dim), axis=(0, 1, 3)
    )
    grad_ssd = (
        lax.optimization_barrier(grad_mixed.astype(jnp.bfloat16))
        .astype(jnp.float32)
        .reshape(micro, length, heads, head_dim)
    )
    grad_reads_c, grad_deltas_c, grad_rate_c, grad_carry = pull_carry(grad_ssd)

    def relay_back(index, incoming):
        return from_behind(grad_carry + overall[:, :, None, None] * incoming, "seq", -1)

    onward = lax.fori_loop(0, lax.axis_size("seq") - 1, relay_back, jnp.zeros_like(grad_carry))
    grad_overall = jnp.sum(onward * carry, axis=(2, 3))
    grad_inputs, grad_writes, grad_reads, grad_deltas, grad_rate = pull_local(
        (grad_ssd, onward, grad_overall)
    )
    grad_reads = grad_reads + grad_reads_c
    grad_deltas = grad_deltas + grad_deltas_c
    grad_rate = grad_rate + grad_rate_c
    grad_x_conv = grad_inputs.reshape(micro, length, inner_width) + grad_mixed * skip_scale
    grad_bc_conv = jnp.concatenate([grad_writes, grad_reads], axis=2)
    grad_x_pre = grad_x_conv * silu_slope(x_pre)
    grad_bc_pre = grad_bc_conv * silu_slope(bc_pre)
    grad_x_ext, grad_conv_x, grad_conv_x_bias = conv_back(
        x_ext, conv_x_weight, tap_masks, grad_x_pre
    )
    grad_bc_ext, grad_conv_bc, grad_conv_bc_bias = conv_back(
        bc_ext, conv_bc_weight, tap_masks, grad_bc_pre
    )
    x_back, bc_back = from_behind((grad_x_ext[:, :rim_rows], grad_bc_ext[:, :rim_rows]), "seq", -1)
    grad_x_in = grad_x_ext[:, rim_rows:] + jnp.pad(x_back, ((0, 0), (length - rim_rows, 0), (0, 0)))
    grad_bc_in = grad_bc_ext[:, rim_rows:] + jnp.pad(
        bc_back, ((0, 0), (length - rim_rows, 0), (0, 0))
    )
    grad_bc_mine = lax.psum_scatter(grad_bc_in, "head", scatter_dimension=2, tiled=True)
    grad_x_low = grad_x_in.astype(jnp.bfloat16)
    grad_bc_low = grad_bc_mine.astype(jnp.bfloat16)
    grad_dt_full = grad_deltas * jax.nn.sigmoid(dt_in + dt_bias)
    grad_dt_bias = jnp.sum(grad_dt_full, axis=(0, 1))
    grad_dt_low = grad_dt_full.astype(jnp.bfloat16)
    grad_a_log = grad_rate * decay_rate
    share = bc_weight.shape[1] // lax.axis_size("head")
    bc_slice = lax.dynamic_slice_in_dim(bc_weight, lax.axis_index("head") * share, share, 1)
    grad_stack = jnp.stack([grad_gate_in, grad_x_low], axis=2)
    grad_normed_part = jnp.einsum(
        "mtgc,dgc->mtd", grad_stack, gate_x_weight, preferred_element_type=jnp.float32
    )
    grad_normed_part = grad_normed_part + jnp.einsum(
        "mtc,dc->mtd", grad_bc_low, bc_slice, preferred_element_type=jnp.float32
    )
    grad_normed_part = grad_normed_part + jnp.einsum(
        "mth,dh->mtd", grad_dt_low, dt_weight, preferred_element_type=jnp.float32
    )
    grad_gate_x = jnp.einsum(
        "mtd,mtgc->dgc", normed, grad_stack, preferred_element_type=jnp.float32
    )
    grad_bc = jnp.einsum("mtd,mtc->dc", normed, grad_bc_low, preferred_element_type=jnp.float32)
    grad_dt = jnp.einsum("mtd,mth->dh", normed, grad_dt_low, preferred_element_type=jnp.float32)
    flat_scale = scale.reshape(flat_rows, 1)
    flat_cot = cotangent.astype(jnp.float32).reshape(flat_rows, width)
    grad_normed = lax.psum(grad_normed_part, "head")
    token_flat, gain_whole = norm_input_back(
        grad_normed.reshape(flat_rows, width), flat_x, flat_scale, norm_gain, flat_cot
    )
    token_out = token_flat.astype(jnp.bfloat16).reshape(micro, length, width)
    grad_norm_gain = gain_whole * (lax.axis_index("head") == 0).astype(jnp.float32)
    summed = lax.psum(
        (
            grad_gate_x,
            grad_bc,
            grad_dt,
            grad_conv_x,
            grad_conv_x_bias,
            grad_dt_bias,
            grad_a_log,
            grad_d_skip,
            grad_gate_gain,
            grad_out,
        ),
        "seq",
    )
    shared = lax.psum((grad_conv_bc, grad_conv_bc_bias, grad_norm_gain), ("seq", "head"))
    return (
        mixed_out,
        token_out,
        shared[2],
        summed[0],
        summed[1],
        summed[2],
        summed[3],
        summed[4],
        shared[0],
        shared[1],
        summed[5],
        summed[6],
        summed[7],
        summed[8],
        summed[9],
    )


def solution(mesh):
    in_specs = (
        P(None, "seq", None),
        P(),
        P(),
        P(None, None, "head"),
        P(),
        P(None, "head"),
        P(None, "head"),
        P("head"),
        P(),
        P(),
        P("head"),
        P("head"),
        P("head"),
        P("head"),
        P("head", None),
        P(None, "seq", None),
    )
    out_specs = (
        P(None, "seq", None),
        P(None, "seq", None),
        P(),
        P(None, None, "head"),
        P(None, "head"),
        P(None, "head"),
        P(None, "head"),
        P("head"),
        P(),
        P(),
        P("head"),
        P("head"),
        P("head"),
        P("head"),
        P("head", None),
    )
    return jax.shard_map(local, mesh=mesh, in_specs=in_specs, out_specs=out_specs, check_vma=False)
```

profile of v0, /device:TPU:0, one launch (start us, length us, event | category | flops | bytes accessed | tf_op | source)
XLA Modules:
  0.0 2038.4 jit_solution(3715232206680371189)
XLA Ops:
  64.8 8.0 fusion.146
  72.8 7.1 copy.536
  104.7 282.2 %while.105 = (s32[]{:T(128)}, f32[2,6,64,128]{3,2,1,0:T(8,128)S(1)}, f32[8,2,256,6,64]{2,4,3,1,0:T(8,128)}, pred[8,2,256,256,6]{3,2,4,1,0:T(32,128)(4,1)}, f32[8...) while((s32[]{:T(128)}, f32[2,6,64,128]{3,2,1,0:T(8,128)S(1)}, ...), condition=%wide.region_5.6_spmd.clone, body=%wide.region_2.5_spmd.clone.sunk | while | flops 1418382336 | bytes 24810980 | solution.py:76
  393.4 82.4 %while.103 = (s32[]{:T(128)}, f32[2,6,64,128]{3,2,1,0:T(8,128)S(1)}, f32[2,6]{1,0:T(2,128)S(1)}, f32[2,6,64,128]{3,2,1,0:T(8,128)S(1)}, s32[]{:T(128)}) while((s32[]{:T(128)}, f32[2,6,64,128]{3,2,1,0:T(8,128)S(1)}, f32[2,6]{1,0:T(2,128)S(1)}, f32[2,6,64,128]{3,2,1,0:T(8,128)S(1)}, s32[]{:T(128)}) %tuple.217), condition=%wide.region_8.9_spmd, body=%wide.region_7.8_spmd.sunk | while | flops 196610 | bytes 2752661 | solution.py:221
  397.1 8.1 collective-permute-done
  410.4 7.2 collective-permute-done
  475.8 8.1 multiply_add_fusion.3
  490.5 9.8 multiply_reduce_fusion.8
  500.3 10.1 psum.119
  510.4 9.4 multiply_reduce_fusion
  519.8 10.5 psum.121
  530.4 14.7 multiply_reduce_fusion.1
  561.9 89.2 %while.104 = (s32[]{:T(128)}, f32[2,6,64,128]{3,2,1,0:T(8,128)S(1)}, f32[2,6]{1,0:T(2,128)S(1)}, f32[2,6,64,128]{3,2,1,0:T(8,128)}, s32[]{:T(128)}) while((s32[]{:T(128)}, f32[2,6,64,128]{3,2,1,0:T(8,128)S(1)}, f32[2,6]{1,0:T(2,128)S(1)}, f32[2,6,64,128]{3,2,1,0:T(8,128)}, s32[]{:T(128)}) %tuple.238), condition=%wide.region_17.18_spmd, body=%wide.region_16.17_spmd.sunk | while | flops 196610 | bytes 2752661 | solution.py:260
  564.4 12.7 collective-permute-done.1
  579.5 12.1 collective-permute-done.1
  593.9 10.5 collective-permute-done.1
  606.9 9.6 collective-permute-done.1
  618.8 9.0 collective-permute-done.1
  630.2 9.3 collective-permute-done.1
  641.9 9.3 collective-permute-done.1
  651.9 8.7 convolution_bitcast_fusion.2
  673.3 489.5 %while.106 = (s32[]{:T(128)}, f32[6]{0:T(128)S(1)}, f32[2,6,64,128]{3,2,1,0:T(8,128)S(1)}, f32[8,2,256,6,64]{2,4,3,1,0:T(8,128)}, f32[8,2,256,128]{3,2,1,0:T(8,1...) while((s32[]{:T(128)}, f32[6]{0:T(128)S(1)}, ...), condition=%wide.region_29.30_spmd.clone, body=%wide.region_18.29_spmd.clone.sunk | while | flops 2827852800 | bytes 32850848 | solution.py:76
  704.1 15.1 reduce-window.74
  765.3 15.1 reduce-window.74
  826.6 15.1 reduce-window.74
  887.7 15.1 reduce-window.74
  948.9 15.1 reduce-window.74
  1010.0 15.1 reduce-window.74
  1071.1 15.1 reduce-window.74
  1132.2 15.1 reduce-window.74
  1164.8 12.4 fusion.155
  1189.5 8.2 pad_add_fusion.1
  1202.2 14.9 reduce-window.62
  1219.4 9.9 copy.565
  1229.3 7.1 reshape.716
  1243.0 21.6 %multiply_reduce_fusion.5 = (f32[384]{0:T(512)}, f32[384]{0:T(512)}, f32[384]{0:T(512)}, f32[384]{0:T(512)}, f32[384]{0:T(512)}, /*index=5*/f32[2,2048,384]{2,1,0:T(8,128)}) fusion(f32[2,2051,384]{2,1,0:T(8,128)} %copy-done.1, f32[2,2048]{1,0:T(2,128)S(1)} %copy-done.35, f32[2,2048]{1,0:T(2,128)S(1)} %copy-done.30, f32[2,2048]{1,0:T(2,128)S(1)} %copy-done.32, ...), kind=kLoop, calls=%fused_computation.224 | loop fusion | flops 34601088 | bytes 50390016 | tf_op jit(solution)/shard_map/reduce_sum | solution.py:136
  1284.2 7.4 copy.571
  1291.6 76.6 %all-reduce.24 = bf16[2,2048,256]{1,0,2:T(2,128)(2,1)} all-reduce(f32[2,2048,256]{1,0,2:T(2,128)} %copy.571), channel_id=2, replica_groups=mesh['seq'=8,'head'=4] {'head'}, use_global_device_ids=true, to_apply=%region_30.31.clone | all-reduce | flops 1048576 | bytes 6291456
  1380.5 6.7 fusion.159
  1389.2 7.2 fusion.187
  1396.4 6.7 fusion.166
  1409.5 15.5 fusion.135
  1429.8 43.1 %all-reduce.14 = (f32[768,6]{0,1:T(8,128)}, f32[4,384]{1,0:T(4,128)}, f32[384]{0:T(512)}, f32[6]{0:T(128)}, f32[6]{0:T(128)}, /*index=5*/f32[6]{0:T(128)}, f32[384]{0:T(512)}) all-reduce(f32[768,6]{0,1:T(8,128)S(1)} %convolution_bitcast_fusion.4, f32[4,384]{1,0:T(4,128)S(1)} %pad_maximum_fusion.5, ...), channel_id=1, replica_groups=mesh['seq'=8,'head'=4] {'seq'}, use_global_device_ids=true, to_apply=%region_41.42 | all-reduce | flops 6930 | bytes 55440 | tf_op jit(solution)/shard_map/psum | solution.py:315
  1472.9 64.6 %all-reduce.21.cloned.1.call-done = (f32[768,2,384]{2,0,1:T(8,128)}, f32[768,64]{0,1:T(8,128)}, f32[384,768]{1,0:T(8,128)}) async-done(((f32[768,2,384]{2,0,1:T(8,128)}, f32[768,64]{0,1:T(8,128)}, f32[384,768]{1,0:T(8,128)}), (f32[768,2,384]{2,0,1:T(8,128)}, f32[768,64]{0,1:T(8,128)}, f32[384,768]{1,0:T(8,128)})) %all-reduce.21.cloned.1.call-update) | async-done | bytes 3735568 | tf_op jit(solution)/shard_map/psum | solution.py:315
  1542.4 420.4 %all-reduce.23.cloned.1.call-done = (f32[2,2048,768]{2,1,0:T(8,128)}, f32[2,2048,768]{2,1,0:T(8,128)}) async-done(((f32[2,2048,768]{2,1,0:T(8,128)}, f32[2,2048,768]{2,1,0:T(8,128)}), (f32[2,2048,768]{2,1,0:T(8,128)}, f32[2,2048,768]{2,1,0:T(8,128)})) %all-reduce.23.cloned.1.call-update) | async-done | bytes 25165840 | tf_op jit(solution)/shard_map/psum | solution.py:234
  1962.8 8.5 fusion.134
  1971.3 39.8 %all-reduce.13 = (f32[768]{0:T(1024)}, f32[4,256]{1,0:T(4,128)}, f32[256]{0:T(256)}) all-reduce(f32[768]{0:T(1024)S(1)} %broadcast_multiply_fusion.4, f32[4,256]{1,0:T(4,128)S(1)} %pad_maximum_fusion.6, f32[256]{0:T(256)S(1)} %copy-done.84), channel_id=1, replica_groups=mesh['seq'=8,'head'=4] {'seq','head'}, use_global_device_ids=true, to_apply=%region_38.39 | all-reduce | flops 2048 | bytes 16384 | tf_op jit(solution)/shard_map/psum | solution.py:330
  2011.1 18.5 fusion.131
  (1139 shorter events, 935.4 us)
Async XLA Ops:
  7.2 503.3 %copy-start = (bf16[384,768]{1,0:T(8,128)(2,1)S(1)}, bf16[384,768]{1,0:T(8,128)(2,1)}, u32[]{:S(2)}) copy-start(bf16[384,768]{1,0:T(8,128)(2,1)} %param.38) | copy-start | bytes 1769476
  7.2 1530.3 %all-reduce.21.cloned.1.call-start = ((), (), s32[]{:S(2)}) async-start(), calls=%async_computation | async-start | bytes 7471104 | tf_op jit(solution)/shard_map/psum | solution.py:315
  12.1 26.7 %copy-start.44 = (f32[2,2048]{1,0:T(2,128)}, f32[2,2048]{1,0:T(2,128)S(1)}, u32[]{:S(2)}) copy-start(f32[2,2048]{1,0:T(2,128)S(1)} %get-tuple-element.2211) | copy-start | bytes 49156
  16.1 36.1 %collective-permute-start.3 = (bf16[2,3,256]{2,1,0:T(4,128)(2,1)}, bf16[2,3,256]{2,1,0:T(4,128)(2,1)}, u32[]{:S(2)}, u32[]{:S(2)}) collective-permute-start(bf16[2,3,256]{2,1,0:T(4,128)(2,1)} %slice.248), channel_id=1, source_target_pairs={{0,4},{4,8},{8,12},{12,16},{16,20},{20,24},{24,28},{1,5},{5,9},{9,... | collective-permute-start | bytes 9224 | tf_op jit(solution)/shard_map/ppermute | solution.py:18
  34.2 28.1 %collective-permute-start.2 = (bf16[2,3,384]{2,1,0:T(4,128)(2,1)}, bf16[2,3,384]{2,1,0:T(4,128)(2,1)}, u32[]{:S(2)}, u32[]{:S(2)}) collective-permute-start(bf16[2,3,384]{2,1,0:T(4,128)(2,1)} %slice.240), channel_id=1, source_target_pairs={{0,4},{4,8},{8,12},{12,16},{16,20},{20,24},{24,28},{1,5},{5,9},{9,... | collective-permute-start | bytes 13832 | tf_op jit(solution)/shard_map/ppermute | solution.py:18
  38.7 26.0 %copy-start.29 = (f32[2,2048]{1,0:T(2,128)}, f32[2,2048]{1,0:T(2,128)S(1)}, u32[]{:S(2)}) copy-start(f32[2,2048]{1,0:T(2,128)S(1)} %get-tuple-element.2205) | copy-start | bytes 49156
  38.7 26.0 %copy-start.31 = (f32[2,2048]{1,0:T(2,128)}, f32[2,2048]{1,0:T(2,128)S(1)}, u32[]{:S(2)}) copy-start(f32[2,2048]{1,0:T(2,128)S(1)} %get-tuple-element.2206) | copy-start | bytes 49156
  38.7 26.0 %copy-start.34 = (f32[2,2048]{1,0:T(2,128)}, f32[2,2048]{1,0:T(2,128)S(1)}, u32[]{:S(2)}) copy-start(f32[2,2048]{1,0:T(2,128)S(1)} %get-tuple-element.2207) | copy-start | bytes 49156
  38.8 25.9 %copy-start.50 = (f32[384]{0:T(512)}, f32[384]{0:T(512)S(1)}, u32[]{:S(2)}) copy-start(f32[384]{0:T(512)S(1)} %get-tuple-element.1987) | copy-start | bytes 4612
  38.8 25.9 %copy-start.52 = (f32[384]{0:T(512)}, f32[384]{0:T(512)S(1)}, u32[]{:S(2)}) copy-start(f32[384]{0:T(512)S(1)} %get-tuple-element.1988) | copy-start | bytes 4612
  38.8 25.9 %copy-start.54 = (f32[384]{0:T(512)}, f32[384]{0:T(512)S(1)}, u32[]{:S(2)}) copy-start(f32[384]{0:T(512)S(1)} %get-tuple-element.1989) | copy-start | bytes 4612
  38.8 25.9 %copy-start.56 = (f32[384]{0:T(512)}, f32[384]{0:T(512)S(1)}, u32[]{:S(2)}) copy-start(f32[384]{0:T(512)S(1)} %get-tuple-element.1990) | copy-start | bytes 4612
  386.9 88.9 %copy-start.9 = (bf16[2,2048,256]{2,1,0:T(8,128)(2,1)S(1)}, bf16[2,2048,256]{2,1,0:T(8,128)(2,1)}, u32[]{:S(2)}) copy-start(bf16[2,2048,256]{2,1,0:T(8,128)(2,1)} %copy-done.8) | copy-start | bytes 6291460
  394.2 11.0 collective-permute-start
  406.1 11.5 collective-permute-start
  418.4 10.6 collective-permute-start
  429.8 10.8 collective-permute-start
  441.4 10.8 collective-permute-start
  453.0 10.9 collective-permute-start
  464.8 11.1 collective-permute-start
  510.4 141.5 %copy-start.37 = (f32[2,2048]{1,0:T(2,128)}, f32[2,2048]{1,0:T(2,128)S(1)}, u32[]{:S(2)}) copy-start(f32[2,2048]{1,0:T(2,128)S(1)} %get-tuple-element.2213) | copy-start | bytes 49156
  563.1 14.0 collective-permute-start.1
  578.2 13.4 collective-permute-start.1
  592.6 11.8 collective-permute-start.1
  605.5 10.9 collective-permute-start.1
  617.5 10.3 collective-permute-start.1
  628.9 10.6 collective-permute-start.1
  640.6 10.6 collective-permute-start.1
  673.3 491.4 %copy-start.19 = (f32[2,2048,6]{1,2,0:T(8,128)S(1)}, f32[2,2048,6]{1,2,0:T(8,128)}, u32[]{:S(2)}) copy-start(f32[2,2048,6]{1,2,0:T(8,128)} %copy.552) | copy-start | bytes 294916
  1197.6 21.2 %copy-start.73 = (f32[2,6]{1,0:T(2,128)S(1)}, f32[2,6]{1,0:T(2,128)}, u32[]{:S(2)}) copy-start(f32[2,6]{1,0:T(2,128)} %copy-done.72) | copy-start | bytes 148
  1197.7 21.1 %copy-start.83 = (f32[2]{0:T(128)S(1)}, f32[2]{0:T(128)}, u32[]{:S(2)}) copy-start(f32[2]{0:T(128)} %copy-done.82) | copy-start | bytes 28
  1243.0 21.6 %copy-start.33 = (f32[2,2048]{1,0:T(2,128)S(1)}, f32[2,2048]{1,0:T(2,128)}, u32[]{:S(2)}) copy-start(f32[2,2048]{1,0:T(2,128)} %copy-done.31) | copy-start | bytes 49156
  1243.0 21.6 %copy-start.36 = (f32[2,2048]{1,0:T(2,128)S(1)}, f32[2,2048]{1,0:T(2,128)}, u32[]{:S(2)}) copy-start(f32[2,2048]{1,0:T(2,128)} %copy-done.34) | copy-start | bytes 49156
  1243.0 21.6 %copy-start.51 = (f32[384]{0:T(512)S(1)}, f32[384]{0:T(512)}, u32[]{:S(2)}) copy-start(f32[384]{0:T(512)} %copy-done.50) | copy-start | bytes 4612
  1243.0 21.6 %copy-start.53 = (f32[384]{0:T(512)S(1)}, f32[384]{0:T(512)}, u32[]{:S(2)}) copy-start(f32[384]{0:T(512)} %copy-done.52) | copy-start | bytes 4612
  1243.0 21.6 %copy-start.55 = (f32[384]{0:T(512)S(1)}, f32[384]{0:T(512)}, u32[]{:S(2)}) copy-start(f32[384]{0:T(512)} %copy-done.54) | copy-start | bytes 4612
  1243.0 21.6 %copy-start.57 = (f32[384]{0:T(512)S(1)}, f32[384]{0:T(512)}, u32[]{:S(2)}) copy-start(f32[384]{0:T(512)} %copy-done.56) | copy-start | bytes 4612
  1270.1 9.7 collective-permute-start.5
  1278.4 96.8 %collective-permute-start.4 = (f32[2,3,384]{2,1,0:T(4,128)}, f32[2,3,384]{2,1,0:T(4,128)S(1)}, u32[]{:S(2)}, u32[]{:S(2)}) collective-permute-start(f32[2,3,384]{2,1,0:T(4,128)} %pad_add_fusion.2), channel_id=1, source_target_pairs={{4,0},{8,4},{12,8},{16,12},{20,16},{24,20},{28,24},{5,1},{9,5},{13... | collective-permute-start | bytes 27656 | tf_op jit(solution)/shard_map/ppermute | solution.py:18
  1284.2 85.5 %copy-start.45 = (f32[2,2048]{1,0:T(2,128)S(1)}, f32[2,2048]{1,0:T(2,128)}, u32[]{:S(2)}) copy-start(f32[2,2048]{1,0:T(2,128)} %copy-done.44) | copy-start | bytes 49156
  1284.2 85.5 %copy-start.61 = (f32[768]{0:T(1024)S(1)}, f32[768]{0:T(1024)}, u32[]{:S(2)}) copy-start(f32[768]{0:T(1024)} %param.26) | copy-start | bytes 9220
  1291.6 88.8 %slice-start.8 = ((s8[6291456]{0:T(1024)(128)(4,1)}), s8[2097152]{0:T(1024)(128)(4,1)S(1)}, s32[]{:S(2)}) async-start(s8[6291456]{0:T(1024)(128)(4,1)} %bitcast.662), calls=%async_computation.10 | async-start | bytes 4194304
  1387.2 575.5 %all-reduce.23.cloned.1.call-start = ((), (), s32[]{:S(2)}) async-start(), calls=%async_computation.1 | async-start | bytes 50331648 | tf_op jit(solution)/shard_map/psum | solution.py:234
  1425.1 47.7 %copy-start.85 = (f32[256]{0:T(256)S(1)}, f32[256]{0:T(256)}, u32[]{:S(2)}) copy-start(f32[256]{0:T(256)} %get-tuple-element.1979) | copy-start | bytes 3076
  1425.1 47.7 %copy-start.86 = (f32[256]{0:T(256)S(1)}, f32[256]{0:T(256)}, u32[]{:S(2)}) copy-start(f32[256]{0:T(256)} %get-tuple-element.1980) | copy-start | bytes 3076
  1425.1 47.7 %copy-start.87 = (f32[256]{0:T(256)S(1)}, f32[256]{0:T(256)}, u32[]{:S(2)}) copy-start(f32[256]{0:T(256)} %get-tuple-element.1981) | copy-start | bytes 3076
  1425.1 47.7 %copy-start.88 = (f32[256]{0:T(256)S(1)}, f32[256]{0:T(256)}, u32[]{:S(2)}) copy-start(f32[256]{0:T(256)} %get-tuple-element.1982) | copy-start | bytes 3076
  1962.8 48.3 %copy-start.47 = (f32[2,2048]{1,0:T(2,128)S(1)}, f32[2,2048]{1,0:T(2,128)}, u32[]{:S(2)}) copy-start(f32[2,2048]{1,0:T(2,128)} %get-tuple-element.2210) | copy-start | bytes 49156
  (82 other events, 579.0 us)
Sparse Core Ops, SparseCore 0:
  1387.3 150.0 all-reduce.20
  1540.1 422.6 all-reduce.22
where the time goes:
time: 2050 us; the launch traced here: 2040 us
  waiting for transfers between devices  601 us (29%)
  other arithmetic  480 us (23%)
  matrix products  415 us (20%)
  local copies, waits for them, and re-layouts  289 us (14%)
  blocking collectives  180 us (9%)
  starting transfers between devices  53.4 us (3%)
    psum x1, waiting for transfers between devices, local(): mixed_out = (x_float + lax.psum(branch_part, 'head')).astype(jnp.bfloat16)  420 us
    another operation x72, other arithmetic  173 us
    dot_general x24, matrix products, group_step(): jnp.einsum('tsh,shp->thp', weights * scores[:, :, None], scaled, precisio...  136 us
    ppermute x18, waiting for transfers between devices, from_behind(): lax.ppermute(value, axis, [(source, source + steps) for source in range(l...  116 us
    dynamic_update_slice x64, other arithmetic, scan_groups(): last_states, outputs = lax.scan(block_step, states, pieces)  86.7 us
    unnamed x1, blocking collectives  76.6 us
    psum x1, waiting for transfers between devices, local(): lax.psum((grad_gate_x, grad_bc, grad_dt, grad_conv_x, grad_conv_x_bias, g...  64.6 us
    dot_general x24, matrix products, group_step(): scores = jnp.dot(reads, writes.T, precision=HIGHEST)  59 us
  transfers between devices with their start and end apart: 20, of which 16 were waited for; matrix products, arithmetic and copies ran while one was open for 5% of the time, Pallas kernels for 0%

commit v1 on v0

v1 whole, which is shorter than its diff:
```python
from functools import partial

import jax
import jax.numpy as jnp
import numpy as np
from jax import lax
from jax.experimental import pallas as pl
from jax.experimental.pallas import tpu as pltpu
from jax.sharding import PartitionSpec as P

EPS = 1e-05
Q = 128
TILE = 256
RIM = 16
NEVER = -1e30
TINY = 1e-37
BF = jnp.bfloat16
F32 = jnp.float32
VMEM_BYTES = 56 * 2**20
GAIN, TAPS, SHIFT, GATE, SKIP, RATE, BIAS, TABLE = 0, 1, 5, 6, 7, 8, 9, 16


def dot(a, b):
    return jnp.dot(a, b, preferred_element_type=F32)


def dot_nt(a, b):
    return lax.dot_general(a, b, (((1,), (1,)), ((), ())), preferred_element_type=F32)


def dot_tn(a, b):
    return lax.dot_general(a, b, (((0,), (0,)), ((), ())), preferred_element_type=F32)


def halves(value):
    high = value.astype(BF)
    return high, (value - high.astype(F32)).astype(BF)


def twice(value, axis):
    return jnp.concatenate([value, value], axis=axis)


def stacked(value, axis):
    return jnp.concatenate(halves(value), axis=axis)


def spread_heads(value, spread):
    return dot(jnp.concatenate(halves(value), axis=1), spread)


def gather_heads(value, gather):
    return dot(jnp.concatenate(halves(value), axis=1), gather)


def add_up(value, wedge):
    return dot(wedge, jnp.concatenate(halves(value), axis=0))


def sigmoid(value):
    return jax.nn.sigmoid(value)


def softplus(value):
    return jnp.maximum(value, 0.0) + jnp.log1p(jnp.exp(-jnp.abs(value)))


def iota(shape, axis):
    return lax.broadcasted_iota(jnp.int32, shape, axis)


class Docs:
    def __init__(self, meta, m):
        self.count = meta.shape[1] - 1
        self.starts = [meta[m, j] for j in range(self.count)]
        self.anchor = meta[m, self.count]

    def counts(self, places):
        total = (places >= self.starts[0]).astype(jnp.int32)
        for start in self.starts[1:]:
            total = total + (places >= start).astype(jnp.int32)
        return total

    def starts_at(self, places):
        hit = places == self.starts[0]
        for start in self.starts[1:]:
            hit = hit | (places == start)
        return hit

    def tap_masks(self, first, rows):
        places = first + iota((rows, 128), 0)
        masks = []
        broken = None
        for back in range(3):
            hit = self.starts_at(places - back)
            broken = hit if broken is None else broken | hit
            masks.append(jnp.where(broken, 0.0, 1.0))
        return masks


class Chunk:
    def __init__(self, docs, first, deltas, rate, wedge):
        self.before = docs.counts(first - 1)
        self.last = docs.counts(first + Q - 1)
        column = docs.counts(first + iota((Q, 128), 0))
        self.docs, self.first, self.column = docs, first, column
        self.run = add_up(deltas * rate, wedge)
        self.total = self.run[Q - 1 : Q]
        self.entry_bias = jnp.where(column == self.before, 0.0, NEVER)
        self.leave_bias = jnp.where(column == self.last, 0.0, NEVER)
        self.through = jnp.where(self.last == self.before, 0.0, NEVER)
        self.deltas = deltas

    def same(self):
        return self.column == self.docs.counts(self.first + iota((8, 128), 1))[0:1]

    def entry(self):
        return jnp.exp(self.run + self.entry_bias)

    def leaving(self):
        return jnp.exp(self.total - self.run + self.leave_bias) * self.deltas

    def overall(self):
        return jnp.exp(self.total + self.through)


def wide_row(row):
    return jnp.broadcast_to(row, (8, row.shape[1]))


def pair_blocks(value, pair, lanes):
    both = value[:, 128 * pair : 128 * pair + 128]
    zero = jnp.zeros_like(both)
    return jnp.concatenate([jnp.where(lanes, both, zero), jnp.where(lanes, zero, both)], axis=0)


def first_kernel(
    tile, channels,
    meta, rim, tokens, weights, table, spread, wedge, *rest, m,
):
    normed_o, gate_o, xbc_o, pre_o, conv_o, deltas_o, held_o, sums_o, leaving_o, edge_o, ext, state, total = rest[-13:]
    step = pl.program_id(0)
    docs = Docs(meta, m)
    width = xbc_o.shape[1]
    taps = table[TAPS : TAPS + 4, :width]
    shift = table[SHIFT : SHIFT + 1, :width]
    gain = table[GAIN : GAIN + 1, : tokens.shape[1]]
    rate = table[RATE : RATE + 1, :128]
    dt_bias = table[BIAS : BIAS + 1, :128]

    def normalize(rows):
        x = rows.astype(F32)
        scale = lax.rsqrt(jnp.mean(x * x, axis=1, keepdims=True) + EPS)
        return (x * scale * gain).astype(BF)

    @pl.when(step == 0)
    def _():
        edge = dot(normalize(rim[...]), weights[:, channels : channels + width]).astype(BF)
        edge_o[...] = edge
        ext[0:8, :] = edge.astype(F32)[RIM - 8 :]
        state[...] = jnp.zeros_like(state)
        total[...] = jnp.zeros_like(total)

    @pl.when(step > 0)
    def _():
        ext[0:8, :] = ext[tile : tile + 8, :]

    normed = normalize(tokens[...])
    normed_o[...] = normed
    gate_o[...] = dot(normed, weights[:, :channels])
    xbc = dot(normed, weights[:, channels : channels + width]).astype(BF)
    xbc_o[...] = xbc
    ext[8:, :] = xbc.astype(F32)
    deltas = softplus(dot(normed, weights[:, channels + width + 256 :]) + dt_bias)
    deltas_o[...] = deltas
    first = docs.anchor + step * tile
    masks = docs.tap_masks(first, tile)
    for slab in range(width // 128):
        lanes = slice(128 * slab, 128 * slab + 128)
        pre = shift[:, lanes] + taps[3:4, lanes] * ext[8 : 8 + tile, lanes]
        for back in range(1, 4):
            pre = pre + taps[3 - back : 4 - back, lanes] * ext[8 - back : 8 - back + tile, lanes] * masks[back - 1]
        pre_o[:, lanes] = pre
        conv_o[:, lanes] = (pre * sigmoid(pre)).astype(BF)
    for part in range(tile // Q):
        rows = slice(Q * part, Q * part + Q)
        chunk = Chunk(docs, first + Q * part, deltas[rows], rate, wedge[...])
        held_o[part] = state[...]
        sums_o[part] = total[...]
        total[...] = total[...] + chunk.total
        writes = conv_o[rows, channels : channels + 128]
        scaled = conv_o[rows, :channels].astype(F32) * spread_heads(chunk.leaving(), spread[...])
        keep = spread_heads(wide_row(chunk.overall()), spread[...])[0:1]
        state[...] = state[...] * keep + dot_tn(twice(writes, 0), stacked(scaled, 0))

    @pl.when(step == pl.num_programs(0) - 1)
    def _():
        end = docs.anchor + (step + 1) * tile - 1
        through = jnp.where(docs.counts(end) == docs.counts(docs.anchor - 1), 0.0, NEVER)
        leaving_o[0:128, :] = state[...]
        leaving_o[128:136, :] = spread_heads(jnp.exp(total[...] + through), spread[...])


def inside_kernel(
    tile, channels,
    meta, conv, deltas, cotangent, out_weight, table, spread, wedge, *rest, m, parts,
):
    mixed_o, back_o, near_o = rest[-3:]
    step = pl.program_id(0)

    @pl.when(step == 0)
    def _():
        near_o[...] = joined([part[...] for part in rest[:parts]])

    docs = Docs(meta, m)
    first = docs.anchor + step * tile
    lanes_q = iota((Q, 128), 1)
    causal = iota((Q, Q), 0) >= iota((Q, Q), 1)
    low = lanes_q < 64
    skip = table[SKIP : SKIP + 1, :channels]
    rate = table[RATE : RATE + 1, :128]
    back_o[...] = dot_nt(cotangent[...], out_weight[...])
    for part in range(tile // Q):
        rows = slice(Q * part, Q * part + Q)
        chunk = Chunk(docs, first + Q * part, deltas[rows, :], rate, wedge[...])
        u = conv[rows, :channels]
        writes = conv[rows, channels : channels + 128]
        reads = conv[rows, channels + 128 :]
        scores = dot_nt(reads, writes)
        bias = jnp.where(chunk.same() & causal, 0.0, NEVER)
        behind = jnp.transpose(jnp.log(jnp.maximum(chunk.deltas, TINY)) - chunk.run)
        pieces = []
        for pair in range(channels // 128):
            both = []
            for head in (2 * pair, 2 * pair + 1):
                decay = jnp.exp(chunk.run[:, head : head + 1] + behind[head : head + 1] + bias)
                both.append((decay * scores).astype(BF))
            pieces.append(dot(jnp.concatenate(both, axis=1), pair_blocks(u, pair, low)))
        mixed_o[rows, :] = jnp.concatenate(pieces, axis=1) + skip * u.astype(F32)


def mix_kernel(
    tile, channels,
    meta, inside, back, conv, deltas, gate, held, sums, table, spread, wedge, *rest, m, parts,
):
    mixed_o, stats_o, carry = rest[-3:]
    step = pl.program_id(0)

    @pl.when(step == 0)
    def _():
        carry[...] = joined([part[...] for part in rest[:parts]])

    docs = Docs(meta, m)
    first = docs.anchor + step * tile
    lanes_q = iota((Q, 128), 1)
    gate_gain = table[GATE : GATE + 1, :channels]
    rate = table[RATE : RATE + 1, :128]
    for part in range(tile // Q):
        rows = slice(Q * part, Q * part + Q)
        chunk = Chunk(docs, first + Q * part, deltas[rows, :], rate, wedge[...])
        reads = conv[rows, channels + 128 :]
        since = jnp.where(chunk.before == docs.counts(docs.anchor - 1), 0.0, NEVER)
        arrived = spread_heads(jnp.exp(sums[part] + since), spread[...])[0:1]
        state = stacked(held[part] + arrived * carry[0:128, :], 0)
        mixed = inside[rows, :] + dot(twice(reads, 1), state) * spread_heads(chunk.entry(), spread[...])
        mixed_o[rows, :] = mixed
        gate_rows = gate[rows, :]
        gated = mixed * gate_rows * sigmoid(gate_rows)
        squares = jnp.sum(gated * gated, axis=1, keepdims=True)
        inner = jnp.sum(gated * back[rows, :] * gate_gain, axis=1, keepdims=True)
        columns = jnp.where(lanes_q == 0, squares, jnp.where(lanes_q == 1, inner, 0.0))
        stats_o[:, rows] = jnp.transpose(columns)[0:8]


def third_kernel(
    tile, channels, full, chained,
    meta, mixed, back, gate, conv, deltas, normed, cotangent, out_weight, table, spread, wedge,
    stats_a, stats_b, stats_c, stats_d, *rest, m,
):
    if chained:
        grad_out_i, grad_gate_i, rows_i, *rest = rest
    branch_o, gate_back_o, ssd_back_o, held_o, sums_o, leaving_o, grad_out, grad_gate, rows_o, state, total = rest[-11:]
    step = pl.program_id(0)
    gate_gain = table[GATE : GATE + 1, :channels]
    rate = table[RATE : RATE + 1, :128]
    docs = Docs(meta, m)
    place = pl.num_programs(0) - 1 - step
    first = docs.anchor + place * tile

    @pl.when(step == 0)
    def _():
        state[...] = jnp.zeros_like(state)
        total[...] = jnp.zeros_like(total)
        if chained:
            grad_out[...] = grad_out_i[...]
            grad_gate[...] = grad_gate_i[...]
            rows_o[...] = rows_i[...]
        else:
            grad_out[...] = jnp.zeros_like(grad_out)
            grad_gate[...] = jnp.zeros_like(grad_gate)
            rows_o[...] = jnp.zeros_like(rows_o)

    stats = stats_a[...] + stats_b[...] + stats_c[...] + stats_d[...]
    branches = []
    for part in reversed(range(tile // Q)):
        rows = slice(Q * part, Q * part + Q)
        sides = jnp.transpose(jnp.concatenate([stats[:, rows], jnp.zeros((120, Q), F32)], axis=0))
        scale = lax.rsqrt(sides[:, 0:1] / full + EPS)
        inner = sides[:, 1:2]
        mixed_rows = mixed[rows, :]
        gate_rows = gate[rows, :]
        sigma = sigmoid(gate_rows)
        act = gate_rows * sigma
        gated = mixed_rows * act
        unit = gated * scale
        branch = (unit * gate_gain).astype(BF)
        branches.append(branch)
        back_rows = back[rows, :]
        grad_gated = scale * (back_rows * gate_gain) - unit * (scale * scale * (inner / full))
        grad_mixed = grad_gated * act
        gate_back_o[rows, :] = (grad_gated * mixed_rows * (sigma * (1.0 + gate_rows * (1.0 - sigma)))).astype(BF)
        ssd_back = grad_mixed.astype(BF)
        ssd_back_o[rows, :] = ssd_back
        u = conv[rows, :channels].astype(F32)
        rows_o[0:8, :] += jnp.sum((back_rows * unit).reshape(Q // 8, 8, channels), axis=0)
        rows_o[8:16, :] += jnp.sum((grad_mixed * u).reshape(Q // 8, 8, channels), axis=0)
        chunk = Chunk(docs, first + Q * part, deltas[rows, :], rate, wedge[...])
        held_o[part] = state[...]
        sums_o[part] = total[...]
        total[...] = total[...] + chunk.total
        reads = conv[rows, channels + 128 :]
        entered = stacked(ssd_back.astype(F32) * spread_heads(chunk.entry(), spread[...]), 0)
        keep = spread_heads(wide_row(chunk.overall()), spread[...])[0:1]
        state[...] = state[...] * keep + dot_tn(twice(reads, 0), entered)
    branch = jnp.concatenate(branches[::-1], axis=0)
    branch_o[...] = dot(branch, out_weight[...]).astype(BF)
    grad_out[...] += dot_tn(branch, cotangent[...])
    grad_gate[...] += dot_tn(normed[...], gate_back_o[...])

    @pl.when(step == pl.num_programs(0) - 1)
    def _():
        end = docs.anchor + pl.num_programs(0) * tile - 1
        through = jnp.where(docs.counts(end) == docs.counts(docs.anchor - 1), 0.0, NEVER)
        leaving_o[0:128, :] = state[...]
        leaving_o[128:136, :] = spread_heads(jnp.exp(total[...] + through), spread[...])


def within_kernel(
    tile, channels,
    meta, conv, deltas, ssd_back, table, wedge, *rest, m, parts,
):
    grads_o, source_o, target_o, near_o = rest[-4:]
    step = pl.program_id(0)

    @pl.when(step == 0)
    def _():
        near_o[...] = joined([part[...] for part in rest[:parts]])

    docs = Docs(meta, m)
    first = docs.anchor + step * tile
    lanes_q = iota((Q, 128), 1)
    rows_8 = iota((8, 128), 0)
    causal = iota((Q, Q), 1) >= iota((Q, Q), 0)
    low = lanes_q < 64
    skip = table[SKIP : SKIP + 1, :channels]
    rate = table[RATE : RATE + 1, :128]
    for part in range(tile // Q):
        rows = slice(Q * part, Q * part + Q)
        chunk = Chunk(docs, first + Q * part, deltas[rows, :], rate, wedge[...])
        u = conv[rows, :channels]
        writes = conv[rows, channels : channels + 128]
        reads = conv[rows, channels + 128 :]
        grad = ssd_back[rows, :]
        scores = dot_nt(writes, reads)
        bias = jnp.where(chunk.same() & causal, 0.0, NEVER)
        ahead = jnp.transpose(chunk.run)
        behind = jnp.log(jnp.maximum(chunk.deltas, TINY)) - chunk.run
        grad_scores = jnp.zeros((Q, Q), F32)
        by_source = jnp.zeros((Q, 128), F32)
        by_target = jnp.zeros((8, 128), F32)
        pieces = []
        for pair in range(channels // 128):
            blocks = pair_blocks(grad, pair, low)
            meets = dot_nt(u[:, 128 * pair : 128 * pair + 128], blocks)
            both = []
            for side in range(2):
                head = 2 * pair + side
                decay = jnp.exp(behind[:, head : head + 1] + ahead[head : head + 1] + bias)
                both.append((decay * scores).astype(BF))
                weighed = decay * meets[:, Q * side : Q * side + Q]
                grad_scores = grad_scores + weighed
                pairs = weighed * scores
                by_source = jnp.where(lanes_q == head, jnp.sum(pairs, axis=1, keepdims=True), by_source)
                by_target = jnp.where(rows_8 == head, jnp.sum(pairs, axis=0, keepdims=True), by_target)
            pieces.append(dot(jnp.concatenate(both, axis=1), blocks))
        source_o[rows, :] = by_source
        target_o[rows, :] = jnp.transpose(jnp.concatenate([by_target, jnp.zeros((120, Q), F32)], axis=0))
        high, low_part = halves(grad_scores)
        grads_o[rows, :channels] = jnp.concatenate(pieces, axis=1) + skip * grad.astype(F32)
        grads_o[rows, channels : channels + 128] = dot(jnp.concatenate([high, low_part], axis=1), twice(reads, 0))
        grads_o[rows, channels + 128 :] = dot_tn(jnp.concatenate([high, low_part], axis=0), twice(writes, 0))


def across_kernel(
    tile, channels, chained,
    meta, conv, pre, xbc, edge, deltas, ssd_back, inside, by_source, by_target,
    held, sums, carry, held_b, sums_b,
    table, spread, gather, wedge, wedge_up, wedge_below, *rest, m, parts,
):
    far, rest = rest[:parts], rest[parts:]
    if chained:
        taps_i, heads_i, *rest = rest
    in_back_o, dt_back_o, rim_o, tail_o, taps_o, heads_o, ext, grads, carry_b = rest[-9:]
    step = pl.program_id(0)
    docs = Docs(meta, m)
    places = pl.num_programs(0)
    place = places - 1 - step
    first = docs.anchor + place * tile
    end = docs.anchor + places * tile - 1
    width = pre.shape[1]
    taps = table[TAPS : TAPS + 4, :width]
    rate = table[RATE : RATE + 1, :128]

    @pl.when(step == 0)
    def _():
        if chained:
            taps_o[...] = taps_i[...]
            heads_o[...] = heads_i[...]
        else:
            taps_o[...] = jnp.zeros_like(taps_o)
            heads_o[...] = jnp.zeros_like(heads_o)
        carry_b[...] = joined([part[...] for part in far])
        ext[:, 0:16, :] = jnp.zeros_like(ext[:, 0:16, :])
        ext[:, 16 + tile :, :] = jnp.zeros_like(ext[:, 16 + tile :, :])

    @pl.when(step > 0)
    def _():
        ext[:, 16 + tile :, :] = ext[:, 16:24, :]

    for part in range(tile // Q):
        rows = slice(Q * part, Q * part + Q)
        chunk = Chunk(docs, first + Q * part, deltas[rows, :], rate, wedge[...])
        u = conv[rows, :channels].astype(F32)
        writes = conv[rows, channels : channels + 128]
        reads = conv[rows, channels + 128 :]
        since = jnp.where(chunk.before == docs.counts(docs.anchor - 1), 0.0, NEVER)
        until = jnp.where(chunk.last == docs.counts(end), 0.0, NEVER)
        arrived = spread_heads(jnp.exp(sums[part] + since), spread[...])[0:1]
        state = held[part] + arrived * carry[0:128, :]
        arrived_b = spread_heads(jnp.exp(sums_b[part] + until), spread[...])[0:1]
        state_b = held_b[part] + arrived_b * carry_b[0:128, :]
        state_high, state_low = halves(state)
        state_b_high, state_b_low = halves(state_b)
        outward = spread_heads(chunk.leaving(), spread[...])
        sent_high, sent_low = halves(u * outward)
        grad_in = ssd_back[rows, :].astype(F32) * spread_heads(chunk.entry(), spread[...])
        grad_high, grad_low = halves(grad_in)
        crossing = dot(twice(writes, 1), jnp.concatenate([state_b_high, state_b_low], axis=0)) * outward
        out_part = gather_heads(u * crossing, gather[...])
        in_part = gather_heads(
            grad_in * dot(twice(reads, 1), jnp.concatenate([state_high, state_low], axis=0)), gather[...]
        )
        between = jnp.sum((state * state_b).reshape(16, 8, channels), axis=0)
        between = jnp.sum(gather_heads(between, gather[...]), axis=0, keepdims=True) * chunk.overall()
        source = by_source[rows, :]
        grad_run = (
            between
            + add_up(in_part + by_target[rows, :] - source, wedge_up[...])
            + add_up(out_part, wedge_below[...])
        )
        slope = 1.0 - jnp.exp(-chunk.deltas)
        ratio = jnp.where(chunk.deltas > 1e-6, slope / jnp.maximum(chunk.deltas, 1e-6), 1.0)
        dt_back = (source + out_part) * ratio + rate * grad_run * slope
        dt_back_o[rows, :] = dt_back.astype(BF)
        heads_o[0:8, :] += jnp.sum(dt_back.reshape(Q // 8, 8, 128), axis=0)
        heads_o[8:16, :] += jnp.sum((grad_run * chunk.deltas).reshape(Q // 8, 8, 128), axis=0)
        grads[rows, :channels] = inside[rows, :channels] + crossing
        grads[rows, channels : channels + 128] = inside[rows, channels : channels + 128] + dot_nt(
            jnp.concatenate([sent_high, sent_low, sent_high], axis=1),
            jnp.concatenate([state_b_high, state_b_high, state_b_low], axis=1),
        )
        grads[rows, channels + 128 :] = inside[rows, channels + 128 :] + dot_nt(
            jnp.concatenate([grad_high, grad_low, grad_high], axis=1),
            jnp.concatenate([state_high, state_high, state_low], axis=1),
        )

    masks = docs.tap_masks(first, tile)
    for slab in range(width // 128):
        lanes = slice(128 * slab, 128 * slab + 128)
        pre_rows = pre[:, lanes]
        sigma = sigmoid(pre_rows)
        grad_pre = grads[:, lanes] * (sigma * (1.0 + pre_rows * (1.0 - sigma)))
        source = xbc[:, lanes].astype(F32)
        result = taps[3:4, lanes] * grad_pre
        taps_o[24:32, lanes] += jnp.sum((grad_pre * source).reshape(tile // 8, 8, 128), axis=0)
        taps_o[32:40, lanes] += jnp.sum(grad_pre.reshape(tile // 8, 8, 128), axis=0)
        for back in range(1, 4):
            ext[back - 1, 16 : 16 + tile, lanes] = grad_pre * masks[back - 1]
            moved = ext[back - 1, 16 + back : 16 + back + tile, lanes]
            result = result + taps[3 - back : 4 - back, lanes] * moved
            taps_o[8 * (3 - back) : 8 * (4 - back), lanes] += jnp.sum((moved * source).reshape(tile // 8, 8, 128), axis=0)
        high = result.astype(BF)
        in_back_o[:, lanes] = high
        if 128 * slab >= channels:
            in_back_o[:, slice(256 + 128 * slab, 384 + 128 * slab)] = (result - high.astype(F32)).astype(BF)

        @pl.when(step == 0)
        def _():
            tail_o[:, lanes] = result[tile - RIM :]

    @pl.when(place == 0)
    def _():
        total = jnp.zeros((RIM, width), F32)
        source = edge[...].astype(F32)
        for back in range(1, 4):
            moved = ext[back - 1, back : back + RIM, :]
            total = total + taps[3 - back : 4 - back, :] * moved
            taps_o[8 * (3 - back) : 8 * (4 - back), :] += jnp.sum((moved * source).reshape(RIM // 8, 8, width), axis=0)
        rim_o[...] = total


def input_kernel(
    tile, channels, chained, last,
    tokens, normed, gate_back, in_back, dt_back, weights, *rest,
):
    if last:
        tail, rim, *rest = rest
    if chained:
        grads_i, rows_i, *rest = rest
    part_o, grads_o, rows_o, every = rest[-4:]
    step = pl.program_id(0)
    wide = in_back.shape[1]
    width = wide - 256

    @pl.when(step == 0)
    def _():
        if chained:
            grads_o[...] = grads_i[...]
            rows_o[...] = rows_i[...]
        else:
            grads_o[...] = jnp.zeros_like(grads_o)
            rows_o[...] = jnp.zeros_like(rows_o)

    every[:, :channels] = gate_back[...]
    every[:, channels : channels + wide] = in_back[...]
    every[:, channels + wide :] = dt_back[...]
    if last:
        high, low = halves(tail[...] + rim[...])
        every[tile - RIM :, channels : channels + width] = high
        every[tile - RIM :, channels + width : channels + wide] = low[:, channels:]
    x = tokens[...].astype(F32)
    scale = lax.rsqrt(jnp.mean(x * x, axis=1, keepdims=True) + EPS)
    part = dot_nt(every[...], weights[...])
    part_o[...] = part.astype(BF)
    rows_o[...] += jnp.sum((part * (x * scale)).reshape(tile // 8, 8, x.shape[1]), axis=0)
    grads_o[...] += dot_tn(normed[...], every[:, channels:])


class Call:
    def __init__(self, kernel, steps, name):
        self.kernel, self.steps, self.name = kernel, steps, name
        self.args, self.in_specs, self.outs, self.out_specs, self.scratch = [], [], [], [], []
        self.aliases = {}

    def whole(self, *arrays):
        for array in arrays:
            self.args.append(array)
            self.in_specs.append(pl.BlockSpec(array.shape, lambda i, rank=array.ndim: (0,) * rank))
        return self

    def scalars(self, array):
        self.args.append(array)
        self.in_specs.append(pl.BlockSpec(memory_space=pltpu.SMEM))
        return self

    def blocks(self, *arrays_specs):
        for array, spec in arrays_specs:
            self.args.append(array)
            self.in_specs.append(spec)
        return self

    def out(self, shape, dtype, spec=None):
        self.outs.append(jax.ShapeDtypeStruct(shape, dtype))
        self.out_specs.append(spec or pl.BlockSpec(shape, lambda i, rank=len(shape): (0,) * rank))
        return self

    def after(self, *arrays):
        for array in arrays:
            self.args.append(array)
            self.in_specs.append(pl.BlockSpec(memory_space=pl.ANY))
        return self

    def alias(self, array):
        self.aliases = {len(self.args): 0}
        return self.after(array)

    def temp(self, shape, dtype):
        self.scratch.append(pltpu.VMEM(shape, dtype))
        return self

    def run(self, micros):
        return pl.pallas_call(
            self.kernel,
            grid=(self.steps,),
            in_specs=self.in_specs,
            out_specs=tuple(self.out_specs),
            out_shape=tuple(self.outs),
            scratch_shapes=self.scratch,
            input_output_aliases=self.aliases,
            compiler_params=pltpu.CompilerParams(
                dimension_semantics=("arbitrary",), vmem_limit_bytes=VMEM_BYTES
            ),
            cost_estimate=pl.CostEstimate(flops=int(micros * 1.15e9), bytes_accessed=0, transcendentals=0),
            name=self.name,
        )(*self.args)


def swap(value, axis, bits):
    count = lax.axis_size(axis)
    return lax.ppermute(value, axis, [(i, i ^ bits) for i in range(count)])


def from_behind(value, axis, steps):
    count = lax.axis_size(axis)
    sources = range(max(0, -steps), min(count, count - steps))
    return lax.ppermute(value, axis, [(i, i + steps) for i in sources])


def joined(parts):
    rows = parts[0].shape[0] - 8
    state, decay = parts[0][:rows], parts[0][rows : rows + 1]
    for part in parts[1:]:
        state = state + decay * part[:rows]
        decay = decay * part[rows : rows + 1]
    return jnp.concatenate([state, jnp.broadcast_to(decay, (8, decay.shape[1]))], axis=0)


def near_parts(leaving, axis, sign):
    return [from_behind(leaving, axis, sign * k) for k in range(1, min(4, lax.axis_size(axis)))]


def far_parts(carry, axis, sign):
    count = lax.axis_size(axis)
    window = 3
    parts = [carry]
    while window < count - 1:
        carry = joined(parts) if len(parts) > 1 else carry
        parts = [carry] + [from_behind(carry, axis, sign * k) for k in (window, 2 * window) if k < count]
        window *= 3
    return parts


def sum_rows(parts):
    total = parts[0].astype(F32)
    for part in parts[1:]:
        total = total + part.astype(F32)
    return total


def head_pair(part):
    rows = part.shape[0] // 2
    side = lax.axis_index("head") % 2
    mine = lax.dynamic_slice_in_dim(part, side * rows, rows, 0)
    other = lax.dynamic_slice_in_dim(part, (1 - side) * rows, rows, 0)
    return (mine.astype(F32) + swap(other, "head", 1).astype(F32)).astype(BF)


def head_rest(low):
    total = low.astype(F32)
    bit = 2
    while bit < lax.axis_size("head"):
        low = total.astype(BF)
        total = low.astype(F32) + swap(low, "head", bit).astype(F32)
        bit *= 2
    return total


def scatter_sum(value, axis):
    count = lax.axis_size(axis)
    me = lax.axis_index(axis)
    rows = value.shape[0] // count
    total = lax.dynamic_slice_in_dim(value, me * rows, rows, 0).astype(F32)
    for bits in range(1, count):
        piece = lax.dynamic_slice_in_dim(value, jnp.bitwise_xor(me, bits) * rows, rows, 0)
        total = total + swap(piece, axis, bits).astype(F32)
    return total


def gather_rows(value, axis):
    count = lax.axis_size(axis)
    me = lax.axis_index(axis)
    rows = value.shape[0]
    result = jnp.zeros((count * rows, value.shape[1]), value.dtype)
    result = lax.dynamic_update_slice_in_dim(result, value, me * rows, 0)
    for bits in range(1, count):
        result = lax.dynamic_update_slice_in_dim(
            result, swap(value, axis, bits), jnp.bitwise_xor(me, bits) * rows, 0
        )
    return result


def all_sum(value, axis):
    bit = 1
    while bit < lax.axis_size(axis):
        value = value + swap(value, axis, bit)
        bit *= 2
    return value


def local(
    tokens,
    doc_starts,
    norm_gain,
    gate_x_weight,
    bc_weight,
    dt_weight,
    conv_x_weight,
    conv_x_bias,
    conv_bc_weight,
    conv_bc_bias,
    dt_bias,
    a_log,
    d_skip,
    gate_gain,
    out_weight,
    cotangent,
):
    micro, length, model = tokens.shape
    channels = gate_x_weight.shape[2]
    heads = dt_weight.shape[1]
    dim = channels // heads
    states = bc_weight.shape[1] // 2
    width = channels + 2 * states
    full = channels * lax.axis_size("head")
    tile = TILE
    steps = length // tile
    per = tile // Q
    blocks = length // Q

    rim_tokens = from_behind(tokens[:, length - RIM :], "seq", 1)
    weights = jnp.concatenate(
        [gate_x_weight[:, 0], gate_x_weight[:, 1], bc_weight, bc_weight,
         jnp.pad(dt_weight, ((0, 0), (0, 128 - heads)))], axis=1
    )
    decay_rate = -jnp.exp(a_log)

    def table_rows(*parts):
        row = jnp.concatenate(parts, axis=-1)
        row = row if row.ndim == 2 else row[None]
        return jnp.pad(row, ((0, 0), (0, model - row.shape[1])))

    table = jnp.concatenate(
        [
            table_rows(norm_gain),
            table_rows(conv_x_weight, conv_bc_weight),
            table_rows(conv_x_bias, conv_bc_bias),
            table_rows(gate_gain),
            table_rows(jnp.repeat(d_skip, dim)),
            table_rows(decay_rate),
            table_rows(dt_bias, jnp.full((128 - heads,), -200.0, F32)),
            jnp.zeros((TABLE - BIAS - 1, model), F32),
        ],
        axis=0,
    )
    owner = np.arange(channels)[None, :] // dim == np.arange(128)[:, None]
    spread = np.concatenate([owner, owner], axis=0).astype(BF)
    gather = np.concatenate([owner.T, owner.T], axis=0).astype(BF)
    order = np.arange(Q)
    until_here = order[:, None] >= order[None, :]
    below = order[:, None] > order[None, :]
    wedge = np.concatenate([until_here] * 2, axis=1).astype(BF)
    wedge_up = np.concatenate([until_here.T] * 2, axis=1).astype(BF)
    wedge_below = np.concatenate([below] * 2, axis=1).astype(BF)
    anchor = lax.axis_index("seq") * length
    meta = jnp.concatenate(
        [jnp.where(doc_starts >= 1, doc_starts, 2**30), jnp.full((micro, 1), anchor)], axis=1
    ).astype(jnp.int32)

    ahead = lambda i: i
    astern = lambda i: steps - 1 - i

    def rows_of(cols, turn):
        return pl.BlockSpec((tile, cols), lambda i: (turn(i), 0))

    def rows_in(m, cols, turn):
        return pl.BlockSpec((None, tile, cols), lambda i: (m, turn(i), 0))

    def chunks_of(turn, rows, cols):
        return pl.BlockSpec((per, rows, cols), lambda i: (turn(i), 0, 0))

    def stat_spec(turn):
        return pl.BlockSpec((8, tile), lambda i: (0, turn(i)))

    def project(m, *waits):
        call = Call(partial(first_kernel, tile, channels, m=m), steps, f"project_{m}")
        call.scalars(meta)
        call.blocks((rim_tokens, pl.BlockSpec((None, RIM, model), lambda i: (m, 0, 0))))
        call.blocks((tokens, rows_in(m, model, ahead)))
        call.whole(weights, table, spread, wedge).after(*waits)
        call.out((length, model), BF, rows_of(model, ahead))
        call.out((length, channels), F32, rows_of(channels, ahead))
        call.out((length, width), BF, rows_of(width, ahead))
        call.out((length, width), F32, rows_of(width, ahead))
        call.out((length, width), BF, rows_of(width, ahead))
        call.out((length, 128), F32, rows_of(128, ahead))
        call.out((blocks, 128, channels), F32, chunks_of(ahead, 128, channels))
        call.out((blocks, 8, 128), F32, chunks_of(ahead, 8, 128))
        call.out((136, channels), F32)
        call.out((RIM, width), BF)
        call.temp((tile + 8, width), F32).temp((128, channels), F32).temp((8, 128), F32)
        return call.run(22)

    def inside(m, kept, parts, *waits):
        normed, gate, xbc, pre, conv, deltas = kept[:6]
        call = Call(partial(inside_kernel, tile, channels, m=m, parts=len(parts)), steps, f"inside_{m}")
        call.scalars(meta)
        call.blocks((conv, rows_of(width, ahead)), (deltas, rows_of(128, ahead)), (cotangent, rows_in(m, model, ahead)))
        call.whole(out_weight, table, spread, wedge, *parts).after(*waits)
        call.out((length, channels), F32, rows_of(channels, ahead))
        call.out((length, channels), F32, rows_of(channels, ahead))
        call.out((136, channels), F32)
        return call.run(12)

    def mix(m, kept, inner, back, parts, *waits):
        normed, gate, xbc, pre, conv, deltas, held, sums = kept[:8]
        call = Call(partial(mix_kernel, tile, channels, m=m, parts=len(parts)), steps, f"mix_{m}")
        call.scalars(meta)
        call.blocks(
            (inner, rows_of(channels, ahead)),
            (back, rows_of(channels, ahead)),
            (conv, rows_of(width, ahead)),
            (deltas, rows_of(128, ahead)),
            (gate, rows_of(channels, ahead)),
            (held, chunks_of(ahead, 128, channels)),
            (sums, chunks_of(ahead, 8, 128)),
        )
        call.whole(table, spread, wedge, *parts).after(*waits)
        call.out((length, channels), F32, rows_of(channels, ahead))
        call.out((8, length), F32, stat_spec(ahead))
        call.out((136, channels), F32)
        return call.run(12)

    def norm(m, kept, mixed, back, stats, chain, *waits):
        normed, gate, xbc, pre, conv, deltas = kept[:6]
        call = Call(partial(third_kernel, tile, channels, float(full), bool(chain), m=m), steps, f"gate_{m}")
        call.scalars(meta)
        call.blocks(
            (mixed, rows_of(channels, astern)),
            (back, rows_of(channels, astern)),
            (gate, rows_of(channels, astern)),
            (conv, rows_of(width, astern)),
            (deltas, rows_of(128, astern)),
            (normed, rows_of(model, astern)),
            (cotangent, rows_in(m, model, astern)),
        )
        call.whole(out_weight, table, spread, wedge)
        call.blocks(*[(part, stat_spec(astern)) for part in stats])
        call.whole(*chain).after(*waits)
        call.out((length, model), BF, rows_of(model, astern))
        call.out((length, channels), BF, rows_of(channels, astern))
        call.out((length, channels), BF, rows_of(channels, astern))
        call.out((blocks, 128, channels), F32, chunks_of(astern, 128, channels))
        call.out((blocks, 8, 128), F32, chunks_of(astern, 8, 128))
        call.out((136, channels), F32)
        call.out((channels, model), F32)
        call.out((model, channels), F32)
        call.out((16, channels), F32)
        call.temp((128, channels), F32).temp((8, 128), F32)
        return call.run(19)

    def within(m, kept, ssd_back, parts, *waits):
        conv, deltas = kept[4:6]
        call = Call(partial(within_kernel, tile, channels, m=m, parts=len(parts)), steps, f"within_{m}")
        call.scalars(meta)
        call.blocks((conv, rows_of(width, ahead)), (deltas, rows_of(128, ahead)), (ssd_back, rows_of(channels, ahead)))
        call.whole(table, wedge, *parts).after(*waits)
        call.out((length, width), F32, rows_of(width, ahead))
        call.out((length, 128), F32, rows_of(128, ahead))
        call.out((length, 128), F32, rows_of(128, ahead))
        call.out((136, channels), F32)
        return call.run(14)

    def across(m, kept, carry, third, inner, parts, chain, *waits):
        normed, gate, xbc, pre, conv, deltas, held, sums, leaving, edge = kept
        call = Call(partial(across_kernel, tile, channels, bool(chain), m=m, parts=len(parts)), steps, f"across_{m}")
        call.scalars(meta)
        call.blocks((conv, rows_of(width, astern)), (pre, rows_of(width, astern)), (xbc, rows_of(width, astern)))
        call.whole(edge)
        call.blocks(
            (deltas, rows_of(128, astern)),
            (third[2], rows_of(channels, astern)),
            (inner[0], rows_of(width, astern)),
            (inner[1], rows_of(128, astern)),
            (inner[2], rows_of(128, astern)),
            (held, chunks_of(astern, 128, channels)),
            (sums, chunks_of(astern, 8, 128)),
        )
        call.whole(carry)
        call.blocks((third[3], chunks_of(astern, 128, channels)), (third[4], chunks_of(astern, 8, 128)))
        call.whole(table, spread, gather, wedge, wedge_up, wedge_below, *parts, *chain).after(*waits)
        call.out((length, width + 256), BF, rows_of(width + 256, astern))
        call.out((length, 128), BF, rows_of(128, astern))
        call.out((RIM, width), F32)
        call.out((RIM, width), F32)
        call.out((40, width), F32)
        call.out((16, 128), F32)
        call.temp((3, tile + 24, width), F32).temp((tile, width), F32).temp((136, channels), F32)
        return call.run(32)

    def input_back(m, kept, gate_back, fourth, span, rows, rim, chain, earlier, *waits):
        count = span[1] - span[0]
        turn = lambda i: i + span[0]
        put = lambda i: i + span[0] - rows[0]
        name = f"input_{m}_{span[0]}"
        call = Call(partial(input_kernel, tile, channels, bool(chain), rim is not None), count, name)
        call.blocks(
            (tokens, rows_in(m, model, turn)),
            (kept[0], rows_of(model, turn)),
            (gate_back, rows_of(channels, turn)),
            (fourth[0], rows_of(width + 256, turn)),
            (fourth[1], rows_of(128, turn)),
        )
        call.whole(weights)
        if rim is not None:
            call.whole(fourth[3], rim)
        call.whole(*chain)
        if earlier is not None:
            call.alias(earlier)
        call.after(*waits)
        call.out((rows[1] * tile, model), BF, rows_of(model, put))
        call.out((model, width + 256 + 128), F32)
        call.out((8, model), F32)
        call.temp((tile, channels + width + 256 + 128), BF)
        return call.run(3 + 1.5 * count)

    def input_all(m, kept, gate_back, fourth, rim, chain, pieces, waits, last_waits):
        outs = []
        size = steps // pieces
        for piece in range(pieces):
            rows = (piece * size, size)
            last = piece == pieces - 1
            most = input_back(
                m, kept, gate_back, fourth, (rows[0], rows[0] + size - last), rows, None, chain, None, *waits
            )
            waits, chain = [], most[1:3]
            if last:
                most = input_back(
                    m, kept, gate_back, fourth, (steps - 1, steps), rows, rim, chain, most[0], *last_waits
                )
                chain = most[1:3]
            outs.append(most[0])
        return outs, chain

    every = range(micro)
    kept, inner, mixes, thirds, order_by, chain = [], [], [], [], [], ()
    for m in every:
        kept.append(project(m, *order_by))
        order_by = [kept[m][8]]
    for m in every:
        inner.append(inside(m, kept[m], near_parts(kept[m][8], "seq", 1), *order_by))
        order_by = [inner[m][2]]
    for m in every:
        mixes.append(mix(m, kept[m], inner[m][0], inner[m][1], far_parts(inner[m][2], "seq", 1), *order_by))
        order_by = [mixes[m][1]]
    for m in every:
        stats = [mixes[m][1]] + [swap(mixes[m][1], "head", bits) for bits in range(1, lax.axis_size("head"))]
        thirds.append(norm(m, kept[m], mixes[m][0], inner[m][1], stats, chain, *order_by))
        chain = thirds[m][6:9]
        order_by = [thirds[m][5]]
    grad_out, grad_gate, gate_rows = chain
    early = lax.psum((grad_out, grad_gate), "seq")
    mixed_pair = [head_pair(thirds[m][0]) for m in every]
    mixed_all = [head_rest(mixed_pair[m]) for m in every]
    inner_b, fourths, token_pair, token_all, chain, chain_b = [], [], [], [], (), ()
    for m in every:
        inner_b.append(within(m, kept[m], thirds[m][2], near_parts(thirds[m][5], "seq", -1), *order_by))
        order_by = [inner_b[m][3], mixed_pair[m]]
    far_next = far_parts(inner_b[0][3], "seq", -1)
    for m in every:
        far = far_next
        if m + 1 < micro:
            far_next = far_parts(inner_b[m + 1][3], "seq", -1)
        fourths.append(across(m, kept[m], mixes[m][2], thirds[m], inner_b[m], far, chain, *order_by))
        chain = fourths[m][4:6]
        rim = from_behind(fourths[m][2], "seq", -1)
        waits = [mixed_all[m]] + (far_next if m + 1 < micro else [])
        pieces = 2 if m + 1 == micro and steps % 2 == 0 else 1
        outs, chain_b = input_all(
            m, kept[m], thirds[m][1], fourths[m], rim, chain_b, pieces, waits, [x for xs in token_all for x in xs]
        )
        token_pair.append([head_pair(out) for out in outs])
        token_all.append([head_rest(low) for low in token_pair[m]])
        order_by = [*token_pair[m]]
    tap_rows, head_rows = chain
    grads, gain_rows = chain_b

    grads, *token_pair[-1] = lax.optimization_barrier((grads, *token_pair[-1]))
    token_all[-1] = [head_rest(low) for low in token_pair[-1]]
    bc_high, bc_low = halves(grads[:, channels:width] + grads[:, width : width + 256])
    part = scatter_sum(
        jnp.concatenate([grads[:, :channels].astype(BF), bc_high, bc_low, grads[:, width + 256 :].astype(BF)], axis=1),
        "seq",
    )
    share = 2 * states // lax.axis_size("head")
    part, token_all[-1][0] = lax.optimization_barrier((part, token_all[-1][0]))
    bc_part = part[:, channels:width] + part[:, width : width + 256]
    bc_part = sum_rows([bc_part] + [swap(bc_part, "head", bits) for bits in range(1, lax.axis_size("head"))])
    bc_mine = lax.dynamic_slice_in_dim(bc_part, lax.axis_index("head") * share, share, 1)
    bc_mine, early = lax.optimization_barrier((bc_mine, early))
    gathered_low = gather_rows(
        jnp.concatenate(
            [part[:, :channels], bc_mine, part[:, width + 256 : width + 256 + heads],
             jnp.zeros((part.shape[0], 128 - share - heads), F32)], axis=1
        ).astype(BF),
        "seq",
    )
    gathered = gathered_low.astype(F32)
    grad_x = gathered[:, :channels]
    grad_bc = gathered[:, channels : channels + share]
    grad_dt = gathered[:, channels + share : channels + share + heads]

    side = lax.axis_index("head") % 2

    def half_of(value, m, begin, rows):
        return lax.dynamic_slice(value, (m, begin + side * rows, 0), (1, rows, model))[0].astype(F32)

    def place(result, m, begin, half):
        rows = half.shape[0]
        other = swap(half, "head", 1)
        result = lax.dynamic_update_slice(result, half[None], (m, begin + side * rows, 0))
        return lax.dynamic_update_slice(result, other[None], (m, begin + (1 - side) * rows, 0))

    mixed_out = jnp.zeros((micro, length, model), BF)
    for m in every:
        mixed_out = place(mixed_out, m, 0, (half_of(tokens, m, 0, length // 2) + mixed_all[m]).astype(BF))

    def finish_token(m, begin, grad_normed):
        rows = grad_normed.shape[0]
        x = half_of(tokens, m, begin, rows)
        scale = lax.rsqrt(jnp.mean(x * x, axis=1, keepdims=True) + EPS)
        grad_hat = grad_normed * norm_gain
        return (
            half_of(cotangent, m, begin, rows)
            + scale * grad_hat
            - x * scale**3 * jnp.mean(grad_hat * x, axis=1, keepdims=True)
        ).astype(BF)

    token_grad = jnp.zeros((micro, length, model), BF)
    for m in every:
        begin = 0
        for piece, grad_normed in enumerate(token_all[m]):
            if m + 1 == micro and piece + 1 == len(token_all[m]):
                grad_normed = lax.optimization_barrier((grad_normed, gathered_low))[0]
            token_grad = place(token_grad, m, begin, finish_token(m, begin, grad_normed))
            begin += 2 * grad_normed.shape[0]

    def folded(rows):
        return jnp.sum(rows.reshape(-1, 8, rows.shape[1]), axis=1)

    by_tap = folded(tap_rows)
    by_row = folded(gate_rows)
    by_head = folded(head_rows)[:, :heads]
    skip_sum = jnp.sum(by_row[1].reshape(heads, dim), axis=1)
    gain_sum = jnp.sum(gain_rows, axis=0)
    small = jnp.concatenate(
        [by_tap[:, channels:].reshape(-1), gain_sum,
         by_tap[:, :channels].reshape(-1), by_row[0], by_head.reshape(-1), skip_sum]
    )
    shared_size = by_tap[:, channels:].size + model
    small = jnp.pad(small, (0, -small.size % 1024)).reshape(-1, 128)
    small = all_sum(small, "seq")
    shared_rows = shared_size // 128
    shared = all_sum(small[:shared_rows], "head").reshape(-1)
    rest = small[shared_rows:].reshape(-1)
    tap_count = conv_x_weight.shape[0]
    bc_taps = shared[: (tap_count + 1) * 2 * states].reshape(tap_count + 1, 2 * states)
    grad_norm_gain = shared[(tap_count + 1) * 2 * states : shared_size]
    cut = (tap_count + 1) * channels
    x_taps = rest[:cut].reshape(tap_count + 1, channels)
    grad_gate_gain = rest[cut : cut + channels]
    tails = rest[cut + channels : cut + channels + 3 * heads].reshape(3, heads)
    return (
        mixed_out,
        token_grad,
        grad_norm_gain,
        jnp.stack([early[1], grad_x], axis=1),
        grad_bc,
        grad_dt,
        x_taps[:tap_count],
        x_taps[tap_count],
        bc_taps[:tap_count],
        bc_taps[tap_count],
        tails[0],
        tails[1] * decay_rate,
        tails[2],
        grad_gate_gain,
        early[0],
    )


def solution(mesh):
    in_specs = (
        P(None, "seq", None),
        P(),
        P(),
        P(None, None, "head"),
        P(),
        P(None, "head"),
        P(None, "head"),
        P("head"),
        P(),
        P(),
        P("head"),
        P("head"),
        P("head"),
        P("head"),
        P("head", None),
        P(None, "seq", None),
    )
    out_specs = (
        P(None, "seq", None),
        P(None, "seq", None),
        P(),
        P(None, None, "head"),
        P(None, "head"),
        P(None, "head"),
        P(None, "head"),
        P("head"),
        P(),
        P(),
        P("head"),
        P("head"),
        P("head"),
        P("head"),
        P("head", None),
    )
    return jax.shard_map(local, mesh=mesh, in_specs=in_specs, out_specs=out_specs, check_vma=False)
```

time: 2050 us -> 569 us (0.28)
  waiting for transfers between devices: 601 us -> 47.8 us
  other arithmetic: 480 us -> 52 us
  matrix products: 415 us -> 0 us
  Pallas kernels: 0 us -> 281 us
  local copies, waits for them, and re-layouts: 289 us -> 53.9 us
  blocking collectives: 180 us -> 0 us
  starting transfers between devices: 53.4 us -> 108 us
    psum x2 -> x1, waiting for transfers between devices: 485 us -> 0.02 us  [local(): early = lax.psum((grad_out, grad_gate), 'seq')]
    dot_general x111 -> x0, matrix products: 415 us -> none  [the longest x24 136 us: group_step(): jnp.einsum('tsh,shp->thp', weights * scores[:, :, None], scaled, precisio...]
    pallas_call x0 -> x17, Pallas kernels: none -> 281 us  [run(): pl.pallas_call(self.kernel, grid=(self.steps,), in_specs=self.in_specs, o...]
    another operation x76 -> x3, other arithmetic: 176 us -> 0.42 us
    psum x4 -> x0, blocking collectives: 103 us -> none  [the longest x1 43.1 us: local(): lax.psum((grad_gate_x, grad_bc, grad_dt, grad_conv_x, grad_conv_x_bias, g...]
    reduce_sum x44 -> x7, other arithmetic: 105 us -> 8.47 us  [the longest x1 4.57 us: finish_token(): scale = lax.rsqrt(jnp.mean(x * x, axis=1, keepdims=True) + EPS)]
    unnamed x1 -> x0, blocking collectives: 76.6 us -> none
    dynamic_update_slice x64 -> x5, other arithmetic: 86.7 us -> 16.3 us  [the longest x4 15.6 us: place(): lax.dynamic_update_slice(result, half[None], (m, begin + side * rows, 0))]
  transfers between devices with their start and end apart: 20 -> 67, of which waited for: 16 -> 13; matrix products, arithmetic and copies ran while one was open for 5% -> 17% of each run, Pallas kernels for 0% -> 46%
where the time goes in v1:
time: 569 us; the launch traced here: 558 us
  Pallas kernels  281 us (49%)
  starting transfers between devices  108 us (19%)
  local copies, waits for them, and re-layouts  53.9 us (9%)
  other arithmetic  52 us (9%)
  waiting for transfers between devices  47.8 us (8%)
  between operations  15.8 us (3%)
    pallas_call x17, Pallas kernels, run(): pl.pallas_call(self.kernel, grid=(self.steps,), in_specs=self.in_specs, o...  281 us
    ppermute x43, starting transfers between devices, swap(): return lax.ppermute(value, axis, [(i, i ^ bits) for i in range(count)])  62.7 us
    ppermute x43, waiting for transfers between devices, swap(): return lax.ppermute(value, axis, [(i, i ^ bits) for i in range(count)])  47.7 us
    ppermute x23, starting transfers between devices, from_behind(): return lax.ppermute(value, axis, [(i, i + steps) for i in sources])  45.4 us
    dynamic_update_slice x4, other arithmetic, place(): lax.dynamic_update_slice(result, half[None], (m, begin + side * rows, 0))  15.6 us
    unnamed x111, local copies, waits for them, and re-layouts  14.6 us
    add x4, other arithmetic, head_rest(): total = low.astype(F32) + swap(low, 'head', bit).astype(F32)  12.2 us
  transfers between devices with their start and end apart: 67, of which 13 were waited for; matrix products, arithmetic and copies ran while one was open for 17% of the time, Pallas kernels for 46%

profile of v1, /device:TPU:0, one launch (start us, length us, event | category | flops | bytes accessed | tf_op | source)
XLA Modules:
  0.0 558.3 jit_solution(18318264995329533844)
XLA Ops:
  8.0 4.9 collective-permute-start
  13.6 3.8 fusion.28
  21.9 23.2 %project_0.1 = (bf16[2048,768]{1,0:T(8,128)(2,1)}, f32[2048,384]{1,0:T(8,128)}, bf16[2048,640]{1,0:T(8,128)(2,1)}, f32[2048,640]{1,0:T(8,128)}, bf16[2048,640]{1...) custom-call(s32[2,9]{1,0:T(2,128)} %concatenate.28.meta, ...), custom_call_target="tpu_custom_call" | custom-call | flops 25300000768 | tf_op jit(solution)/shard_map/project_0/pallas_call | solution.py:602
  45.1 3.4 collective-permute-start.1
  48.5 3.5 collective-permute-start.2
  52.0 4.4 collective-permute-start.3
  56.5 23.3 %project_1.1 = (bf16[2048,768]{1,0:T(8,128)(2,1)}, f32[2048,384]{1,0:T(8,128)}, bf16[2048,640]{1,0:T(8,128)(2,1)}, f32[2048,640]{1,0:T(8,128)}, bf16[2048,640]{1...) custom-call(s32[2,9]{1,0:T(2,128)} %concatenate.28.meta, ...), custom_call_target="tpu_custom_call" | custom-call | flops 25300000768 | tf_op jit(solution)/shard_map/project_1/pallas_call | solution.py:602
  86.3 11.9 %inside_0.1 = (f32[2048,384]{1,0:T(8,128)}, f32[2048,384]{1,0:T(8,128)}, f32[136,384]{1,0:T(8,128)}) custom-call(s32[2,9]{1,0:T(2,128)} %concatenate.28.meta, bf16[2048,640]{1,0:T(8,128)(2,1)} %get-tuple-element.109.conv, f32[2048,128]{1,0:T(8,128)} %get-tuple-element.110.deltas, bf16[2,2048,768]{2,1,0:T(8,128)(2,1)} %cotangent.7, ...), custom_call_target="tpu_custom_call" | custom-call | flops 13799999488 | tf_op jit(solution)/shard_map/inside_0/pallas_call | solution.py:602
  102.4 11.9 %inside_1.1 = (f32[2048,384]{1,0:T(8,128)}, f32[2048,384]{1,0:T(8,128)}, f32[136,384]{1,0:T(8,128)}) custom-call(s32[2,9]{1,0:T(2,128)} %concatenate.28.meta, bf16[2048,640]{1,0:T(8,128)(2,1)} %get-tuple-element.119.conv, f32[2048,128]{1,0:T(8,128)} %get-tuple-element.120.deltas, bf16[2,2048,768]{2,1,0:T(8,128)(2,1)} %cotangent.7, ...), custom_call_target="tpu_custom_call" | custom-call | flops 13799999488 | tf_op jit(solution)/shard_map/inside_1/pallas_call | solution.py:602
  115.6 2.7 collective-permute-start.13
  119.1 13.1 %mix_0.1 = (f32[2048,384]{1,0:T(8,128)}, f32[8,2048]{1,0:T(8,128)}, f32[136,384]{1,0:T(8,128)}) custom-call(s32[2,9]{1,0:T(2,128)} %concatenate.28.meta, f32[2048,384]{1,0:T(8,128)} %get-tuple-element.113.inside, f32[2048,384]{1,0:T(8,128)} %get-tuple-element.114.back, bf16[2048,640]{1,0:T(8,128)(2,1)} %get-tuple-element.109.conv, ...), custom_call_target="tpu_custom_call" | custom-call | flops 13799999488 | tf_op jit(solution)/shard_map/mix_0/pallas_call | solution.py:602
  134.8 13.1 %mix_1.1 = (f32[2048,384]{1,0:T(8,128)}, f32[8,2048]{1,0:T(8,128)}, f32[136,384]{1,0:T(8,128)}) custom-call(s32[2,9]{1,0:T(2,128)} %concatenate.28.meta, f32[2048,384]{1,0:T(8,128)} %get-tuple-element.125.inside, f32[2048,384]{1,0:T(8,128)} %get-tuple-element.126.back, bf16[2048,640]{1,0:T(8,128)(2,1)} %get-tuple-element.119.conv, ...), custom_call_target="tpu_custom_call" | custom-call | flops 13799999488 | tf_op jit(solution)/shard_map/mix_1/pallas_call | solution.py:602
  150.6 19.4 %gate_0.1 = (bf16[2048,768]{1,0:T(8,128)(2,1)}, bf16[2048,384]{1,0:T(8,128)(2,1)}, bf16[2048,384]{1,0:T(8,128)(2,1)}, f32[16,128,384]{2,1,0:T(8,128)}, f32[16,8,...) custom-call(s32[2,9]{1,0:T(2,128)} %concatenate.28.meta, ...), custom_call_target="tpu_custom_call" | custom-call | flops 21849999360 | tf_op jit(solution)/shard_map/gate_0/pallas_call | solution.py:602
  174.5 20.2 %gate_1.1 = (bf16[2048,768]{1,0:T(8,128)(2,1)}, bf16[2048,384]{1,0:T(8,128)(2,1)}, bf16[2048,384]{1,0:T(8,128)(2,1)}, f32[16,128,384]{2,1,0:T(8,128)}, f32[16,8,...) custom-call(s32[2,9]{1,0:T(2,128)} %concatenate.28.meta, ...), custom_call_target="tpu_custom_call" | custom-call | flops 21849999360 | tf_op jit(solution)/shard_map/gate_1/pallas_call | solution.py:602
  202.2 16.1 %within_0.1 = (f32[2048,640]{1,0:T(8,128)}, f32[2048,128]{1,0:T(8,128)}, f32[2048,128]{1,0:T(8,128)}, f32[136,384]{1,0:T(8,128)}) custom-call(s32[2,9]{1,0:T(2,128)} %concatenate.28.meta, bf16[2048,640]{1,0:T(8,128)(2,1)} %get-tuple-element.109.conv, f32[2048,128]{1,0:T(8,128)} %get-tuple-element.110.deltas, bf16[2048,384]{1,0:T(8,128)(2,1)} %get-tuple-element.143.ssd_back, ...), custom_call_target="tpu_custom_call" | custom-call | flops 16099999744 | tf_op jit(solution)/shard_map/within_0/pallas_call | solution.py:602
  224.1 16.1 %within_1.1 = (f32[2048,640]{1,0:T(8,128)}, f32[2048,128]{1,0:T(8,128)}, f32[2048,128]{1,0:T(8,128)}, f32[136,384]{1,0:T(8,128)}) custom-call(s32[2,9]{1,0:T(2,128)} %concatenate.28.meta, bf16[2048,640]{1,0:T(8,128)(2,1)} %get-tuple-element.119.conv, f32[2048,128]{1,0:T(8,128)} %get-tuple-element.120.deltas, bf16[2048,384]{1,0:T(8,128)(2,1)} %get-tuple-element.152.ssd_back, ...), custom_call_target="tpu_custom_call" | custom-call | flops 16099999744 | tf_op jit(solution)/shard_map/within_1/pallas_call | solution.py:602
  243.0 3.0 add_convert_fusion.1.rest_4_
  247.2 33.9 %across_0.1 = (bf16[2048,896]{1,0:T(8,128)(2,1)}, bf16[2048,128]{1,0:T(8,128)(2,1)}, f32[16,640]{1,0:T(8,128)}, f32[16,640]{1,0:T(8,128)}, f32[40,640]{1,0:T(8,128)}, /*index=5*/f32[16,128]{1,0:T(8,128)}) custom-call(s32[2,9]{1,0:T(2,128)} %concatenate.28.meta, bf16[2048,640]{1,0:T(8,128)(2,1)} %get-tuple-element.109.conv, ...), custom_call_target="tpu_custom_call" | custom-call | flops 36800000000 | tf_op jit(solution)/shard_map/across_0/pallas_call | solution.py:602
  282.4 3.4 convert_add_fusion.5.rest_0_
  286.5 13.1 %input_0_0.1 = (bf16[2048,768]{1,0:T(8,128)(2,1)}, f32[768,1024]{1,0:T(8,128)}, f32[8,768]{1,0:T(8,128)}) custom-call(bf16[2,2048,768]{2,1,0:T(8,128)(2,1)} %tokens.13, bf16[2048,768]{1,0:T(8,128)(2,1)} %get-tuple-element.123.normed, bf16[2048,384]{1,0:T(8,128)(2,1)} %get-tuple-element.139.gate_back, bf16[2048,896]{1,0:T(8,128)(2,1)} %get-tuple-element.154.in_back, ...), custom_call_target="tpu_custom_call" | custom-call | flops 15525000192 | tf_op jit(solution)/shard_map/input_0_0/pallas_call | solution.py:602
  300.3 5.9 %input_0_7.1 = (bf16[2048,768]{1,0:T(8,128)(2,1)}, f32[768,1024]{1,0:T(8,128)}, f32[8,768]{1,0:T(8,128)}) custom-call(bf16[2,2048,768]{2,1,0:T(8,128)(2,1)} %tokens.13, bf16[2048,768]{1,0:T(8,128)(2,1)} %get-tuple-element.123.normed, bf16[2048,384]{1,0:T(8,128)(2,1)} %get-tuple-element.139.gate_back, ...), custom_call_target="tpu_custom_call", output_to_operand_aliasing={{0}: (10, {})} | custom-call | flops 5175000064 | tf_op jit(solution)/shard_map/input_0_7/pallas_call | solution.py:602
  309.6 3.7 bitcast_dynamic-update-slice_fusion.5
  313.8 6.0 %convert_add_fusion.4.rest_2_ = f32[1024,768]{1,0:T(8,128)} fusion(bf16[1024,768]{1,0:T(8,128)(2,1)S(1)} %collective-permute-done.21, bf16[1024,768]{1,0:T(8,128)(2,1)} %add_convert_fusion.1.rest_4_), kind=kLoop, calls=%fused_computation.15 | loop fusion | flops 2359296 | bytes 6291456 | tf_op jit(solution)/shard_map/add | solution.py:673
  319.8 3.0 add_convert_fusion.rest_5_
  324.3 34.1 %across_1.1 = (bf16[2048,896]{1,0:T(8,128)(2,1)}, bf16[2048,128]{1,0:T(8,128)(2,1)}, f32[16,640]{1,0:T(8,128)}, f32[16,640]{1,0:T(8,128)}, f32[40,640]{1,0:T(8,128)}, /*index=5*/f32[16,128]{1,0:T(8,128)}) custom-call(s32[2,9]{1,0:T(2,128)} %concatenate.28.meta, bf16[2048,640]{1,0:T(8,128)(2,1)} %get-tuple-element.119.conv, ...), custom_call_target="tpu_custom_call" | custom-call | flops 36800000000 | tf_op jit(solution)/shard_map/across_1/pallas_call | solution.py:602
  360.9 10.2 %input_1_0.1 = (bf16[1024,768]{1,0:T(8,128)(2,1)}, f32[768,1024]{1,0:T(8,128)}, f32[8,768]{1,0:T(8,128)}) custom-call(bf16[2,2048,768]{2,1,0:T(8,128)(2,1)} %tokens.13, bf16[2048,768]{1,0:T(8,128)(2,1)} %get-tuple-element.133.normed, bf16[2048,384]{1,0:T(8,128)(2,1)} %get-tuple-element.162.gate_back, bf16[2048,896]{1,0:T(8,128)(2,1)} %get-tuple-element.174.in_back, ...), custom_call_target="tpu_custom_call" | custom-call | flops 10350000128 | tf_op jit(solution)/shard_map/input_1_0/pallas_call | solution.py:602
  373.4 2.7 bitcast_dynamic-update-slice_fusion.4
  376.0 9.2 %input_1_4.1 = (bf16[1024,768]{1,0:T(8,128)(2,1)}, f32[768,1024]{1,0:T(8,128)}, f32[8,768]{1,0:T(8,128)}) custom-call(bf16[2,2048,768]{2,1,0:T(8,128)(2,1)} %tokens.13, bf16[2048,768]{1,0:T(8,128)(2,1)} %get-tuple-element.133.normed, bf16[2048,384]{1,0:T(8,128)(2,1)} %get-tuple-element.162.gate_back, bf16[2048,896]{1,0:T(8,128)(2,1)} %get-tuple-element.174.in_back, ...), custom_call_target="tpu_custom_call" | custom-call | flops 8625000448 | tf_op jit(solution)/shard_map/input_1_4/pallas_call | solution.py:602
  387.5 4.6 fusion.1
  392.7 5.9 %input_1_7.1 = (bf16[1024,768]{1,0:T(8,128)(2,1)}, f32[768,1024]{1,0:T(8,128)}, f32[8,768]{1,0:T(8,128)}) custom-call(bf16[2,2048,768]{2,1,0:T(8,128)(2,1)} %tokens.13, bf16[2048,768]{1,0:T(8,128)(2,1)} %get-tuple-element.133.normed, bf16[2048,384]{1,0:T(8,128)(2,1)} %get-tuple-element.162.gate_back, ...), custom_call_target="tpu_custom_call", output_to_operand_aliasing={{0}: (10, {})} | custom-call | flops 5175000064 | tf_op jit(solution)/shard_map/input_1_7/pallas_call | solution.py:602
  402.1 4.3 collective-permute-start.61
  406.9 5.8 %bitcast_dynamic-update-slice_fusion.1 = (bf16[2,2048,768]{2,1,0:T(8,128)(2,1)S(1)}, bf16[1024,768]{1,0:T(8,128)(2,1)}, bf16[2,2048,768]{2,1,0:T(8,128)(2,1)}, bf16[1024,768]{1,0:T(8,128)(2,1)}) fusion(bf16[2,2048,768]{2,1,0:T(8,128)(2,1)S(1)} %broadcast.108, s32[]{:T(128)S(6)} %select_n.101, f32[1024]{0:T(1024)S(1)} %get-tuple-element.280, ...), kind=kLoop, calls=%fused_computation.40 | loop fusion | flops 14155776 | bytes 17317892 | tf_op jit(solution)/shard_map/dynamic_update_slice | solution.py:1030
  412.9 5.0 collective-permute-start.62
  421.2 5.4 collective-permute-start.46
  428.0 9.6 %collective-permute-done.63 = f32[40,128]{1,0:T(8,128)S(1)} collective-permute-done((f32[40,128]{1,0:T(8,128)S(1)}, f32[40,128]{1,0:T(8,128)S(1)}, u32[]{:S(2)}, u32[]{:S(2)}) %collective-permute-start.63) | collective-permute-done | bytes 20512 | tf_op jit(solution)/shard_map/ppermute | solution.py:620
  439.7 4.2 collective-permute-start.43
  443.9 3.5 collective-permute-done.45
  447.4 11.3 %collective-permute-start.42 = (bf16[96,1024]{1,0:T(8,128)(2,1)}, bf16[96,1024]{1,0:T(8,128)(2,1)S(1)}, u32[]{:S(2)}, u32[]{:S(2)}) collective-permute-start(bf16[96,1024]{1,0:T(8,128)(2,1)} %get-tuple-element.265), channel_id=1, source_target_pairs={{0,12},{4,8},{8,4},{12,0},{16,28},{20,24},{24,20},{28,16},{1,13},{... | collective-permute-start | bytes 589832 | tf_op jit(solution)/shard_map/ppermute | solution.py:620
  458.7 3.7 collective-permute-done.44
  466.3 2.9 collective-permute-done.42
  470.1 3.0 collective-permute-start.49
  479.4 13.8 %collective-permute-done.52 = f32[96,256]{1,0:T(8,128)S(1)} collective-permute-done((f32[96,256]{1,0:T(8,128)S(1)}, f32[96,256]{1,0:T(8,128)S(1)}, u32[]{:S(2)}, u32[]{:S(2)}) %collective-permute-start.52) | collective-permute-done | bytes 98336 | tf_op jit(solution)/shard_map/ppermute | solution.py:620
  499.2 2.8 collective-permute-start.55
  510.2 5.1 collective-permute-done.56
  519.7 2.9 collective-permute-done.59
  525.4 3.0 bitcast_dynamic-update-slice_fusion.9
  533.7 3.0 bitcast_dynamic-update-slice_fusion.7
  544.2 3.2 copy.47
  (323 shorter events, 120.1 us)
Async XLA Ops:
  7.2 488.0 %all-reduce.13.cloned.1.call-start = ((), (), s32[]{:S(2)}) async-start(), calls=%async_computation | async-start | bytes 4718592 | tf_op jit(solution)/shard_map/psum | solution.py:971
  45.1 39.1 %collective-permute-start.1 = (f32[136,384]{1,0:T(8,128)}, f32[136,384]{1,0:T(8,128)S(1)}, u32[]{:S(2)}, u32[]{:S(2)}) collective-permute-start(f32[136,384]{1,0:T(8,128)} %get-tuple-element.111.rest_0_), channel_id=1, source_target_pairs={{0,4},{4,8},{8,12},{12,16},{16,20},{20,24},{24,28},{1,5},{5,9},{9,... | collective-permute-start | bytes 626696 | tf_op jit(solution)/shard_map/ppermute | solution.py:626
  48.5 37.1 %collective-permute-start.2 = (f32[136,384]{1,0:T(8,128)}, f32[136,384]{1,0:T(8,128)S(1)}, u32[]{:S(2)}, u32[]{:S(2)}) collective-permute-start(f32[136,384]{1,0:T(8,128)} %get-tuple-element.111.rest_0_), channel_id=1, source_target_pairs={{0,8},{4,12},{8,16},{12,20},{16,24},{20,28},{1,9},{5,13},{9,17},{1... | collective-permute-start | bytes 626696 | tf_op jit(solution)/shard_map/ppermute | solution.py:626
  52.0 33.6 %collective-permute-start.3 = (f32[136,384]{1,0:T(8,128)}, f32[136,384]{1,0:T(8,128)S(1)}, u32[]{:S(2)}, u32[]{:S(2)}) collective-permute-start(f32[136,384]{1,0:T(8,128)} %get-tuple-element.111.rest_0_), channel_id=1, source_target_pairs={{0,12},{4,16},{8,20},{12,24},{16,28},{1,13},{5,17},{9,21},{13,25},... | collective-permute-start | bytes 626696 | tf_op jit(solution)/shard_map/ppermute | solution.py:626
  79.8 21.7 %collective-permute-start.6 = (f32[136,384]{1,0:T(8,128)}, f32[136,384]{1,0:T(8,128)S(1)}, u32[]{:S(2)}, u32[]{:S(2)}) collective-permute-start(f32[136,384]{1,0:T(8,128)} %get-tuple-element.112.rest_3_), channel_id=1, source_target_pairs={{0,4},{4,8},{8,12},{12,16},{16,20},{20,24},{24,28},{1,5},{5,9},{9,... | collective-permute-start | bytes 626696 | tf_op jit(solution)/shard_map/ppermute | solution.py:626
  81.7 19.8 %collective-permute-start.7 = (f32[136,384]{1,0:T(8,128)}, f32[136,384]{1,0:T(8,128)S(1)}, u32[]{:S(2)}, u32[]{:S(2)}) collective-permute-start(f32[136,384]{1,0:T(8,128)} %get-tuple-element.112.rest_3_), channel_id=1, source_target_pairs={{0,8},{4,12},{8,16},{12,20},{16,24},{20,28},{1,9},{5,13},{9,17},{1... | collective-permute-start | bytes 626696 | tf_op jit(solution)/shard_map/ppermute | solution.py:626
  84.2 17.3 %collective-permute-start.8 = (f32[136,384]{1,0:T(8,128)}, f32[136,384]{1,0:T(8,128)S(1)}, u32[]{:S(2)}, u32[]{:S(2)}) collective-permute-start(f32[136,384]{1,0:T(8,128)} %get-tuple-element.112.rest_3_), channel_id=1, source_target_pairs={{0,12},{4,16},{8,20},{12,24},{16,28},{1,13},{5,17},{9,21},{13,25},... | collective-permute-start | bytes 626696 | tf_op jit(solution)/shard_map/ppermute | solution.py:626
  98.3 20.0 %collective-permute-start.4 = (f32[136,384]{1,0:T(8,128)}, f32[136,384]{1,0:T(8,128)S(1)}, u32[]{:S(2)}, u32[]{:S(2)}) collective-permute-start(f32[136,384]{1,0:T(8,128)} %get-tuple-element.118.rest_3_.rest_0_), channel_id=1, source_target_pairs={{0,12},{4,16},{8,20},{12,24},{16,28},{1,13},{5,17},{9,21},{13,25},... | collective-permute-start | bytes 626696 | tf_op jit(solution)/shard_map/ppermute | solution.py:626
  100.2 18.1 %collective-permute-start.5 = (f32[136,384]{1,0:T(8,128)}, f32[136,384]{1,0:T(8,128)S(1)}, u32[]{:S(2)}, u32[]{:S(2)}) collective-permute-start(f32[136,384]{1,0:T(8,128)} %get-tuple-element.118.rest_3_.rest_0_), channel_id=1, source_target_pairs={{0,24},{4,28},{1,25},{5,29},{2,26},{6,30},{3,27},{7,31}} | collective-permute-start | bytes 626696 | tf_op jit(solution)/shard_map/ppermute | solution.py:626
  114.3 19.8 %collective-permute-start.12 = (f32[136,384]{1,0:T(8,128)}, f32[136,384]{1,0:T(8,128)S(1)}, u32[]{:S(2)}, u32[]{:S(2)}) collective-permute-start(f32[136,384]{1,0:T(8,128)} %get-tuple-element.121.rest_3_.rest_0_), channel_id=1, source_target_pairs={{0,12},{4,16},{8,20},{12,24},{16,28},{1,13},{5,17},{9,21},{13,25},... | collective-permute-start | bytes 626696 | tf_op jit(solution)/shard_map/ppermute | solution.py:626
  115.6 18.5 %collective-permute-start.13 = (f32[136,384]{1,0:T(8,128)}, f32[136,384]{1,0:T(8,128)S(1)}, u32[]{:S(2)}, u32[]{:S(2)}) collective-permute-start(f32[136,384]{1,0:T(8,128)} %get-tuple-element.121.rest_3_.rest_0_), channel_id=1, source_target_pairs={{0,24},{4,28},{1,25},{5,29},{2,26},{6,30},{3,27},{7,31}} | collective-permute-start | bytes 626696 | tf_op jit(solution)/shard_map/ppermute | solution.py:626
  132.1 17.7 %collective-permute-start.9 = (f32[8,2048]{1,0:T(8,128)}, f32[8,2048]{1,0:T(8,128)S(1)}, u32[]{:S(2)}, u32[]{:S(2)}) collective-permute-start(f32[8,2048]{1,0:T(8,128)} %get-tuple-element.124.rest_3_.stats_a), channel_id=1, source_target_pairs={{0,1},{1,0},{2,3},{3,2},{4,5},{5,4},{6,7},{7,6},{8,9},{9,8},{10,11... | collective-permute-start | bytes 196616 | tf_op jit(solution)/shard_map/ppermute | solution.py:620
  132.2 17.7 %collective-permute-start.10 = (f32[8,2048]{1,0:T(8,128)}, f32[8,2048]{1,0:T(8,128)S(1)}, u32[]{:S(2)}, u32[]{:S(2)}) collective-permute-start(f32[8,2048]{1,0:T(8,128)} %get-tuple-element.124.rest_3_.stats_a), channel_id=1, source_target_pairs={{0,2},{1,3},{2,0},{3,1},{4,6},{5,7},{6,4},{7,5},{8,10},{9,11},{10,... | collective-permute-start | bytes 196616 | tf_op jit(solution)/shard_map/ppermute | solution.py:620
  133.8 16.1 %collective-permute-start.11 = (f32[8,2048]{1,0:T(8,128)}, f32[8,2048]{1,0:T(8,128)S(1)}, u32[]{:S(2)}, u32[]{:S(2)}) collective-permute-start(f32[8,2048]{1,0:T(8,128)} %get-tuple-element.124.rest_3_.stats_a), channel_id=1, source_target_pairs={{0,3},{1,2},{2,1},{3,0},{4,7},{5,6},{6,5},{7,4},{8,11},{9,10},{10,... | collective-permute-start | bytes 196616 | tf_op jit(solution)/shard_map/ppermute | solution.py:620
  147.9 24.6 %collective-permute-start.17 = (f32[8,2048]{1,0:T(8,128)}, f32[8,2048]{1,0:T(8,128)S(1)}, u32[]{:S(2)}, u32[]{:S(2)}) collective-permute-start(f32[8,2048]{1,0:T(8,128)} %get-tuple-element.130.rest_0_.stats_a), channel_id=1, source_target_pairs={{0,1},{1,0},{2,3},{3,2},{4,5},{5,4},{6,7},{7,6},{8,9},{9,8},{10,11... | collective-permute-start | bytes 196616 | tf_op jit(solution)/shard_map/ppermute | solution.py:620
  148.4 25.5 %collective-permute-start.18 = (f32[8,2048]{1,0:T(8,128)}, f32[8,2048]{1,0:T(8,128)S(1)}, u32[]{:S(2)}, u32[]{:S(2)}) collective-permute-start(f32[8,2048]{1,0:T(8,128)} %get-tuple-element.130.rest_0_.stats_a), channel_id=1, source_target_pairs={{0,2},{1,3},{2,0},{3,1},{4,6},{5,7},{6,4},{7,5},{8,10},{9,11},{10,... | collective-permute-start | bytes 196616 | tf_op jit(solution)/shard_map/ppermute | solution.py:620
  149.9 24.0 %collective-permute-start.19 = (f32[8,2048]{1,0:T(8,128)}, f32[8,2048]{1,0:T(8,128)S(1)}, u32[]{:S(2)}, u32[]{:S(2)}) collective-permute-start(f32[8,2048]{1,0:T(8,128)} %get-tuple-element.130.rest_0_.stats_a), channel_id=1, source_target_pairs={{0,3},{1,2},{2,1},{3,0},{4,7},{5,6},{6,5},{7,4},{8,11},{9,10},{10,... | collective-permute-start | bytes 196616 | tf_op jit(solution)/shard_map/ppermute | solution.py:620
  169.9 29.6 %collective-permute-start.23 = (f32[136,384]{1,0:T(8,128)}, f32[136,384]{1,0:T(8,128)}, u32[]{:S(2)}, u32[]{:S(2)}) collective-permute-start(f32[136,384]{1,0:T(8,128)} %get-tuple-element.137.rest_3_), channel_id=1, source_target_pairs={{4,0},{8,4},{12,8},{16,12},{20,16},{24,20},{28,24},{5,1},{9,5},{13... | collective-permute-start | bytes 626696 | tf_op jit(solution)/shard_map/ppermute | solution.py:626
  171.2 29.6 %collective-permute-start.24 = (f32[136,384]{1,0:T(8,128)}, f32[136,384]{1,0:T(8,128)}, u32[]{:S(2)}, u32[]{:S(2)}) collective-permute-start(f32[136,384]{1,0:T(8,128)} %get-tuple-element.137.rest_3_), channel_id=1, source_target_pairs={{8,0},{12,4},{16,8},{20,12},{24,16},{28,20},{9,1},{13,5},{17,9},{2... | collective-permute-start | bytes 626696 | tf_op jit(solution)/shard_map/ppermute | solution.py:626
  172.5 29.6 %collective-permute-start.25 = (f32[136,384]{1,0:T(8,128)}, f32[136,384]{1,0:T(8,128)}, u32[]{:S(2)}, u32[]{:S(2)}) collective-permute-start(f32[136,384]{1,0:T(8,128)} %get-tuple-element.137.rest_3_), channel_id=1, source_target_pairs={{12,0},{16,4},{20,8},{24,12},{28,16},{13,1},{17,5},{21,9},{25,13},... | collective-permute-start | bytes 626696 | tf_op jit(solution)/shard_map/ppermute | solution.py:626
  194.7 26.5 %collective-permute-start.28 = (f32[136,384]{1,0:T(8,128)}, f32[136,384]{1,0:T(8,128)}, u32[]{:S(2)}, u32[]{:S(2)}) collective-permute-start(f32[136,384]{1,0:T(8,128)} %get-tuple-element.144.rest_3_), channel_id=1, source_target_pairs={{4,0},{8,4},{12,8},{16,12},{20,16},{24,20},{28,24},{5,1},{9,5},{13... | collective-permute-start | bytes 626696 | tf_op jit(solution)/shard_map/ppermute | solution.py:626
  197.6 20.7 %collective-permute-start.14 = (bf16[1024,768]{1,0:T(8,128)(2,1)}, bf16[1024,768]{1,0:T(8,128)(2,1)S(1)}, u32[]{:S(2)}, u32[]{:S(2)}) collective-permute-start(bf16[1024,768]{1,0:T(8,128)(2,1)} %constant_dynamic-slice_fusion.11), channel_id=1, source_target_pairs={{0,1},{1,0},{2,3},{3,2},{4,5},{5,4},{6,7},{7,6},{8,9},{9,8},{10,11... | collective-permute-start | bytes 4718600 | tf_op jit(solution)/shard_map/ppermute | solution.py:620
  199.5 22.9 %collective-permute-start.29 = (f32[136,384]{1,0:T(8,128)S(1)}, f32[136,384]{1,0:T(8,128)}, u32[]{:S(2)}, u32[]{:S(2)}) collective-permute-start(f32[136,384]{1,0:T(8,128)S(1)} %copy-done.31), channel_id=1, source_target_pairs={{8,0},{12,4},{16,8},{20,12},{24,16},{28,20},{9,1},{13,5},{17,9},{2... | collective-permute-start | bytes 626696 | tf_op jit(solution)/shard_map/ppermute | solution.py:626
  200.8 23.2 %collective-permute-start.30 = (f32[136,384]{1,0:T(8,128)S(1)}, f32[136,384]{1,0:T(8,128)}, u32[]{:S(2)}, u32[]{:S(2)}) collective-permute-start(f32[136,384]{1,0:T(8,128)S(1)} %copy-done.31), channel_id=1, source_target_pairs={{12,0},{16,4},{20,8},{24,12},{28,16},{13,1},{17,5},{21,9},{25,13},... | collective-permute-start | bytes 626696 | tf_op jit(solution)/shard_map/ppermute | solution.py:626
  202.1 39.3 %collective-permute-start.20 = (bf16[1024,768]{1,0:T(8,128)(2,1)}, bf16[1024,768]{1,0:T(8,128)(2,1)}, u32[]{:S(2)}, u32[]{:S(2)}) collective-permute-start(bf16[1024,768]{1,0:T(8,128)(2,1)} %constant_dynamic-slice_fusion.10), channel_id=1, source_target_pairs={{0,1},{1,0},{2,3},{3,2},{4,5},{5,4},{6,7},{7,6},{8,9},{9,8},{10,11... | collective-permute-start | bytes 4718600 | tf_op jit(solution)/shard_map/ppermute | solution.py:620
  218.3 27.7 %collective-permute-start.26 = (f32[136,384]{1,0:T(8,128)}, f32[136,384]{1,0:T(8,128)}, u32[]{:S(2)}, u32[]{:S(2)}) collective-permute-start(f32[136,384]{1,0:T(8,128)} %get-tuple-element.151.rest_3_.rest_0_), channel_id=1, source_target_pairs={{12,0},{16,4},{20,8},{24,12},{28,16},{13,1},{17,5},{21,9},{25,13},... | collective-permute-start | bytes 626696 | tf_op jit(solution)/shard_map/ppermute | solution.py:626
  221.2 25.3 %collective-permute-start.27 = (f32[136,384]{1,0:T(8,128)}, f32[136,384]{1,0:T(8,128)S(1)}, u32[]{:S(2)}, u32[]{:S(2)}) collective-permute-start(f32[136,384]{1,0:T(8,128)} %get-tuple-element.151.rest_3_.rest_0_), channel_id=1, source_target_pairs={{24,0},{28,4},{25,1},{29,5},{26,2},{30,6},{27,3},{31,7}} | collective-permute-start | bytes 626696 | tf_op jit(solution)/shard_map/ppermute | solution.py:626
  222.5 59.9 %collective-permute-start.15 = (bf16[1024,768]{1,0:T(8,128)(2,1)}, bf16[1024,768]{1,0:T(8,128)(2,1)S(1)}, u32[]{:S(2)}, u32[]{:S(2)}) collective-permute-start(bf16[1024,768]{1,0:T(8,128)(2,1)} %add_convert_fusion.2.rest_4_), channel_id=1, source_target_pairs={{0,2},{1,3},{2,0},{3,1},{4,6},{5,7},{6,4},{7,5},{8,10},{9,11},{10,... | collective-permute-start | bytes 4718600 | tf_op jit(solution)/shard_map/ppermute | solution.py:620
  240.2 45.6 %collective-permute-start.32 = (f32[136,384]{1,0:T(8,128)}, f32[136,384]{1,0:T(8,128)S(1)}, u32[]{:S(2)}, u32[]{:S(2)}) collective-permute-start(f32[136,384]{1,0:T(8,128)} %get-tuple-element.153.rest_3_.rest_1_.rest_0_), channel_id=1, source_target_pairs={{12,0},{16,4},{20,8},{24,12},{28,16},{13,1},{17,5},{21,9},{25,13},... | collective-permute-start | bytes 626696 | tf_op jit(solution)/shard_map/ppermute | solution.py:626
  241.5 44.3 %collective-permute-start.33 = (f32[136,384]{1,0:T(8,128)}, f32[136,384]{1,0:T(8,128)S(1)}, u32[]{:S(2)}, u32[]{:S(2)}) collective-permute-start(f32[136,384]{1,0:T(8,128)} %get-tuple-element.153.rest_3_.rest_1_.rest_0_), channel_id=1, source_target_pairs={{24,0},{28,4},{25,1},{29,5},{26,2},{30,6},{27,3},{31,7}} | collective-permute-start | bytes 626696 | tf_op jit(solution)/shard_map/ppermute | solution.py:626
  245.9 67.9 %collective-permute-start.21 = (bf16[1024,768]{1,0:T(8,128)(2,1)}, bf16[1024,768]{1,0:T(8,128)(2,1)S(1)}, u32[]{:S(2)}, u32[]{:S(2)}) collective-permute-start(bf16[1024,768]{1,0:T(8,128)(2,1)} %add_convert_fusion.1.rest_4_), channel_id=1, source_target_pairs={{0,2},{1,3},{2,0},{3,1},{4,6},{5,7},{6,4},{7,5},{8,10},{9,11},{10,... | collective-permute-start | bytes 4718600 | tf_op jit(solution)/shard_map/ppermute | solution.py:620
  281.1 18.6 %collective-permute-start.31 = (f32[16,640]{1,0:T(8,128)}, f32[16,640]{1,0:T(8,128)S(1)}, u32[]{:S(2)}, u32[]{:S(2)}) collective-permute-start(f32[16,640]{1,0:T(8,128)} %get-tuple-element.157), channel_id=1, source_target_pairs={{4,0},{8,4},{12,8},{16,12},{20,16},{24,20},{28,24},{5,1},{9,5},{13... | collective-permute-start | bytes 122888 | tf_op jit(solution)/shard_map/ppermute | solution.py:626
  313.3 60.1 %collective-permute-start.16 = (bf16[1024,768]{1,0:T(8,128)(2,1)}, bf16[1024,768]{1,0:T(8,128)(2,1)}, u32[]{:S(2)}, u32[]{:S(2)}) collective-permute-start(bf16[1024,768]{1,0:T(8,128)(2,1)} %get-tuple-element.256), channel_id=1, source_target_pairs={{0,1},{1,0},{2,3},{3,2},{4,5},{5,4},{6,7},{7,6},{8,9},{9,8},{10,11... | collective-permute-start | bytes 4718600 | tf_op jit(solution)/shard_map/ppermute | solution.py:620
  322.8 64.7 %collective-permute-start.35 = (bf16[1024,768]{1,0:T(8,128)(2,1)}, bf16[1024,768]{1,0:T(8,128)(2,1)S(1)}, u32[]{:S(2)}, u32[]{:S(2)}) collective-permute-start(bf16[1024,768]{1,0:T(8,128)(2,1)} %add_convert_fusion.rest_5_), channel_id=1, source_target_pairs={{0,2},{1,3},{2,0},{3,1},{4,6},{5,7},{6,4},{7,5},{8,10},{9,11},{10,... | collective-permute-start | bytes 4718600 | tf_op jit(solution)/shard_map/ppermute | solution.py:620
  359.4 32.7 %collective-permute-start.37 = (f32[16,640]{1,0:T(8,128)}, f32[16,640]{1,0:T(8,128)S(1)}, u32[]{:S(2)}, u32[]{:S(2)}) collective-permute-start(f32[16,640]{1,0:T(8,128)} %get-tuple-element.177), channel_id=1, source_target_pairs={{4,0},{8,4},{12,8},{16,12},{20,16},{24,20},{28,24},{5,1},{9,5},{13... | collective-permute-start | bytes 122888 | tf_op jit(solution)/shard_map/ppermute | solution.py:626
  400.8 17.1 %collective-permute-start.39 = (bf16[512,768]{1,0:T(8,128)(2,1)}, bf16[512,768]{1,0:T(8,128)(2,1)}, u32[]{:S(2)}, u32[]{:S(2)}) collective-permute-start(bf16[512,768]{1,0:T(8,128)(2,1)} %constant_dynamic-slice_fusion.7), channel_id=1, source_target_pairs={{0,1},{1,0},{2,3},{3,2},{4,5},{5,4},{6,7},{7,6},{8,9},{9,8},{10,11... | collective-permute-start | bytes 2359304 | tf_op jit(solution)/shard_map/ppermute | solution.py:620
  412.8 63.4 %collective-permute-start.36 = (bf16[1024,768]{1,0:T(8,128)(2,1)}, bf16[1024,768]{1,0:T(8,128)(2,1)}, u32[]{:S(2)}, u32[]{:S(2)}) collective-permute-start(bf16[1024,768]{1,0:T(8,128)(2,1)} %get-tuple-element.252), channel_id=1, source_target_pairs={{0,1},{1,0},{2,3},{3,2},{4,5},{5,4},{6,7},{7,6},{8,9},{9,8},{10,11... | collective-permute-start | bytes 4718600 | tf_op jit(solution)/shard_map/ppermute | solution.py:620
  421.2 18.5 %collective-permute-start.46 = (bf16[96,1024]{1,0:T(8,128)(2,1)}, bf16[96,1024]{1,0:T(8,128)(2,1)S(1)}, u32[]{:S(2)}, u32[]{:S(2)}) collective-permute-start(bf16[96,1024]{1,0:T(8,128)(2,1)} %get-tuple-element.261), channel_id=1, source_target_pairs={{0,28},{4,24},{8,20},{12,16},{16,12},{20,8},{24,4},{28,0},{1,29},{... | collective-permute-start | bytes 589832 | tf_op jit(solution)/shard_map/ppermute | solution.py:620
  426.5 46.9 %collective-permute-start.47 = (bf16[512,768]{1,0:T(8,128)(2,1)S(1)}, bf16[512,768]{1,0:T(8,128)(2,1)}, u32[]{:S(2)}, u32[]{:S(2)}) collective-permute-start(bf16[512,768]{1,0:T(8,128)(2,1)S(1)} %copy-done.8), channel_id=1, source_target_pairs={{0,2},{1,3},{2,0},{3,1},{4,6},{5,7},{6,4},{7,5},{8,10},{9,11},{10,... | collective-permute-start | bytes 2359304 | tf_op jit(solution)/shard_map/ppermute | solution.py:620
  439.7 22.7 %collective-permute-start.44 = (bf16[96,1024]{1,0:T(8,128)(2,1)}, bf16[96,1024]{1,0:T(8,128)(2,1)S(1)}, u32[]{:S(2)}, u32[]{:S(2)}) collective-permute-start(bf16[96,1024]{1,0:T(8,128)(2,1)} %get-tuple-element.263), channel_id=1, source_target_pairs={{0,20},{4,16},{8,28},{12,24},{16,4},{20,0},{24,12},{28,8},{1,21},{... | collective-permute-start | bytes 589832 | tf_op jit(solution)/shard_map/ppermute | solution.py:620
  439.7 24.2 %collective-permute-start.43 = (bf16[96,1024]{1,0:T(8,128)(2,1)}, bf16[96,1024]{1,0:T(8,128)(2,1)S(1)}, u32[]{:S(2)}, u32[]{:S(2)}) collective-permute-start(bf16[96,1024]{1,0:T(8,128)(2,1)} %get-tuple-element.264), channel_id=1, source_target_pairs={{0,16},{4,20},{8,24},{12,28},{16,0},{20,4},{24,8},{28,12},{1,17},{... | collective-permute-start | bytes 589832 | tf_op jit(solution)/shard_map/ppermute | solution.py:620
  447.4 21.7 %collective-permute-start.42 = (bf16[96,1024]{1,0:T(8,128)(2,1)}, bf16[96,1024]{1,0:T(8,128)(2,1)S(1)}, u32[]{:S(2)}, u32[]{:S(2)}) collective-permute-start(bf16[96,1024]{1,0:T(8,128)(2,1)} %get-tuple-element.265), channel_id=1, source_target_pairs={{0,12},{4,8},{8,4},{12,0},{16,28},{20,24},{24,20},{28,16},{1,13},{... | collective-permute-start | bytes 589832 | tf_op jit(solution)/shard_map/ppermute | solution.py:620
  469.2 68.7 %collective-permute-start.22 = (bf16[1024,768]{1,0:T(8,128)(2,1)}, bf16[1024,768]{1,0:T(8,128)(2,1)}, u32[]{:S(2)}, u32[]{:S(2)}) collective-permute-start(bf16[1024,768]{1,0:T(8,128)(2,1)} %get-tuple-element.258), channel_id=1, source_target_pairs={{0,1},{1,0},{2,3},{3,2},{4,5},{5,4},{6,7},{7,6},{8,9},{9,8},{10,11... | collective-permute-start | bytes 4718600 | tf_op jit(solution)/shard_map/ppermute | solution.py:620
  470.1 27.5 %collective-permute-start.49 = (bf16[512,768]{1,0:T(8,128)(2,1)S(1)}, bf16[512,768]{1,0:T(8,128)(2,1)}, u32[]{:S(2)}, u32[]{:S(2)}) collective-permute-start(bf16[512,768]{1,0:T(8,128)(2,1)S(1)} %add_convert_fusion.3), channel_id=1, source_target_pairs={{0,2},{1,3},{2,0},{3,1},{4,6},{5,7},{6,4},{7,5},{8,10},{9,11},{10,... | collective-permute-start | bytes 2359304 | tf_op jit(solution)/shard_map/ppermute | solution.py:620
  474.7 18.4 %collective-permute-start.52 = (f32[96,256]{1,0:T(8,128)S(1)}, f32[96,256]{1,0:T(8,128)S(1)}, u32[]{:S(2)}, u32[]{:S(2)}) collective-permute-start(f32[96,256]{1,0:T(8,128)S(1)} %slice_add_fusion.1), channel_id=1, source_target_pairs={{0,3},{1,2},{2,1},{3,0},{4,7},{5,6},{6,5},{7,4},{8,11},{9,10},{10,... | collective-permute-start | bytes 294920 | tf_op jit(solution)/shard_map/ppermute | solution.py:620
  474.9 20.2 %collective-permute-start.51 = (f32[96,256]{1,0:T(8,128)S(1)}, f32[96,256]{1,0:T(8,128)S(1)}, u32[]{:S(2)}, u32[]{:S(2)}) collective-permute-start(f32[96,256]{1,0:T(8,128)S(1)} %slice_add_fusion.1), channel_id=1, source_target_pairs={{0,2},{1,3},{2,0},{3,1},{4,6},{5,7},{6,4},{7,5},{8,10},{9,11},{10,... | collective-permute-start | bytes 294920 | tf_op jit(solution)/shard_map/ppermute | solution.py:620
  476.1 18.9 %collective-permute-start.50 = (f32[96,256]{1,0:T(8,128)S(1)}, f32[96,256]{1,0:T(8,128)S(1)}, u32[]{:S(2)}, u32[]{:S(2)}) collective-permute-start(f32[96,256]{1,0:T(8,128)S(1)} %slice_add_fusion.1), channel_id=1, source_target_pairs={{0,1},{1,0},{2,3},{3,2},{4,5},{5,4},{6,7},{7,6},{8,9},{9,8},{10,11... | collective-permute-start | bytes 294920 | tf_op jit(solution)/shard_map/ppermute | solution.py:620
  493.2 35.2 %collective-permute-start.64 = (f32[16,128]{1,0:T(8,128)S(1)}, f32[16,128]{1,0:T(8,128)S(1)}, u32[]{:S(2)}, u32[]{:S(2)}) collective-permute-start(f32[16,128]{1,0:T(8,128)S(1)} %slice.167), channel_id=1, source_target_pairs={{0,1},{1,0},{2,3},{3,2},{4,5},{5,4},{6,7},{7,6},{8,9},{9,8},{10,11... | collective-permute-start | bytes 24584 | tf_op jit(solution)/shard_map/ppermute | solution.py:620
  (70 other events, 379.9 us)
Sparse Core Ops, SparseCore 0:
  309.3 118.5 all-reduce.12

commit v2 on v1

v2 whole, which is shorter than its diff:
```python
from functools import partial

import jax
import jax.numpy as jnp
import numpy as np
from jax import lax
from jax.experimental import pallas as pl
from jax.experimental.pallas import tpu as pltpu
from jax.sharding import PartitionSpec as P

EPS = 1e-05
Q = 128
STATES = 128
TILE = 512
SMALL = 256
RIM = 16
NEVER = -1e30
TINY = 1e-37
BF = jnp.bfloat16
F32 = jnp.float32
VMEM_BYTES = 48 * 2**20
SCALE = 1.0
GAIN, TAPS, SHIFT, GATE, SKIP, RATE, BIAS, TABLE = 0, 1, 5, 6, 7, 8, 9, 16


def dot(a, b):
    return jnp.dot(a, b, preferred_element_type=F32)


def dot_nt(a, b):
    return lax.dot_general(a, b, (((1,), (1,)), ((), ())), preferred_element_type=F32)


def dot_tn(a, b):
    return lax.dot_general(a, b, (((0,), (0,)), ((), ())), preferred_element_type=F32)


def halves(value):
    high = value.astype(BF)
    return high, (value - high.astype(F32)).astype(BF)


def twice(value, axis):
    return jnp.concatenate([value, value], axis=axis)


def stacked(value, axis):
    return jnp.concatenate(halves(value), axis=axis)


def cut_rows(value, likes):
    pieces, at = [], 0
    for like in likes:
        pieces.append(value[at : at + like.shape[0]])
        at += like.shape[0]
    return pieces


def spread_heads(values, spread):
    both = stacked(jnp.concatenate(values, axis=0), 1)
    return cut_rows(dot(both, spread), values)


def gather_heads(values, gather):
    both = stacked(jnp.concatenate(values, axis=0), 1)
    return cut_rows(dot(both, gather), values)


def add_up(values, wedge):
    result = dot(wedge, jnp.concatenate([stacked(value, 0) for value in values], axis=1))
    return [result[:, 128 * c : 128 * c + 128] for c in range(len(values))]


def near_f32(left, right):
    rows, columns = left.shape[0], right.shape[0]
    product = dot_nt(stacked(left, 0), stacked(right, 0))
    return product[:rows, :columns] + product[:rows, columns:] + product[rows:, :columns]


def sigmoid(value):
    return jax.nn.sigmoid(value)


def softplus(value):
    return jnp.maximum(value, 0.0) + jnp.log1p(jnp.exp(-jnp.abs(value)))


def iota(shape, axis):
    return lax.broadcasted_iota(jnp.int32, shape, axis)


class Docs:
    def __init__(self, meta, m):
        self.count = meta.shape[1] - 1
        self.starts = [meta[m, j] for j in range(self.count)]
        self.anchor = meta[m, self.count]

    def counts(self, places):
        total = (places >= self.starts[0]).astype(jnp.int32)
        for start in self.starts[1:]:
            total = total + (places >= start).astype(jnp.int32)
        return total

    def starts_at(self, places):
        hit = places == self.starts[0]
        for start in self.starts[1:]:
            hit = hit | (places == start)
        return hit

    def tap_masks(self, first, rows):
        places = first + iota((rows, 128), 0)
        masks = []
        broken = None
        for back in range(3):
            hit = self.starts_at(places - back)
            broken = hit if broken is None else broken | hit
            masks.append(jnp.where(broken, 0.0, 1.0))
        return masks


class Tile:
    def __init__(self, docs, first, deltas, rate, wedge):
        count = deltas.shape[0] // Q
        self.docs, self.first = docs, first
        self.parts = [slice(Q * c, Q * c + Q) for c in range(count)]
        self.deltas = [deltas[rows] for rows in self.parts]
        runs = add_up([part * rate for part in self.deltas], wedge)
        self.run = runs
        self.total = [run[Q - 1 : Q] for run in runs]
        self.before = [docs.counts(first + Q * c - 1) for c in range(count)]
        self.last = [docs.counts(first + Q * c + Q - 1) for c in range(count)]
        self.column = [docs.counts(first + Q * c + iota((Q, 128), 0)) for c in range(count)]

    def same(self, c):
        return self.column[c] == self.docs.counts(self.first + Q * c + iota((8, 128), 1))[0:1]

    def entry(self, c):
        return jnp.exp(self.run[c] + jnp.where(self.column[c] == self.before[c], 0.0, NEVER))

    def leaving(self, c):
        bias = jnp.where(self.column[c] == self.last[c], 0.0, NEVER)
        return jnp.exp(self.total[c] - self.run[c] + bias) * self.deltas[c]

    def overall(self, c):
        return jnp.exp(self.total[c] + jnp.where(self.last[c] == self.before[c], 0.0, NEVER))


def wide_row(row):
    return jnp.broadcast_to(row, (8, row.shape[1]))


def pair_blocks(value, pair, lanes):
    both = value[:, 128 * pair : 128 * pair + 128]
    zero = jnp.zeros_like(both)
    return jnp.concatenate([jnp.where(lanes, both, zero), jnp.where(lanes, zero, both)], axis=0)


def first_kernel(
    tile, channels,
    meta, rim, tokens, weights, table, spread, wedge, *rest, m,
):
    normed_o, gate_o, xbc_o, pre_o, conv_o, deltas_o, held_o, sums_o, leaving_o, edge_o, ext, state, total = rest[-13:]
    step = pl.program_id(0)
    docs = Docs(meta, m)
    width = xbc_o.shape[1]
    taps = table[TAPS : TAPS + 4, :width]
    shift = table[SHIFT : SHIFT + 1, :width]
    gain = table[GAIN : GAIN + 1, : tokens.shape[1]]
    rate = table[RATE : RATE + 1, :128]
    dt_bias = table[BIAS : BIAS + 1, :128]

    def normalize(rows):
        x = rows.astype(F32)
        scale = lax.rsqrt(jnp.mean(x * x, axis=1, keepdims=True) + EPS)
        return (x * scale * gain).astype(BF)

    @pl.when(step == 0)
    def _():
        edge = dot(normalize(rim[...]), weights[:, channels : channels + width]).astype(BF)
        edge_o[...] = edge
        ext[0:8, :] = edge.astype(F32)[RIM - 8 :]
        state[...] = jnp.zeros_like(state)
        total[...] = jnp.zeros_like(total)

    @pl.when(step > 0)
    def _():
        ext[0:8, :] = ext[tile : tile + 8, :]

    normed = normalize(tokens[...])
    normed_o[...] = normed
    gate_o[...] = dot(normed, weights[:, :channels])
    xbc = dot(normed, weights[:, channels : channels + width]).astype(BF)
    xbc_o[...] = xbc
    ext[8:, :] = xbc.astype(F32)
    deltas = softplus(dot(normed, weights[:, channels + width + 256 :]) + dt_bias)
    deltas_o[...] = deltas
    first = docs.anchor + step * tile
    masks = docs.tap_masks(first, tile)
    for slab in range(width // 128):
        lanes = slice(128 * slab, 128 * slab + 128)
        pre = shift[:, lanes] + taps[3:4, lanes] * ext[8 : 8 + tile, lanes]
        for back in range(1, 4):
            pre = pre + taps[3 - back : 4 - back, lanes] * ext[8 - back : 8 - back + tile, lanes] * masks[back - 1]
        pre_o[:, lanes] = pre.astype(BF)
        conv_o[:, lanes] = (pre * sigmoid(pre)).astype(BF)
    parts = Tile(docs, first, deltas, rate, wedge[...])
    count = len(parts.parts)
    wide = spread_heads(
        [parts.leaving(c) for c in range(count)] + [wide_row(parts.overall(c)) for c in range(count)], spread[...]
    )
    for c, rows in enumerate(parts.parts):
        held_o[c] = state[...]
        sums_o[c] = total[...]
        total[...] = total[...] + parts.total[c]
        writes = conv_o[rows, channels : channels + 128]
        scaled = conv_o[rows, :channels].astype(F32) * wide[c]
        state[...] = state[...] * wide[count + c][0:1] + dot_tn(twice(writes, 0), stacked(scaled, 0))

    @pl.when(step == pl.num_programs(0) - 1)
    def _():
        end = docs.anchor + (step + 1) * tile - 1
        through = jnp.where(docs.counts(end) == docs.counts(docs.anchor - 1), 0.0, NEVER)
        leaving_o[...] = packed(state[...], spread_heads([jnp.exp(total[...] + through)], spread[...])[0][0:1])


def inside_kernel(
    tile, channels,
    meta, conv, deltas, table, wedge, *rest, m, sources,
):
    mixed_o, near_o, send_o = rest[-3:]
    step = pl.program_id(0)

    @pl.when(step == 0)
    def _():
        state, decay = joined([part[...] for part in rest[:sources]])
        near_o[:STATES, :] = state
        near_o[STATES:, :] = jnp.broadcast_to(decay, (8, channels))
        send_o[...] = packed(state, decay)

    docs = Docs(meta, m)
    first = docs.anchor + step * tile
    lanes_q = iota((Q, 128), 1)
    causal = iota((Q, Q), 0) >= iota((Q, Q), 1)
    low = lanes_q < 64
    skip = table[SKIP : SKIP + 1, :channels]
    rate = table[RATE : RATE + 1, :128]
    parts = Tile(docs, first, deltas[...], rate, wedge[...])
    for c, rows in enumerate(parts.parts):
        u = conv[rows, :channels]
        writes = conv[rows, channels : channels + 128]
        reads = conv[rows, channels + 128 :]
        scores = dot_nt(reads, writes)
        run = parts.run[c]
        bias = jnp.where(parts.same(c) & causal, 0.0, NEVER)
        behind = jnp.transpose(jnp.log(jnp.maximum(parts.deltas[c], TINY)) - run)
        pieces = []
        for pair in range(channels // 128):
            both = []
            for head in (2 * pair, 2 * pair + 1):
                decay = jnp.exp(run[:, head : head + 1] + behind[head : head + 1] + bias)
                both.append((decay * scores).astype(BF))
            pieces.append(dot(jnp.concatenate(both, axis=1), pair_blocks(u, pair, low)))
        mixed_o[rows, :] = jnp.concatenate(pieces, axis=1) + skip * u.astype(F32)


def mix_kernel(
    tile, channels,
    meta, inside, conv, deltas, gate, held, sums, cotangent, out_weight, table, spread, wedge, *rest, m, sources,
):
    mixed_o, stats_o, carry = rest[-3:]
    step = pl.program_id(0)

    @pl.when(step == 0)
    def _():
        carry[...] = joined([part[...] for part in rest[:sources]])[0]

    back = dot_nt(cotangent[...], out_weight[...]) * table[GATE : GATE + 1, :channels]
    docs = Docs(meta, m)
    first = docs.anchor + step * tile
    lanes_q = iota((Q, 128), 1)
    rate = table[RATE : RATE + 1, :128]
    parts = Tile(docs, first, deltas[...], rate, wedge[...])
    count = len(parts.parts)
    start = docs.counts(docs.anchor - 1)
    arrived = [jnp.exp(sums[c] + jnp.where(parts.before[c] == start, 0.0, NEVER)) for c in range(count)]
    wide = spread_heads([parts.entry(c) for c in range(count)] + arrived, spread[...])
    for c, rows in enumerate(parts.parts):
        reads = conv[rows, channels + 128 :]
        state = stacked(held[c] + wide[count + c][0:1] * carry[...], 0)
        mixed = inside[rows, :] + dot(twice(reads, 1), state) * wide[c]
        mixed_o[rows, :] = mixed
        gate_rows = gate[rows, :]
        gated = mixed * gate_rows * sigmoid(gate_rows)
        squares = jnp.sum(gated * gated, axis=1, keepdims=True)
        inner = jnp.sum(gated * back[rows], axis=1, keepdims=True)
        columns = jnp.where(lanes_q == 0, squares, jnp.where(lanes_q == 1, inner, 0.0))
        stats_o[:, rows] = jnp.transpose(columns)[0:8]


def third_kernel(
    tile, channels, full, chained,
    meta, mixed, gate, conv, deltas, normed, cotangent, out_weight, table, spread, wedge,
    stats_a, stats_b, stats_c, stats_d, *rest, m,
):
    if chained:
        grad_out_i, grad_gate_i, rows_i, *rest = rest
    branch_o, gate_back_o, ssd_back_o, held_o, sums_o, leaving_o, grad_out, grad_gate, rows_o, state, total = rest[-11:]
    step = pl.program_id(0)
    gate_gain = table[GATE : GATE + 1, :channels]
    rate = table[RATE : RATE + 1, :128]
    docs = Docs(meta, m)
    place = pl.num_programs(0) - 1 - step
    first = docs.anchor + place * tile

    @pl.when(step == 0)
    def _():
        state[...] = jnp.zeros_like(state)
        total[...] = jnp.zeros_like(total)
        if chained:
            grad_out[...] = grad_out_i[...]
            grad_gate[...] = grad_gate_i[...]
            rows_o[...] = rows_i[...]
        else:
            grad_out[...] = jnp.zeros_like(grad_out)
            grad_gate[...] = jnp.zeros_like(grad_gate)
            rows_o[...] = jnp.zeros_like(rows_o)

    stats = stats_a[...] + stats_b[...] + stats_c[...] + stats_d[...]
    branches = []
    back = dot_nt(cotangent[...], out_weight[...])
    parts = Tile(docs, first, deltas[...], rate, wedge[...])
    count = len(parts.parts)
    wide = spread_heads(
        [parts.entry(c) for c in range(count)] + [wide_row(parts.overall(c)) for c in range(count)], spread[...]
    )
    for c in reversed(range(count)):
        rows = parts.parts[c]
        sides = jnp.transpose(jnp.concatenate([stats[:, rows], jnp.zeros((120, Q), F32)], axis=0))
        scale = lax.rsqrt(sides[:, 0:1] / full + EPS)
        inner = sides[:, 1:2]
        mixed_rows = mixed[rows, :]
        gate_rows = gate[rows, :]
        sigma = sigmoid(gate_rows)
        act = gate_rows * sigma
        gated = mixed_rows * act
        unit = gated * scale
        branch = (unit * gate_gain).astype(BF)
        branches.append(branch)
        back_rows = back[rows]
        grad_gated = scale * (back_rows * gate_gain) - unit * (scale * scale * (inner / full))
        grad_mixed = grad_gated * act
        gate_back_o[rows, :] = (grad_gated * mixed_rows * (sigma * (1.0 + gate_rows * (1.0 - sigma)))).astype(BF)
        ssd_back = grad_mixed.astype(BF)
        ssd_back_o[rows, :] = ssd_back
        u = conv[rows, :channels].astype(F32)
        rows_o[0:8, :] += jnp.sum((back_rows * unit).reshape(Q // 8, 8, channels), axis=0)
        rows_o[8:16, :] += jnp.sum((grad_mixed * u).reshape(Q // 8, 8, channels), axis=0)
        held_o[c] = state[...]
        sums_o[c] = total[...]
        total[...] = total[...] + parts.total[c]
        reads = conv[rows, channels + 128 :]
        entered = stacked(ssd_back.astype(F32) * wide[c], 0)
        state[...] = state[...] * wide[count + c][0:1] + dot_tn(twice(reads, 0), entered)
    branch = jnp.concatenate(branches[::-1], axis=0)
    branch_o[...] = dot(branch, out_weight[...]).astype(BF)
    grad_out[...] += dot_tn(branch, cotangent[...])
    grad_gate[...] += dot_tn(normed[...], gate_back_o[...])

    @pl.when(step == pl.num_programs(0) - 1)
    def _():
        end = docs.anchor + pl.num_programs(0) * tile - 1
        through = jnp.where(docs.counts(end) == docs.counts(docs.anchor - 1), 0.0, NEVER)
        leaving_o[...] = packed(state[...], spread_heads([jnp.exp(total[...] + through)], spread[...])[0][0:1])


def within_kernel(
    tile, channels,
    meta, conv, deltas, ssd_back, table, wedge, *rest, m, sources,
):
    grads_o, ends_o, near_o, send_o = rest[-4:]
    step = pl.program_id(0)

    @pl.when(step == 0)
    def _():
        state, decay = joined([part[...] for part in rest[:sources]])
        near_o[:STATES, :] = state
        near_o[STATES:, :] = jnp.broadcast_to(decay, (8, channels))
        send_o[...] = packed(state, decay)

    docs = Docs(meta, m)
    first = docs.anchor + step * tile
    lanes_q = iota((Q, 128), 1)
    rows_16 = iota((16, 128), 0)
    causal = iota((Q, Q), 1) >= iota((Q, Q), 0)
    low = lanes_q < 64
    skip = table[SKIP : SKIP + 1, :channels]
    rate = table[RATE : RATE + 1, :128]
    parts = Tile(docs, first, deltas[...], rate, wedge[...])
    for c, rows in enumerate(parts.parts):
        u = conv[rows, :channels]
        writes = conv[rows, channels : channels + 128]
        reads = conv[rows, channels + 128 :]
        grad = ssd_back[rows, :]
        scores = dot_nt(writes, reads)
        bias = jnp.where(parts.same(c) & causal, 0.0, NEVER)
        ahead = jnp.transpose(parts.run[c])
        behind = jnp.log(jnp.maximum(parts.deltas[c], TINY)) - parts.run[c]
        grad_scores = jnp.zeros((Q, Q), F32)
        by_source = jnp.zeros((Q, 128), F32)
        by_target = jnp.zeros((16, 128), F32)
        pieces = []
        for pair in range(channels // 128):
            blocks = pair_blocks(grad, pair, low)
            meets = dot_nt(u[:, 128 * pair : 128 * pair + 128], blocks)
            both = []
            for side in range(2):
                head = 2 * pair + side
                decay = jnp.exp(behind[:, head : head + 1] + ahead[head : head + 1] + bias)
                both.append((decay * scores).astype(BF))
                weighed = decay * meets[:, Q * side : Q * side + Q]
                grad_scores = grad_scores + weighed
                pairs = weighed * scores
                by_source = jnp.where(lanes_q == head, jnp.sum(pairs, axis=1, keepdims=True), by_source)
                by_target = jnp.where(rows_16 == head + 8, jnp.sum(pairs, axis=0, keepdims=True), by_target)
            pieces.append(dot(jnp.concatenate(both, axis=1), blocks))
        ends_o[rows, :] = by_source + jnp.transpose(jnp.concatenate([by_target, jnp.zeros((112, Q), F32)], axis=0))
        high, low_part = halves(grad_scores)
        grads_o[rows, :channels] = jnp.concatenate(pieces, axis=1) + skip * grad.astype(F32)
        grads_o[rows, channels : channels + 128] = dot(jnp.concatenate([high, low_part], axis=1), twice(reads, 0))
        grads_o[rows, channels + 128 :] = dot_tn(jnp.concatenate([high, low_part], axis=0), twice(writes, 0))


def across_kernel(
    tile, channels, chained,
    meta, conv, pre, xbc, edge, deltas, ssd_back, inside, ends,
    held, sums, carry, held_b, sums_b,
    table, spread, gather, wedge, wedge_up, wedge_below, *rest, m, sources,
):
    far, rest = rest[:sources], rest[sources:]
    if chained:
        taps_i, heads_i, *rest = rest
    in_back_o, dt_back_o, rim_o, tail_o, taps_o, heads_o, ext, grads, carry_b = rest[-9:]
    step = pl.program_id(0)
    docs = Docs(meta, m)
    places = pl.num_programs(0)
    place = places - 1 - step
    first = docs.anchor + place * tile
    end = docs.anchor + places * tile - 1
    width = pre.shape[1]
    taps = table[TAPS : TAPS + 4, :width]
    rate = table[RATE : RATE + 1, :128]
    lanes_q = iota((Q, 128), 1)

    @pl.when(step == 0)
    def _():
        if chained:
            taps_o[...] = taps_i[...]
            heads_o[...] = heads_i[...]
        else:
            taps_o[...] = jnp.zeros_like(taps_o)
            heads_o[...] = jnp.zeros_like(heads_o)
        carry_b[...] = joined([part[...] for part in far])[0]
        ext[:, 0:16, :] = jnp.zeros_like(ext[:, 0:16, :])
        ext[:, 16 + tile :, :] = jnp.zeros_like(ext[:, 16 + tile :, :])

    @pl.when(step > 0)
    def _():
        ext[:, 16 + tile :, :] = ext[:, 16:24, :]

    parts = Tile(docs, first, deltas[...], rate, wedge[...])
    count = len(parts.parts)
    start, stop = docs.counts(docs.anchor - 1), docs.counts(end)
    each = range(count)
    arrived = [jnp.exp(sums[c] + jnp.where(parts.before[c] == start, 0.0, NEVER)) for c in each]
    arrived_b = [jnp.exp(sums_b[c] + jnp.where(parts.last[c] == stop, 0.0, NEVER)) for c in each]
    wide = spread_heads(
        [parts.entry(c) for c in each] + [parts.leaving(c) for c in each] + arrived + arrived_b, spread[...]
    )
    crossings, products = [], []
    for c, rows in enumerate(parts.parts):
        u = conv[rows, :channels].astype(F32)
        writes = conv[rows, channels : channels + 128]
        reads = conv[rows, channels + 128 :]
        outward = wide[count + c]
        state = held[c] + wide[2 * count + c][0:1] * carry[...]
        state_b = held_b[c] + wide[3 * count + c][0:1] * carry_b[...]
        grad_in = ssd_back[rows, :].astype(F32) * wide[c]
        crossing = dot(twice(writes, 1), stacked(state_b, 0)) * outward
        products.append(u * crossing)
        crossings.append(grad_in * dot(twice(reads, 1), stacked(state, 0)))
        products.append(jnp.sum((state * state_b).reshape(16, 8, channels), axis=0))
        grads[rows, :channels] = inside[rows, :channels] + crossing
        grads[rows, channels : channels + 128] = inside[rows, channels : channels + 128] + near_f32(u * outward, state_b)
        grads[rows, channels + 128 :] = inside[rows, channels + 128 :] + near_f32(grad_in, state)
    gathered = gather_heads(crossings + products, gather[...])
    in_parts, out_parts = gathered[:count], gathered[count : count + 2 * count : 2]
    ups, sources = [], []
    for c, rows in enumerate(parts.parts):
        both_ends = ends[rows, :]
        sources.append(jnp.where(lanes_q < 8, both_ends, 0.0))
        target = jnp.where(lanes_q < 8, pltpu.roll(both_ends, 120, 1), 0.0)
        ups.append(in_parts[c] + target - sources[c])
    ups = add_up(ups, wedge_up[...])
    belows = add_up(out_parts, wedge_below[...])
    for c, rows in enumerate(parts.parts):
        between = jnp.sum(gathered[count + 2 * c + 1], axis=0, keepdims=True) * parts.overall(c)
        grad_run = between + ups[c] + belows[c]
        part_deltas = parts.deltas[c]
        slope = 1.0 - jnp.exp(-part_deltas)
        ratio = jnp.where(part_deltas > 1e-6, slope / jnp.maximum(part_deltas, 1e-6), 1.0)
        dt_back = (sources[c] + out_parts[c]) * ratio + rate * grad_run * slope
        dt_back_o[rows, :] = dt_back.astype(BF)
        heads_o[0:8, :] += jnp.sum(dt_back.reshape(Q // 8, 8, 128), axis=0)
        heads_o[8:16, :] += jnp.sum((grad_run * part_deltas).reshape(Q // 8, 8, 128), axis=0)

    masks = docs.tap_masks(first, tile)
    for slab in range(width // 128):
        lanes = slice(128 * slab, 128 * slab + 128)
        pre_rows = pre[:, lanes].astype(F32)
        sigma = sigmoid(pre_rows)
        grad_pre = grads[:, lanes] * (sigma * (1.0 + pre_rows * (1.0 - sigma)))
        source = xbc[:, lanes].astype(F32)
        result = taps[3:4, lanes] * grad_pre
        taps_o[24:32, lanes] += jnp.sum((grad_pre * source).reshape(tile // 8, 8, 128), axis=0)
        taps_o[32:40, lanes] += jnp.sum(grad_pre.reshape(tile // 8, 8, 128), axis=0)
        for back in range(1, 4):
            ext[back - 1, 16 : 16 + tile, lanes] = grad_pre * masks[back - 1]
            moved = ext[back - 1, 16 + back : 16 + back + tile, lanes]
            result = result + taps[3 - back : 4 - back, lanes] * moved
            taps_o[8 * (3 - back) : 8 * (4 - back), lanes] += jnp.sum((moved * source).reshape(tile // 8, 8, 128), axis=0)
        high = result.astype(BF)
        in_back_o[:, lanes] = high
        if 128 * slab >= channels:
            in_back_o[:, slice(256 + 128 * slab, 384 + 128 * slab)] = (result - high.astype(F32)).astype(BF)

        @pl.when(step == 0)
        def _():
            tail_o[:, lanes] = result[tile - RIM :]

    @pl.when(place == 0)
    def _():
        total = jnp.zeros((RIM, width), F32)
        source = edge[...].astype(F32)
        for back in range(1, 4):
            moved = ext[back - 1, back : back + RIM, :]
            total = total + taps[3 - back : 4 - back, :] * moved
            taps_o[8 * (3 - back) : 8 * (4 - back), :] += jnp.sum((moved * source).reshape(RIM // 8, 8, width), axis=0)
        rim_o[...] = total


def part_kernel(
    tile, channels, chained, last, tiles,
    tokens, gate_back, in_back, dt_back, weights, *rest,
):
    if last:
        tail, rim, *rest = rest
    if chained:
        rows_i, *rest = rest
    part_o, rows_o, every = rest[-3:]
    step = pl.program_id(0)
    wide = in_back.shape[1]
    width = wide - 256

    @pl.when(step == 0)
    def _():
        rows_o[...] = rows_i[...] if chained else jnp.zeros_like(rows_o)

    every[:, :channels] = gate_back[...]
    every[:, channels : channels + wide] = in_back[...]
    every[:, channels + wide :] = dt_back[...]
    if last:

        @pl.when(step == tiles - 1)
        def _():
            high, low = halves(tail[...] + rim[...])
            every[tile - RIM :, channels : channels + width] = high
            every[tile - RIM :, channels + width : channels + wide] = low[:, channels:]

    x = tokens[...].astype(F32)
    scale = lax.rsqrt(jnp.mean(x * x, axis=1, keepdims=True) + EPS)
    part = dot_nt(every[...], weights[...])
    part_o[...] = part.astype(BF)
    rows_o[...] += jnp.sum((part * (x * scale)).reshape(tile // 8, 8, x.shape[1]), axis=0)


def weight_kernel(
    tile, channels, chained, tiles,
    normed, in_back, dt_back, tail, rim, *rest,
):
    if chained:
        grads_i, dt_i, *rest = rest
    grads_o, dt_o, every, total, dt_total = rest[-5:]
    step = pl.program_id(0)
    wide = in_back.shape[1]
    width = wide - 256

    @pl.when(step == 0)
    def _():
        total[...] = grads_i[...] if chained else jnp.zeros_like(total)
        dt_total[...] = jnp.zeros_like(dt_total)

    every[...] = in_back[...]

    @pl.when(step == tiles - 1)
    def _():
        high, low = halves(tail[...] + rim[...])
        every[tile - RIM :, :width] = high
        every[tile - RIM :, width:] = low[:, channels:]

    turned = jnp.transpose(normed[...])
    total[:, :channels] += dot(turned, every[:, :channels])
    total[:, channels:] += dot(
        twice(turned, 1), jnp.concatenate([every[:, channels:width], every[:, width:]], axis=0)
    )
    dt_total[...] += dot_nt(jnp.transpose(dt_back[...]), turned)

    @pl.when(step == tiles - 1)
    def _():
        grads_o[...] = total[...].astype(grads_o.dtype)
        dt_o[...] = dt_total[0:8] + dt_i[...] if chained else dt_total[0:8]


def place_kernel(
    token,
    side, mine, other, tokens, *rest,
):
    if token:
        cotangent, table, *rest = rest
    out = rest[-1]
    step = pl.program_id(0)

    def finish(total):
        x = tokens[...].astype(F32)
        total = total.astype(F32)
        if not token:
            return (x + total).astype(BF)
        scale = lax.rsqrt(jnp.mean(x * x, axis=1, keepdims=True) + EPS)
        grad_hat = total * table[GAIN : GAIN + 1, :]
        inner = jnp.mean(grad_hat * x, axis=1, keepdims=True)
        return (cotangent[...].astype(F32) + scale * grad_hat - x * (scale * scale * scale * inner)).astype(BF)

    here = step // (pl.num_programs(0) // 2) == side[0]

    @pl.when(here)
    def _():
        out[...] = finish(mine[...])

    @pl.when(jnp.logical_not(here))
    def _():
        out[...] = finish(other[...])


class Call:
    def __init__(self, kernel, steps, name):
        self.kernel, self.steps, self.name = kernel, steps, name
        self.args, self.in_specs, self.outs, self.out_specs, self.scratch = [], [], [], [], []
        self.aliases = {}

    def whole(self, *arrays):
        for array in arrays:
            self.args.append(array)
            self.in_specs.append(pl.BlockSpec(array.shape, lambda i, rank=array.ndim: (0,) * rank))
        return self

    def scalars(self, array):
        self.args.append(array)
        self.in_specs.append(pl.BlockSpec(memory_space=pltpu.SMEM))
        return self

    def blocks(self, *arrays_specs):
        for array, spec in arrays_specs:
            self.args.append(array)
            self.in_specs.append(spec)
        return self

    def out(self, shape, dtype, spec=None):
        self.outs.append(jax.ShapeDtypeStruct(shape, dtype))
        self.out_specs.append(spec or pl.BlockSpec(shape, lambda i, rank=len(shape): (0,) * rank))
        return self

    def after(self, *arrays):
        for array in arrays:
            self.args.append(array)
            self.in_specs.append(pl.BlockSpec(memory_space=pl.ANY))
        return self

    def alias(self, array):
        self.aliases = {len(self.args): 0}
        return self.after(array)

    def temp(self, shape, dtype):
        self.scratch.append(pltpu.VMEM(shape, dtype))
        return self

    def run(self, micros, scalars=None):
        ahead = () if scalars is None else (scalars,)
        return pl.pallas_call(
            self.kernel,
            grid_spec=pltpu.PrefetchScalarGridSpec(
                num_scalar_prefetch=len(ahead),
                grid=(self.steps,),
                in_specs=self.in_specs,
                out_specs=tuple(self.out_specs),
                scratch_shapes=self.scratch,
            ),
            out_shape=tuple(self.outs),
            input_output_aliases={at + len(ahead): to for at, to in self.aliases.items()},
            compiler_params=pltpu.CompilerParams(
                dimension_semantics=("arbitrary",), vmem_limit_bytes=VMEM_BYTES
            ),
            cost_estimate=pl.CostEstimate(flops=int(micros * SCALE * 1.15e9), bytes_accessed=0, transcendentals=0),
            name=self.name,
        )(*ahead, *self.args)


def swap(value, axis, bits):
    count = lax.axis_size(axis)
    return lax.ppermute(value, axis, [(i, i ^ bits) for i in range(count)])


def from_behind(value, axis, steps):
    count = lax.axis_size(axis)
    sources = range(max(0, -steps), min(count, count - steps))
    return lax.ppermute(value, axis, [(i, i + steps) for i in sources])


def packed(state, decay):
    high, low = halves(jnp.broadcast_to(decay, (8, decay.shape[1])))
    return jnp.concatenate([state.astype(BF), high, low], axis=0)


def unpacked(part):
    if part.dtype == F32:
        return part[:STATES], part[STATES : STATES + 1]
    part = part.astype(F32)
    return part[:STATES], part[STATES : STATES + 1] + part[STATES + 8 : STATES + 9]


def joined(parts):
    state, decay = unpacked(parts[0])
    for part in parts[1:]:
        more, keep = unpacked(part)
        state = state + decay * more
        decay = decay * keep
    return state, decay


def near_parts(leaving, axis, sign):
    return [from_behind(leaving, axis, sign * k) for k in range(1, min(4, lax.axis_size(axis)))]


def far_parts(carry, sent, axis, sign):
    count = lax.axis_size(axis)
    window = 3
    parts = [carry]
    while window < count - 1:
        if len(parts) > 1:
            state, decay = joined(parts)
            sent = packed(state, decay)
            carry = jnp.concatenate([state, jnp.broadcast_to(decay, (8, decay.shape[1]))], axis=0)
        parts = [carry] + [from_behind(sent, axis, sign * k) for k in (window, 2 * window) if k < count]
        window *= 3
    return parts


def sum_rows(parts):
    total = parts[0].astype(F32)
    for part in parts[1:]:
        total = total + part.astype(F32)
    return total


def head_pair(part):
    rows = part.shape[0] // 2
    side = lax.axis_index("head") % 2
    mine = lax.dynamic_slice_in_dim(part, side * rows, rows, 0)
    other = lax.dynamic_slice_in_dim(part, (1 - side) * rows, rows, 0)
    return (mine.astype(F32) + swap(other, "head", 1).astype(F32)).astype(BF)


def head_rest(low):
    total = low.astype(F32)
    bit = 2
    while bit < lax.axis_size("head"):
        low = total.astype(BF)
        total = low.astype(F32) + swap(low, "head", bit).astype(F32)
        bit *= 2
    return total


def pair_parts(value, axis):
    rows = value.shape[0] // 2
    half = lax.axis_index(axis) % 2
    mine = lax.dynamic_slice_in_dim(value, half * rows, rows, 0)
    return mine, swap(lax.dynamic_slice_in_dim(value, (1 - half) * rows, rows, 0), axis, 1)


def scatter_parts(value, axis):
    count = lax.axis_size(axis) // 2
    me = lax.axis_index(axis) // 2
    rows = value.shape[0] // count
    parts = [lax.dynamic_slice_in_dim(value, me * rows, rows, 0)]
    for bits in range(1, count):
        piece = lax.dynamic_slice_in_dim(value, jnp.bitwise_xor(me, bits) * rows, rows, 0)
        parts.append(swap(piece, axis, 2 * bits))
    return parts


def gather_half(value, axis):
    count = lax.axis_size(axis) // 2
    me = lax.axis_index(axis) // 2
    rows = value.shape[0]
    result = jnp.zeros((count * rows, value.shape[1]), value.dtype)
    result = lax.dynamic_update_slice_in_dim(result, value, me * rows, 0)
    for bits in range(1, count):
        result = lax.dynamic_update_slice_in_dim(
            result, swap(value, axis, 2 * bits), jnp.bitwise_xor(me, bits) * rows, 0
        )
    return result


def gather_pair(half, axis):
    other = swap(half, axis, 1)
    first = lax.axis_index(axis) % 2 == 0
    return jnp.concatenate([jnp.where(first, half, other), jnp.where(first, other, half)], axis=0)


def all_sum(value, axis):
    bit = 1
    while bit < lax.axis_size(axis):
        value = value + swap(value, axis, bit)
        bit *= 2
    return value


def local(
    tokens,
    doc_starts,
    norm_gain,
    gate_x_weight,
    bc_weight,
    dt_weight,
    conv_x_weight,
    conv_x_bias,
    conv_bc_weight,
    conv_bc_bias,
    dt_bias,
    a_log,
    d_skip,
    gate_gain,
    out_weight,
    cotangent,
):
    micro, length, model = tokens.shape
    channels = gate_x_weight.shape[2]
    heads = dt_weight.shape[1]
    dim = channels // heads
    states = bc_weight.shape[1] // 2
    width = channels + 2 * states
    full = channels * lax.axis_size("head")
    tile, small = min(TILE, length), min(SMALL, length)
    steps = length // tile
    per = tile // Q
    blocks = length // Q

    rim_tokens = from_behind(tokens[:, length - RIM :], "seq", 1)
    weights = jnp.concatenate(
        [gate_x_weight[:, 0], gate_x_weight[:, 1], bc_weight, bc_weight,
         jnp.pad(dt_weight, ((0, 0), (0, 128 - heads)))], axis=1
    )
    decay_rate = -jnp.exp(a_log)

    def table_rows(*parts):
        row = jnp.concatenate(parts, axis=-1)
        row = row if row.ndim == 2 else row[None]
        return jnp.pad(row, ((0, 0), (0, model - row.shape[1])))

    table = jnp.concatenate(
        [
            table_rows(norm_gain),
            table_rows(conv_x_weight, conv_bc_weight),
            table_rows(conv_x_bias, conv_bc_bias),
            table_rows(gate_gain),
            table_rows(jnp.repeat(d_skip, dim)),
            table_rows(decay_rate),
            table_rows(dt_bias, jnp.full((128 - heads,), -200.0, F32)),
            jnp.zeros((TABLE - BIAS - 1, model), F32),
        ],
        axis=0,
    )
    owner = np.arange(channels)[None, :] // dim == np.arange(128)[:, None]
    spread = np.concatenate([owner, owner], axis=0).astype(BF)
    gather = np.concatenate([owner.T, owner.T], axis=0).astype(BF)
    order = np.arange(Q)
    until_here = order[:, None] >= order[None, :]
    below = order[:, None] > order[None, :]
    wedge = np.concatenate([until_here] * 2, axis=1).astype(BF)
    wedge_up = np.concatenate([until_here.T] * 2, axis=1).astype(BF)
    wedge_below = np.concatenate([below] * 2, axis=1).astype(BF)
    anchor = lax.axis_index("seq") * length
    meta = jnp.concatenate(
        [jnp.where(doc_starts >= 1, doc_starts, 2**30), jnp.full((micro, 1), anchor)], axis=1
    ).astype(jnp.int32)

    ahead = lambda i: i
    astern = lambda i: steps - 1 - i

    def rows_of(cols, turn, rows=tile):
        return pl.BlockSpec((rows, cols), lambda i: (turn(i), 0))

    def rows_in(m, cols, turn):
        return pl.BlockSpec((None, tile, cols), lambda i: (m, turn(i), 0))

    def chunks_of(turn, rows, cols):
        return pl.BlockSpec((per, rows, cols), lambda i: (turn(i), 0, 0))

    def stat_spec(turn):
        return pl.BlockSpec((8, tile), lambda i: (0, turn(i)))

    def project(m, *waits):
        call = Call(partial(first_kernel, tile, channels, m=m), steps, f"project_{m}")
        call.scalars(meta)
        call.blocks((rim_tokens, pl.BlockSpec((None, RIM, model), lambda i: (m, 0, 0))))
        call.blocks((tokens, rows_in(m, model, ahead)))
        call.whole(weights, table, spread, wedge).after(*waits)
        call.out((length, model), BF, rows_of(model, ahead))
        call.out((length, channels), F32, rows_of(channels, ahead))
        call.out((length, width), BF, rows_of(width, ahead))
        call.out((length, width), BF, rows_of(width, ahead))
        call.out((length, width), BF, rows_of(width, ahead))
        call.out((length, 128), F32, rows_of(128, ahead))
        call.out((blocks, 128, channels), F32, chunks_of(ahead, 128, channels))
        call.out((blocks, 8, 128), F32, chunks_of(ahead, 8, 128))
        call.out((STATES + 16, channels), BF)
        call.out((RIM, width), BF)
        call.temp((tile + 8, width), F32).temp((128, channels), F32).temp((8, 128), F32)
        return call.run(22)

    def inside(m, kept, parts, *waits):
        conv, deltas = kept[4:6]
        call = Call(partial(inside_kernel, tile, channels, m=m, sources=len(parts)), steps, f"inside_{m}")
        call.scalars(meta)
        call.blocks((conv, rows_of(width, ahead)), (deltas, rows_of(128, ahead)))
        call.whole(table, wedge, *parts).after(*waits)
        call.out((length, channels), F32, rows_of(channels, ahead))
        call.out((STATES + 8, channels), F32).out((STATES + 16, channels), BF)
        return call.run(11)

    def mix(m, kept, inner, parts, *waits):
        normed, gate, xbc, pre, conv, deltas, held, sums = kept[:8]
        call = Call(partial(mix_kernel, tile, channels, m=m, sources=len(parts)), steps, f"mix_{m}")
        call.scalars(meta)
        call.blocks(
            (inner, rows_of(channels, ahead)),
            (conv, rows_of(width, ahead)),
            (deltas, rows_of(128, ahead)),
            (gate, rows_of(channels, ahead)),
            (held, chunks_of(ahead, 128, channels)),
            (sums, chunks_of(ahead, 8, 128)),
            (cotangent, rows_in(m, model, ahead)),
        )
        call.whole(out_weight, table, spread, wedge, *parts).after(*waits)
        call.out((length, channels), F32, rows_of(channels, ahead))
        call.out((8, length), F32, stat_spec(ahead))
        call.out((STATES, channels), F32)
        return call.run(12)

    def norm(m, kept, mixed, stats, chain, *waits):
        normed, gate, xbc, pre, conv, deltas = kept[:6]
        call = Call(partial(third_kernel, tile, channels, float(full), bool(chain), m=m), steps, f"gate_{m}")
        call.scalars(meta)
        call.blocks(
            (mixed, rows_of(channels, astern)),
            (gate, rows_of(channels, astern)),
            (conv, rows_of(width, astern)),
            (deltas, rows_of(128, astern)),
            (normed, rows_of(model, astern)),
            (cotangent, rows_in(m, model, astern)),
        )
        call.whole(out_weight, table, spread, wedge)
        call.blocks(*[(part, stat_spec(astern)) for part in stats])
        call.whole(*chain).after(*waits)
        call.out((length, model), BF, rows_of(model, astern))
        call.out((length, channels), BF, rows_of(channels, astern))
        call.out((length, channels), BF, rows_of(channels, astern))
        call.out((blocks, 128, channels), F32, chunks_of(astern, 128, channels))
        call.out((blocks, 8, 128), F32, chunks_of(astern, 8, 128))
        call.out((STATES + 16, channels), BF)
        call.out((channels, model), F32)
        call.out((model, channels), F32)
        call.out((16, channels), F32)
        call.temp((128, channels), F32).temp((8, 128), F32)
        return call.run(19)

    def within(m, kept, ssd_back, parts, *waits):
        conv, deltas = kept[4:6]
        call = Call(partial(within_kernel, small, channels, m=m, sources=len(parts)), length // small, f"within_{m}")
        call.scalars(meta)
        call.blocks((conv, rows_of(width, ahead, small)), (deltas, rows_of(128, ahead, small)), (ssd_back, rows_of(channels, ahead, small)))
        call.whole(table, wedge, *parts).after(*waits)
        call.out((length, width), F32, rows_of(width, ahead, small))
        call.out((length, 128), F32, rows_of(128, ahead, small))
        call.out((STATES + 8, channels), F32).out((STATES + 16, channels), BF)
        return call.run(14)

    def across(m, kept, carry, third, inner, parts, chain, *waits):
        normed, gate, xbc, pre, conv, deltas, held, sums, leaving, edge = kept
        call = Call(partial(across_kernel, tile, channels, bool(chain), m=m, sources=len(parts)), steps, f"across_{m}")
        call.scalars(meta)
        call.blocks((conv, rows_of(width, astern)), (pre, rows_of(width, astern)), (xbc, rows_of(width, astern)))
        call.whole(edge)
        call.blocks(
            (deltas, rows_of(128, astern)),
            (third[2], rows_of(channels, astern)),
            (inner[0], rows_of(width, astern)),
            (inner[1], rows_of(128, astern)),
            (held, chunks_of(astern, 128, channels)),
            (sums, chunks_of(astern, 8, 128)),
        )
        call.whole(carry)
        call.blocks((third[3], chunks_of(astern, 128, channels)), (third[4], chunks_of(astern, 8, 128)))
        call.whole(table, spread, gather, wedge, wedge_up, wedge_below, *parts, *chain).after(*waits)
        call.out((length, width + 256), BF, rows_of(width + 256, astern))
        call.out((length, 128), BF, rows_of(128, astern))
        call.out((RIM, width), F32)
        call.out((RIM, width), F32)
        call.out((40, width), F32)
        call.out((16, 128), F32)
        call.temp((3, tile + 24, width), F32).temp((tile, width), F32).temp((STATES, channels), F32)
        return call.run(32)

    def part_of(m, gate_back, fourth, span, rows, rim, chain, earlier, micros, *waits):
        count = span[1] - span[0]
        turn = lambda i: i + span[0]
        put = lambda i: i + span[0] - rows[0]
        call = Call(partial(part_kernel, tile, channels, bool(chain), rim is not None, count), count, f"input_{m}_{span[0]}")
        call.blocks(
            (tokens, rows_in(m, model, turn)),
            (gate_back, rows_of(channels, turn)),
            (fourth[0], rows_of(width + 256, turn)),
            (fourth[1], rows_of(128, turn)),
        )
        call.whole(weights)
        if rim is not None:
            call.whole(fourth[3], rim)
        call.whole(*chain)
        if earlier is not None:
            call.alias(earlier)
        call.after(*waits)
        call.out((rows[1] * tile, model), BF, rows_of(model, put))
        call.out((8, model), F32)
        call.temp((tile, channels + width + 256 + 128), BF)
        return call.run(micros)

    def weight_back(m, kept, fourth, rim, chain, kind, *waits):
        call = Call(partial(weight_kernel, tile, channels, bool(chain), steps), steps, f"weigh_{m}")
        call.blocks(
            (kept[0], rows_of(model, ahead)), (fourth[0], rows_of(width + 256, ahead)), (fourth[1], rows_of(128, ahead))
        )
        call.whole(fourth[3], rim, *chain).after(*waits)
        call.out((model, width), kind)
        call.out((8, model), F32)
        call.temp((tile, width + 256), BF).temp((model, width), F32).temp((128, model), F32)
        return call.run(8)

    side = (lax.axis_index("head") % 2).astype(jnp.int32)[None]

    def place(m, begin, totals, token, earlier, *waits):
        low = totals.astype(BF)
        other = swap(low, "head", 1)
        big = min(512, low.shape[0])
        half = low.shape[0] // big
        call = Call(partial(place_kernel, token), 2 * half, f"place_{m}_{begin}_{token:d}")

        def source(flip):
            return pl.BlockSpec(
                (big, model), lambda i, s: (jnp.clip(i - (s[0] if flip == 0 else 1 - s[0]) * half, 0, half - 1), 0)
            )

        spot = pl.BlockSpec((None, big, model), lambda i, s: (m, i + begin // big, 0))
        call.blocks((low, source(0)), (other, source(1)), (tokens, spot))
        if token:
            call.blocks((cotangent, spot))
            call.args.append(table)
            call.in_specs.append(pl.BlockSpec(table.shape, lambda i, s: (0, 0)))
        if earlier is not None:
            call.alias(earlier)
        call.after(*waits)
        call.out((micro, length, model), BF, spot)
        return call.run(4, side)[0]

    every = range(micro)
    kept, inner, mixes, thirds, order_by, chain = [], [], [], [], [], ()
    for m in every:
        kept.append(project(m, *order_by))
        order_by = [kept[m][8]]
    for m in every:
        inner.append(inside(m, kept[m], near_parts(kept[m][8], "seq", 1), *order_by))
        order_by = [inner[m][1]]
    for m in every:
        mixes.append(mix(m, kept[m], inner[m][0], far_parts(inner[m][1], inner[m][2], "seq", 1), *order_by))
        order_by = [mixes[m][1]]
    for m in every:
        stats = [mixes[m][1]] + [swap(mixes[m][1], "head", bits) for bits in range(1, lax.axis_size("head"))]
        thirds.append(norm(m, kept[m], mixes[m][0], stats, chain, *order_by))
        chain = thirds[m][6:9]
        order_by = [thirds[m][5]]
    grad_out, grad_gate, gate_rows = chain
    grad_out, grad_gate = lax.psum((grad_out, grad_gate), "seq")
    mixed_pair = [head_pair(thirds[m][0]) for m in every]
    mixed_all = [head_rest(mixed_pair[m]) for m in every]
    inner_b, fourths, chain = [], [], ()
    for m in every:
        inner_b.append(within(m, kept[m], thirds[m][2], near_parts(thirds[m][5], "seq", -1), *order_by))
        order_by = [inner_b[m][2], mixed_pair[m]]
    far = [far_parts(inner_b[m][2], inner_b[m][3], "seq", -1) for m in every]
    gain_rows, grads, token_all, half_steps = (), (), [], steps // 2
    for m in every:
        final = m + 1 == micro
        fourths.append(across(m, kept[m], mixes[m][2], thirds[m], inner_b[m], far[m], chain, *order_by))
        chain = fourths[m][4:6]
        rim = from_behind(fourths[m][2], "seq", -1)
        gate_back = thirds[m][1]
        if not final:
            both = (0, steps)
            first = part_of(m, gate_back, fourths[m], (0, half_steps), both, None, gain_rows, None, 6, mixed_all[m], *far[m + 1])
            second = part_of(m, gate_back, fourths[m], (half_steps, steps), both, rim, first[1:], first[0], 6)
            grads = weight_back(m, kept[m], fourths[m], rim, grads, F32, second[1])
            pair = head_pair(second[0])
            token_all.append(head_rest(pair))
            gain_rows = second[1:]
            order_by = [pair, grads[1], mixed_all[m + 1]]
        else:
            first = part_of(m, gate_back, fourths[m], (0, half_steps), (0, half_steps), None, gain_rows, None, 6, token_all[-1])
            grads = weight_back(m, kept[m], fourths[m], rim, grads, BF, first[1])
            pair = head_pair(first[0])
            second = part_of(
                m, gate_back, fourths[m], (half_steps, steps), (half_steps, half_steps), rim, first[1:], None, 6,
                pair, grads[1],
            )
            gain_rows = second[1:]
            last_pair = [pair, head_pair(second[0])]
    tap_rows, head_rows = chain
    grads, dt_rows = grads
    gain_rows = gain_rows[0]
    halved = pair_parts(grads, "seq")
    last_all = [head_rest(last_pair[0])]
    halved, last_pair, dt_rows = lax.optimization_barrier((halved, last_pair, dt_rows))
    last_all.append(head_rest(last_pair[1]))
    halved = sum_rows(halved).astype(BF)
    pieces = scatter_parts(halved, "seq")
    mixed_out = token_grad = None
    for m in every:
        mixed_out = place(m, 0, mixed_all[m], False, mixed_out, halved, last_all[0], grad_out, grad_gate)
    pieces, mixed_out = lax.optimization_barrier((pieces, mixed_out))
    part = sum_rows(pieces)
    share = 2 * states // lax.axis_size("head")
    bc_parts = [part[:, channels:width]]
    bc_parts += [swap(bc_parts[0], "head", bits) for bits in range(1, lax.axis_size("head"))]
    for m in range(micro - 1):
        token_grad = place(m, 0, token_all[m], True, token_grad, part, last_all[1])
    bc_parts, token_grad = lax.optimization_barrier((bc_parts, token_grad))
    bc_mine = lax.dynamic_slice_in_dim(sum_rows(bc_parts), lax.axis_index("head") * share, share, 1)
    gathered = gather_half(
        jnp.concatenate(
            [part[:, :channels], bc_mine, jnp.zeros((part.shape[0], -share % 128), F32)], axis=1
        ).astype(BF),
        "seq",
    )
    gathered = gather_pair(gathered, "seq")
    grad_x = gathered[:, :channels].astype(F32)
    grad_bc = gathered[:, channels : channels + share].astype(F32)

    token_grad = place(micro - 1, 0, last_all[0], True, token_grad)
    token_grad = place(micro - 1, length // 2, last_all[1], True, token_grad)

    def folded(rows):
        return jnp.sum(rows.reshape(-1, 8, rows.shape[1]), axis=1)

    by_tap = folded(tap_rows)
    by_row = folded(gate_rows)
    by_head = folded(head_rows)[:, :heads]
    skip_sum = jnp.sum(by_row[1].reshape(heads, dim), axis=1)
    gain_sum = jnp.sum(gain_rows, axis=0)
    small = jnp.concatenate(
        [by_tap[:, channels:].reshape(-1), gain_sum,
         dt_rows[:heads].reshape(-1), by_tap[:, :channels].reshape(-1), by_row[0], by_head.reshape(-1), skip_sum]
    )
    shared_size = by_tap[:, channels:].size + model
    small = jnp.pad(small, (0, -small.size % 1024)).reshape(-1, 128)
    small = all_sum(small, "seq")
    shared_rows = shared_size // 128
    shared = all_sum(small[:shared_rows], "head").reshape(-1)
    rest = small[shared_rows:].reshape(-1)
    tap_count = conv_x_weight.shape[0]
    bc_taps = shared[: (tap_count + 1) * 2 * states].reshape(tap_count + 1, 2 * states)
    grad_norm_gain = shared[(tap_count + 1) * 2 * states : shared_size]
    grad_dt = rest[: heads * model].reshape(heads, model).T
    rest = rest[heads * model :]
    cut = (tap_count + 1) * channels
    x_taps = rest[:cut].reshape(tap_count + 1, channels)
    grad_gate_gain = rest[cut : cut + channels]
    tails = rest[cut + channels : cut + channels + 3 * heads].reshape(3, heads)
    return (
        mixed_out,
        token_grad,
        grad_norm_gain,
        jnp.stack([grad_gate, grad_x], axis=1),
        grad_bc,
        grad_dt,
        x_taps[:tap_count],
        x_taps[tap_count],
        bc_taps[:tap_count],
        bc_taps[tap_count],
        tails[0],
        tails[1] * decay_rate,
        tails[2],
        grad_gate_gain,
        grad_out,
    )


def solution(mesh):
    in_specs = (
        P(None, "seq", None),
        P(),
        P(),
        P(None, None, "head"),
        P(),
        P(None, "head"),
        P(None, "head"),
        P("head"),
        P(),
        P(),
        P("head"),
        P("head"),
        P("head"),
        P("head"),
        P("head", None),
        P(None, "seq", None),
    )
    out_specs = (
        P(None, "seq", None),
        P(None, "seq", None),
        P(),
        P(None, None, "head"),
        P(None, "head"),
        P(None, "head"),
        P(None, "head"),
        P("head"),
        P(),
        P(),
        P("head"),
        P("head"),
        P("head"),
        P("head"),
        P("head", None),
    )
    return jax.shard_map(local, mesh=mesh, in_specs=in_specs, out_specs=out_specs, check_vma=False)
```

time: 569 us -> 477 us (0.84)
  Pallas kernels: 281 us -> 250 us
  starting transfers between devices: 108 us -> 86.4 us
  other arithmetic: 52 us -> 32.6 us
  local copies, waits for them, and re-layouts: 53.9 us -> 34.8 us
    pallas_call x17 -> x23, Pallas kernels: 281 us -> 250 us  [run(): pl.pallas_call(self.kernel, grid_spec=pltpu.PrefetchScalarGridSpec(num_sc...]
    ppermute x43 -> x37, starting transfers between devices: 62.7 us -> 40.6 us  [swap(): return lax.ppermute(value, axis, [(i, i ^ bits) for i in range(count)])]
    dynamic_update_slice x5 -> x1, other arithmetic: 16.3 us -> 0.67 us  [gather_half(): result = lax.dynamic_update_slice_in_dim(result, value, me * rows, 0)]
    convert_element_type x2 -> x6, other arithmetic: 1.47 us -> 14.9 us  [the longest x4 13.7 us: place(): low = totals.astype(BF)]
    dynamic_update_slice x12 -> x3, local copies, waits for them, and re-layouts: 14.4 us -> 1.94 us  [gather_half(): lax.dynamic_update_slice_in_dim(result, swap(value, axis, 2 * bits), jnp....]
    add x4 -> x1, other arithmetic: 12.2 us -> 2.46 us  [head_rest(): total = low.astype(F32) + swap(low, 'head', bit).astype(F32)]
    reduce_sum x2 -> x0, other arithmetic: 6.64 us -> none  [the longest x1 4.57 us: finish_token(): scale = lax.rsqrt(jnp.mean(x * x, axis=1, keepdims=True) + EPS)]
    unnamed x111 -> x138, local copies, waits for them, and re-layouts: 14.6 us -> 15 us
  transfers between devices with their start and end apart: 67 -> 61, of which waited for: 13 -> 7; matrix products, arithmetic and copies ran while one was open for 17% -> 12% of each run, Pallas kernels for 46% -> 48%
where the time goes in v2:
time: 477 us; the launch traced here: 467 us
  Pallas kernels  250 us (52%)
  starting transfers between devices  86.4 us (18%)
  waiting for transfers between devices  48 us (10%)
  local copies, waits for them, and re-layouts  34.8 us (7%)
  other arithmetic  32.6 us (7%)
  between operations  15.9 us (3%)
    pallas_call x23, Pallas kernels, run(): pl.pallas_call(self.kernel, grid_spec=pltpu.PrefetchScalarGridSpec(num_sc...  250 us
    ppermute x37, waiting for transfers between devices, swap(): return lax.ppermute(value, axis, [(i, i ^ bits) for i in range(count)])  47.9 us
    ppermute x23, starting transfers between devices, from_behind(): return lax.ppermute(value, axis, [(i, i + steps) for i in sources])  45.7 us
    ppermute x37, starting transfers between devices, swap(): return lax.ppermute(value, axis, [(i, i ^ bits) for i in range(count)])  40.6 us
    unnamed x138, local copies, waits for them, and re-layouts  15 us
    convert_element_type x4, other arithmetic, place(): low = totals.astype(BF)  13.7 us
    convert_element_type x5, other arithmetic, head_pair(): return (mine.astype(F32) + swap(other, 'head', 1).astype(F32)).astype(BF)  9.99 us
  transfers between devices with their start and end apart: 61, of which 7 were waited for; matrix products, arithmetic and copies ran while one was open for 12% of the time, Pallas kernels for 48%

profile of v2, /device:TPU:0, one launch (start us, length us, event | category | flops | bytes accessed | tf_op | source)
XLA Modules:
  0.0 467.4 jit_solution(10498553364481349079)
XLA Ops:
  8.0 4.9 %collective-permute-start = (bf16[2,16,768]{2,1,0:T(8,128)(2,1)S(1)}, bf16[2,16,768]{2,1,0:T(8,128)(2,1)S(1)}, u32[]{:S(2)}, u32[]{:S(2)}) collective-permute-start(bf16[2,16,768]{2,1,0:T(8,128)(2,1)S(1)} %slice.114), channel_id=1, source_target_pairs={{0,4},{4,8},{8,12},{12,16},{16,20},{20,24},{24,28},{1,5},{5,9},{9,... | collective-permute-start | bytes 147464 | tf_op jit(solution)/shard_map/ppermute | solution.py:724
  13.6 3.7 fusion.14
  19.3 19.5 %project_0.1 = (bf16[2048,768]{1,0:T(8,128)(2,1)}, f32[2048,384]{1,0:T(8,128)}, bf16[2048,640]{1,0:T(8,128)(2,1)}, bf16[2048,640]{1,0:T(8,128)(2,1)}, bf16[2048,...) custom-call(s32[2,9]{1,0:T(2,128)S(1)} %concatenate.28.meta, ...), custom_call_target="tpu_custom_call" | custom-call | flops 25300000768 | tf_op jit(solution)/shard_map/project_0/pallas_call | solution.py:697
  38.8 3.7 collective-permute-start.4
  42.5 3.5 collective-permute-start.5
  46.0 4.4 collective-permute-start.6
  50.4 19.4 %project_1.1 = (bf16[2048,768]{1,0:T(8,128)(2,1)}, f32[2048,384]{1,0:T(8,128)}, bf16[2048,640]{1,0:T(8,128)(2,1)}, bf16[2048,640]{1,0:T(8,128)(2,1)}, bf16[2048,...) custom-call(s32[2,9]{1,0:T(2,128)S(1)} %concatenate.28.meta, ...), custom_call_target="tpu_custom_call" | custom-call | flops 25300000768 | tf_op jit(solution)/shard_map/project_1/pallas_call | solution.py:697
  71.7 2.5 collective-permute-start.2
  75.9 6.1 %inside_0.1 = (f32[2048,384]{1,0:T(8,128)}, f32[136,384]{1,0:T(8,128)S(1)}, bf16[144,384]{1,0:T(8,128)(2,1)S(1)}) custom-call(s32[2,9]{1,0:T(2,128)S(1)} %concatenate.28.meta, bf16[2048,640]{1,0:T(8,128)(2,1)S(1)} %copy-done.25, f32[2048,128]{1,0:T(8,128)S(1)} %get-tuple-element.120.deltas, f32[16,768]{1,0:T(8,128)S(1)} %concatenate.33.table.rest_1_, ...), custom_call_target="tpu_custom_call" | custom-call | flops 12650000384 | tf_op jit(solution)/shard_map/inside_0/pallas_call | solution.py:697
  85.2 6.1 %inside_1.1 = (f32[2048,384]{1,0:T(8,128)}, f32[136,384]{1,0:T(8,128)S(1)}, bf16[144,384]{1,0:T(8,128)(2,1)S(1)}) custom-call(s32[2,9]{1,0:T(2,128)S(1)} %concatenate.28.meta, bf16[2048,640]{1,0:T(8,128)(2,1)S(1)} %copy-done.26, f32[2048,128]{1,0:T(8,128)S(1)} %get-tuple-element.117.deltas, f32[16,768]{1,0:T(8,128)S(1)} %concatenate.33.table.rest_1_, ...), custom_call_target="tpu_custom_call" | custom-call | flops 12650000384 | tf_op jit(solution)/shard_map/inside_1/pallas_call | solution.py:697
  93.9 9.6 %mix_0.1 = (f32[2048,384]{1,0:T(8,128)}, f32[8,2048]{1,0:T(8,128)S(1)}, f32[128,384]{1,0:T(8,128)S(1)}) custom-call(s32[2,9]{1,0:T(2,128)S(1)} %concatenate.28.meta, f32[2048,384]{1,0:T(8,128)} %get-tuple-element.128.inside, bf16[2048,640]{1,0:T(8,128)(2,1)S(1)} %copy-done.25, f32[2048,128]{1,0:T(8,128)S(1)} %get-tuple-element.120.deltas, ...), custom_call_target="tpu_custom_call" | custom-call | flops 13799999488 | tf_op jit(solution)/shard_map/mix_0/pallas_call | solution.py:697
  105.4 9.6 %mix_1.1 = (f32[2048,384]{1,0:T(8,128)}, f32[8,2048]{1,0:T(8,128)S(1)}, f32[128,384]{1,0:T(8,128)S(1)}) custom-call(s32[2,9]{1,0:T(2,128)S(1)} %concatenate.28.meta, f32[2048,384]{1,0:T(8,128)} %get-tuple-element.122.inside, bf16[2048,640]{1,0:T(8,128)(2,1)S(1)} %copy-done.26, f32[2048,128]{1,0:T(8,128)S(1)} %get-tuple-element.117.deltas, ...), custom_call_target="tpu_custom_call" | custom-call | flops 13799999488 | tf_op jit(solution)/shard_map/mix_1/pallas_call | solution.py:697
  116.8 16.3 %gate_0.1 = (bf16[2048,768]{1,0:T(8,128)(2,1)}, bf16[2048,384]{1,0:T(8,128)(2,1)}, bf16[2048,384]{1,0:T(8,128)(2,1)}, f32[16,128,384]{2,1,0:T(8,128)}, f32[16,8,...) custom-call(s32[2,9]{1,0:T(2,128)S(1)} %concatenate.28.meta, ...), custom_call_target="tpu_custom_call" | custom-call | flops 21849999360 | tf_op jit(solution)/shard_map/gate_0/pallas_call | solution.py:697
  138.3 18.2 %gate_1.1 = (bf16[2048,768]{1,0:T(8,128)(2,1)}, bf16[2048,384]{1,0:T(8,128)(2,1)}, bf16[2048,384]{1,0:T(8,128)(2,1)}, f32[16,128,384]{2,1,0:T(8,128)}, f32[16,8,...) custom-call(s32[2,9]{1,0:T(2,128)S(1)} %concatenate.28.meta, ...), custom_call_target="tpu_custom_call" | custom-call | flops 21849999360 | tf_op jit(solution)/shard_map/gate_1/pallas_call | solution.py:697
  164.8 13.4 %within_0.1 = (f32[2048,640]{1,0:T(8,128)}, f32[2048,128]{1,0:T(8,128)S(1)}, f32[136,384]{1,0:T(8,128)S(1)}, bf16[144,384]{1,0:T(8,128)(2,1)S(1)}) custom-call(s32[2,9]{1,0:T(2,128)S(1)} %concatenate.28.meta, bf16[2048,640]{1,0:T(8,128)(2,1)} %get-tuple-element.119.conv, f32[2048,128]{1,0:T(8,128)S(1)} %get-tuple-element.120.deltas, ...), custom_call_target="tpu_custom_call" | custom-call | flops 16099999744 | tf_op jit(solution)/shard_map/within_0/pallas_call | solution.py:697
  184.3 13.4 %within_1.1 = (f32[2048,640]{1,0:T(8,128)}, f32[2048,128]{1,0:T(8,128)S(1)}, f32[136,384]{1,0:T(8,128)S(1)}, bf16[144,384]{1,0:T(8,128)(2,1)S(1)}) custom-call(s32[2,9]{1,0:T(2,128)S(1)} %concatenate.28.meta, bf16[2048,640]{1,0:T(8,128)(2,1)} %get-tuple-element.113.conv, f32[2048,128]{1,0:T(8,128)S(1)} %copy-done.30, bf16[2048,384]{1,0:T(8,128)(2,1)S(1)} %copy-done.32, ...), custom_call_target="tpu_custom_call" | custom-call | flops 16099999744 | tf_op jit(solution)/shard_map/within_1/pallas_call | solution.py:697
  202.7 3.0 add_convert_fusion.1.rest_4_
  206.3 29.2 %across_0.1 = (bf16[2048,896]{1,0:T(8,128)(2,1)}, bf16[2048,128]{1,0:T(8,128)(2,1)S(1)}, f32[16,640]{1,0:T(8,128)S(1)}, f32[16,640]{1,0:T(8,128)S(1)}, f32[40,640]{1,0:T(8,128)S(1)}, /*index=5*/f32[16,128]{1,0:T(8,128)S(1)}) custom-call(s32[2,9]{1,0:T(2,128)S(1)} %concatenate.28.meta, bf16[2048,640]{1,0:T(8,128)(2,1)} %get-tuple-element.119.conv, ...), custom_call_target="tpu_custom_call" | custom-call | flops 36800000000 | tf_op jit(solution)/shard_map/across_0/pallas_call | solution.py:697
  240.5 5.8 %input_0_0.1 = (bf16[2048,768]{1,0:T(8,128)(2,1)}, f32[8,768]{1,0:T(8,128)S(1)}) custom-call(bf16[2,2048,768]{2,1,0:T(8,128)(2,1)} %tokens.21, bf16[2048,384]{1,0:T(8,128)(2,1)S(1)} %copy-done.20, bf16[2048,896]{1,0:T(8,128)(2,1)} %get-tuple-element.167.in_back, bf16[2048,128]{1,0:T(8,128)(2,1)S(1)} %get-tuple-element.168.dt_back, ...), custom_call_target="tpu_custom_call" | custom-call | flops 6899999744 | tf_op jit(solution)/shard_map/input_0_0/pallas_call | solution.py:697
  246.3 5.5 %input_0_2.1 = (bf16[2048,768]{1,0:T(8,128)(2,1)}, f32[8,768]{1,0:T(8,128)S(1)}) custom-call(bf16[2,2048,768]{2,1,0:T(8,128)(2,1)} %tokens.21, bf16[2048,384]{1,0:T(8,128)(2,1)S(1)} %copy-done.20, bf16[2048,896]{1,0:T(8,128)(2,1)} %get-tuple-element.167.in_back, bf16[2048,128]{1,0:T(8,128)(2,1)S(1)} %get-tuple-element.168.dt_back, ...), custom_call_target="tpu_custom_call", output_to_operand_aliasing={{0}: (8, {})} | custom-call | flops 6899999744 | tf_op jit(solution)/shard_map/input_0_2/pallas_call | solution.py:697
  251.8 2.7 constant_dynamic-slice_fusion.8
  254.5 16.8 %collective-permute-done.32 = bf16[1024,768]{1,0:T(8,128)(2,1)} collective-permute-done((bf16[1024,768]{1,0:T(8,128)(2,1)}, bf16[1024,768]{1,0:T(8,128)(2,1)}, u32[]{:S(2)}, u32[]{:S(2)}) %collective-permute-start.32) | collective-permute-done | bytes 1572896 | tf_op jit(solution)/shard_map/ppermute | solution.py:718
  271.3 4.4 fusion.12
  275.8 6.9 %weigh_0.1 = (f32[768,640]{1,0:T(8,128)S(1)}, f32[8,768]{1,0:T(8,128)S(1)}) custom-call(bf16[2048,768]{1,0:T(8,128)(2,1)S(1)} %copy-done.22, bf16[2048,896]{1,0:T(8,128)(2,1)} %get-tuple-element.167.in_back, bf16[2048,128]{1,0:T(8,128)(2,1)S(1)} %get-tuple-element.168.dt_back, f32[16,640]{1,0:T(8,128)S(1)} %get-tuple-element.169.rest_0_.tail, ...), custom_call_target="tpu_custom_call" | custom-call | flops 9200000000 | tf_op jit(solution)/shard_map/weigh_0/pallas_call | solution.py:697
  286.4 29.1 %across_1.1 = (bf16[2048,896]{1,0:T(8,128)(2,1)}, bf16[2048,128]{1,0:T(8,128)(2,1)S(1)}, f32[16,640]{1,0:T(8,128)S(1)}, f32[16,640]{1,0:T(8,128)S(1)}, f32[40,640]{1,0:T(8,128)S(1)}, /*index=5*/f32[16,128]{1,0:T(8,128)S(1)}) custom-call(s32[2,9]{1,0:T(2,128)S(1)} %concatenate.28.meta, bf16[2048,640]{1,0:T(8,128)(2,1)} %get-tuple-element.113.conv, ...), custom_call_target="tpu_custom_call" | custom-call | flops 36800000000 | tf_op jit(solution)/shard_map/across_1/pallas_call | solution.py:697
  317.2 3.2 collective-permute-done.34
  320.4 4.5 fusion.13
  324.9 4.4 input_1_0.1
  329.5 7.1 %weigh_1.1 = (bf16[768,640]{1,0:T(8,128)(2,1)S(1)}, f32[8,768]{1,0:T(8,128)S(1)}) custom-call(bf16[2048,768]{1,0:T(8,128)(2,1)} %get-tuple-element.112.normed, bf16[2048,896]{1,0:T(8,128)(2,1)} %get-tuple-element.176.in_back, bf16[2048,128]{1,0:T(8,128)(2,1)S(1)} %get-tuple-element.177.dt_back, f32[16,640]{1,0:T(8,128)S(1)} %get-tuple-element.178.tail.rest_0_, ...), custom_call_target="tpu_custom_call" | custom-call | flops 9200000000 | tf_op jit(solution)/shard_map/weigh_1/pallas_call | solution.py:697
  336.8 5.3 %input_1_2.1 = (bf16[1024,768]{1,0:T(8,128)(2,1)S(1)}, f32[8,768]{1,0:T(8,128)S(1)}) custom-call(bf16[2,2048,768]{2,1,0:T(8,128)(2,1)} %tokens.21, bf16[2048,384]{1,0:T(8,128)(2,1)S(1)} %copy-done.21, bf16[2048,896]{1,0:T(8,128)(2,1)} %get-tuple-element.176.in_back, bf16[2048,128]{1,0:T(8,128)(2,1)S(1)} %get-tuple-element.177.dt_back, ...), custom_call_target="tpu_custom_call" | custom-call | flops 6899999744 | tf_op jit(solution)/shard_map/input_1_2/pallas_call | solution.py:697
  347.1 3.5 collective-permute-start.35
  352.4 2.5 add_convert_fusion.3
  354.9 9.7 %collective-permute-done.35 = bf16[384,640]{1,0:T(8,128)(2,1)S(1)} collective-permute-done((bf16[384,640]{1,0:T(8,128)(2,1)}, bf16[384,640]{1,0:T(8,128)(2,1)S(1)}, u32[]{:S(2)}, u32[]{:S(2)}) %collective-permute-start.35) | collective-permute-done | bytes 491552 | tf_op jit(solution)/shard_map/ppermute | solution.py:718
  367.2 2.6 collective-permute-start.38
  371.7 2.7 fusion.9
  374.4 6.2 %collective-permute-start.39 = (bf16[96,640]{1,0:T(8,128)(2,1)S(1)}, bf16[96,640]{1,0:T(8,128)(2,1)}, u32[]{:S(2)}, u32[]{:S(2)}) collective-permute-start(bf16[96,640]{1,0:T(8,128)(2,1)S(1)} %get-tuple-element.260), channel_id=1, source_target_pairs={{0,16},{4,20},{8,24},{12,28},{16,0},{20,4},{24,8},{28,12},{1,17},{... | collective-permute-start | bytes 368648 | tf_op jit(solution)/shard_map/ppermute | solution.py:718
  380.6 2.8 collective-permute-start.52
  387.4 5.1 %place_0_0_0.1.rest_0_ = bf16[2,2048,768]{2,1,0:T(8,128)(2,1)} custom-call(s32[1]{0:T(128)} %bitcast.4.side, bf16[1024,768]{1,0:T(8,128)(2,1)S(1)} %copy-done.5, bf16[1024,768]{1,0:T(8,128)(2,1)} %collective-permute-done.42.other, bf16[2,2048,768]{2,1,0:T(8,128)(2,1)} %tokens.21, bf16[384,640]{1,0:T(8,128)(2,1)S(1)} %add_convert_fusion.5.rest_0_.rest_1_, ...), custom_call_target="tpu_custom_call" | custom-call | flops 4600000000 | tf_op jit(solution)/shard_map/place_0_0_0/pallas_call | solution.py:697
  394.1 5.2 %place_1_0_0.1 = bf16[2,2048,768]{2,1,0:T(8,128)(2,1)} custom-call(s32[1]{0:T(128)} %bitcast.4.side, bf16[1024,768]{1,0:T(8,128)(2,1)} %get-tuple-element.247.mine, bf16[1024,768]{1,0:T(8,128)(2,1)} %collective-permute-done.41.other, bf16[2,2048,768]{2,1,0:T(8,128)(2,1)} %tokens.21, ...), custom_call_target="tpu_custom_call", output_to_operand_aliasing={{}: (4, {})} | custom-call | flops 4600000000 | tf_op jit(solution)/shard_map/place_1_0_0/pallas_call | solution.py:697
  404.8 4.5 collective-permute-done.40
  412.9 2.5 convert_add_fusion.3
  415.4 6.9 %place_0_0_1.1.rest_2_ = bf16[2,2048,768]{2,1,0:T(8,128)(2,1)} custom-call(s32[1]{0:T(128)} %bitcast.4.side, bf16[1024,768]{1,0:T(8,128)(2,1)} %get-tuple-element.243.mine, bf16[1024,768]{1,0:T(8,128)(2,1)} %collective-permute-done.50.other, bf16[2,2048,768]{2,1,0:T(8,128)(2,1)} %tokens.21, bf16[2,2048,768]{2,1,0:T(8,128)(2,1)} %rest_0_.5, ...), custom_call_target="tpu_custom_call" | custom-call | flops 4600000000 | tf_op jit(solution)/shard_map/place_0_0_1/pallas_call | solution.py:697
  423.8 2.4 collective-permute-start.56
  430.7 7.2 %collective-permute-done.57 = bf16[96,512]{1,0:T(8,128)(2,1)S(1)} collective-permute-done((bf16[96,512]{1,0:T(8,128)(2,1)S(1)}, bf16[96,512]{1,0:T(8,128)(2,1)S(1)}, u32[]{:S(2)}, u32[]{:S(2)}) %collective-permute-start.57) | collective-permute-done | bytes 98336 | tf_op jit(solution)/shard_map/ppermute | solution.py:718
  440.0 4.1 place_1_0_1.1.rest_2_
  444.2 5.2 %collective-permute-done.59 = bf16[384,512]{1,0:T(8,128)(2,1)S(1)} collective-permute-done((bf16[384,512]{1,0:T(8,128)(2,1)}, bf16[384,512]{1,0:T(8,128)(2,1)S(1)}, u32[]{:S(2)}, u32[]{:S(2)}) %collective-permute-start.59) | collective-permute-done | bytes 393248 | tf_op jit(solution)/shard_map/ppermute | solution.py:718
  450.8 3.2 copy.48
  455.2 3.9 place_1_1024_1.1
  (322 shorter events, 89.5 us)
Async XLA Ops:
  7.2 376.2 %all-reduce.13.cloned.1.call-start = ((), (), s32[]{:S(2)}) async-start(), calls=%async_computation | async-start | bytes 4718592 | tf_op jit(solution)/shard_map/psum | solution.py:1109
  8.0 11.2 %collective-permute-start = (bf16[2,16,768]{2,1,0:T(8,128)(2,1)S(1)}, bf16[2,16,768]{2,1,0:T(8,128)(2,1)S(1)}, u32[]{:S(2)}, u32[]{:S(2)}) collective-permute-start(bf16[2,16,768]{2,1,0:T(8,128)(2,1)S(1)} %slice.114), channel_id=1, source_target_pairs={{0,4},{4,8},{8,12},{12,16},{16,20},{20,24},{24,28},{1,5},{5,9},{9,... | collective-permute-start | bytes 147464 | tf_op jit(solution)/shard_map/ppermute | solution.py:724
  38.8 35.4 %collective-permute-start.4 = (bf16[144,384]{1,0:T(8,128)(2,1)S(1)}, bf16[144,384]{1,0:T(8,128)(2,1)S(1)}, u32[]{:S(2)}, u32[]{:S(2)}) collective-permute-start(bf16[144,384]{1,0:T(8,128)(2,1)S(1)} %get-tuple-element.111.rest_0_), channel_id=1, source_target_pairs={{0,4},{4,8},{8,12},{12,16},{16,20},{20,24},{24,28},{1,5},{5,9},{9,... | collective-permute-start | bytes 331784 | tf_op jit(solution)/shard_map/ppermute | solution.py:724
  42.5 33.3 %collective-permute-start.5 = (bf16[144,384]{1,0:T(8,128)(2,1)S(1)}, bf16[144,384]{1,0:T(8,128)(2,1)S(1)}, u32[]{:S(2)}, u32[]{:S(2)}) collective-permute-start(bf16[144,384]{1,0:T(8,128)(2,1)S(1)} %get-tuple-element.111.rest_0_), channel_id=1, source_target_pairs={{0,8},{4,12},{8,16},{12,20},{16,24},{20,28},{1,9},{5,13},{9,17},{1... | collective-permute-start | bytes 331784 | tf_op jit(solution)/shard_map/ppermute | solution.py:724
  46.0 29.9 %collective-permute-start.6 = (bf16[144,384]{1,0:T(8,128)(2,1)S(1)}, bf16[144,384]{1,0:T(8,128)(2,1)S(1)}, u32[]{:S(2)}, u32[]{:S(2)}) collective-permute-start(bf16[144,384]{1,0:T(8,128)(2,1)S(1)} %get-tuple-element.111.rest_0_), channel_id=1, source_target_pairs={{0,12},{4,16},{8,20},{12,24},{16,28},{1,13},{5,17},{9,21},{13,25},... | collective-permute-start | bytes 331784 | tf_op jit(solution)/shard_map/ppermute | solution.py:724
  69.8 15.3 %collective-permute-start.1 = (bf16[144,384]{1,0:T(8,128)(2,1)S(1)}, bf16[144,384]{1,0:T(8,128)(2,1)S(1)}, u32[]{:S(2)}, u32[]{:S(2)}) collective-permute-start(bf16[144,384]{1,0:T(8,128)(2,1)S(1)} %get-tuple-element.118.rest_3_), channel_id=1, source_target_pairs={{0,4},{4,8},{8,12},{12,16},{16,20},{20,24},{24,28},{1,5},{5,9},{9,... | collective-permute-start | bytes 331784 | tf_op jit(solution)/shard_map/ppermute | solution.py:724
  71.7 13.4 %collective-permute-start.2 = (bf16[144,384]{1,0:T(8,128)(2,1)S(1)}, bf16[144,384]{1,0:T(8,128)(2,1)S(1)}, u32[]{:S(2)}, u32[]{:S(2)}) collective-permute-start(bf16[144,384]{1,0:T(8,128)(2,1)S(1)} %get-tuple-element.118.rest_3_), channel_id=1, source_target_pairs={{0,8},{4,12},{8,16},{12,20},{16,24},{20,28},{1,9},{5,13},{9,17},{1... | collective-permute-start | bytes 331784 | tf_op jit(solution)/shard_map/ppermute | solution.py:724
  74.2 10.9 %collective-permute-start.3 = (bf16[144,384]{1,0:T(8,128)(2,1)S(1)}, bf16[144,384]{1,0:T(8,128)(2,1)S(1)}, u32[]{:S(2)}, u32[]{:S(2)}) collective-permute-start(bf16[144,384]{1,0:T(8,128)(2,1)S(1)} %get-tuple-element.118.rest_3_), channel_id=1, source_target_pairs={{0,12},{4,16},{8,20},{12,24},{16,28},{1,13},{5,17},{9,21},{13,25},... | collective-permute-start | bytes 331784 | tf_op jit(solution)/shard_map/ppermute | solution.py:724
  81.9 11.9 %collective-permute-start.9 = (bf16[144,384]{1,0:T(8,128)(2,1)S(1)}, bf16[144,384]{1,0:T(8,128)(2,1)S(1)}, u32[]{:S(2)}, u32[]{:S(2)}) collective-permute-start(bf16[144,384]{1,0:T(8,128)(2,1)S(1)} %get-tuple-element.132), channel_id=1, source_target_pairs={{0,12},{4,16},{8,20},{12,24},{16,28},{1,13},{5,17},{9,21},{13,25},... | collective-permute-start | bytes 331784 | tf_op jit(solution)/shard_map/ppermute | solution.py:724
  91.3 14.1 %collective-permute-start.7 = (bf16[144,384]{1,0:T(8,128)(2,1)S(1)}, bf16[144,384]{1,0:T(8,128)(2,1)S(1)}, u32[]{:S(2)}, u32[]{:S(2)}) collective-permute-start(bf16[144,384]{1,0:T(8,128)(2,1)S(1)} %get-tuple-element.127), channel_id=1, source_target_pairs={{0,12},{4,16},{8,20},{12,24},{16,28},{1,13},{5,17},{9,21},{13,25},... | collective-permute-start | bytes 331784 | tf_op jit(solution)/shard_map/ppermute | solution.py:724
  92.5 12.8 %collective-permute-start.8 = (bf16[144,384]{1,0:T(8,128)(2,1)S(1)}, bf16[144,384]{1,0:T(8,128)(2,1)S(1)}, u32[]{:S(2)}, u32[]{:S(2)}) collective-permute-start(bf16[144,384]{1,0:T(8,128)(2,1)S(1)} %get-tuple-element.127), channel_id=1, source_target_pairs={{0,24},{4,28},{1,25},{5,29},{2,26},{6,30},{3,27},{7,31}} | collective-permute-start | bytes 331784 | tf_op jit(solution)/shard_map/ppermute | solution.py:724
  103.5 13.3 %collective-permute-start.14 = (f32[8,2048]{1,0:T(8,128)S(1)}, f32[8,2048]{1,0:T(8,128)S(1)}, u32[]{:S(2)}, u32[]{:S(2)}) collective-permute-start(f32[8,2048]{1,0:T(8,128)S(1)} %get-tuple-element.133.rest_3_.stats_a), channel_id=1, source_target_pairs={{0,1},{1,0},{2,3},{3,2},{4,5},{5,4},{6,7},{7,6},{8,9},{9,8},{10,11... | collective-permute-start | bytes 196616 | tf_op jit(solution)/shard_map/ppermute | solution.py:718
  103.5 13.3 %collective-permute-start.15 = (f32[8,2048]{1,0:T(8,128)S(1)}, f32[8,2048]{1,0:T(8,128)S(1)}, u32[]{:S(2)}, u32[]{:S(2)}) collective-permute-start(f32[8,2048]{1,0:T(8,128)S(1)} %get-tuple-element.133.rest_3_.stats_a), channel_id=1, source_target_pairs={{0,2},{1,3},{2,0},{3,1},{4,6},{5,7},{6,4},{7,5},{8,10},{9,11},{10,... | collective-permute-start | bytes 196616 | tf_op jit(solution)/shard_map/ppermute | solution.py:718
  105.0 11.8 %collective-permute-start.16 = (f32[8,2048]{1,0:T(8,128)S(1)}, f32[8,2048]{1,0:T(8,128)S(1)}, u32[]{:S(2)}, u32[]{:S(2)}) collective-permute-start(f32[8,2048]{1,0:T(8,128)S(1)} %get-tuple-element.133.rest_3_.stats_a), channel_id=1, source_target_pairs={{0,3},{1,2},{2,1},{3,0},{4,7},{5,6},{6,5},{7,4},{8,11},{9,10},{10,... | collective-permute-start | bytes 196616 | tf_op jit(solution)/shard_map/ppermute | solution.py:718
  115.0 21.8 %collective-permute-start.11 = (f32[8,2048]{1,0:T(8,128)S(1)}, f32[8,2048]{1,0:T(8,128)S(1)}, u32[]{:S(2)}, u32[]{:S(2)}) collective-permute-start(f32[8,2048]{1,0:T(8,128)S(1)} %get-tuple-element.135.rest_0_.stats_a), channel_id=1, source_target_pairs={{0,1},{1,0},{2,3},{3,2},{4,5},{5,4},{6,7},{7,6},{8,9},{9,8},{10,11... | collective-permute-start | bytes 196616 | tf_op jit(solution)/shard_map/ppermute | solution.py:718
  115.2 23.1 %collective-permute-start.12 = (f32[8,2048]{1,0:T(8,128)S(1)}, f32[8,2048]{1,0:T(8,128)S(1)}, u32[]{:S(2)}, u32[]{:S(2)}) collective-permute-start(f32[8,2048]{1,0:T(8,128)S(1)} %get-tuple-element.135.rest_0_.stats_a), channel_id=1, source_target_pairs={{0,2},{1,3},{2,0},{3,1},{4,6},{5,7},{6,4},{7,5},{8,10},{9,11},{10,... | collective-permute-start | bytes 196616 | tf_op jit(solution)/shard_map/ppermute | solution.py:718
  116.8 21.6 %collective-permute-start.13 = (f32[8,2048]{1,0:T(8,128)S(1)}, f32[8,2048]{1,0:T(8,128)S(1)}, u32[]{:S(2)}, u32[]{:S(2)}) collective-permute-start(f32[8,2048]{1,0:T(8,128)S(1)} %get-tuple-element.135.rest_0_.stats_a), channel_id=1, source_target_pairs={{0,3},{1,2},{2,1},{3,0},{4,7},{5,6},{6,5},{7,4},{8,11},{9,10},{10,... | collective-permute-start | bytes 196616 | tf_op jit(solution)/shard_map/ppermute | solution.py:718
  134.2 27.4 %collective-permute-start.20 = (bf16[144,384]{1,0:T(8,128)(2,1)S(1)}, bf16[144,384]{1,0:T(8,128)(2,1)S(1)}, u32[]{:S(2)}, u32[]{:S(2)}) collective-permute-start(bf16[144,384]{1,0:T(8,128)(2,1)S(1)} %get-tuple-element.141.rest_3_), channel_id=1, source_target_pairs={{4,0},{8,4},{12,8},{16,12},{20,16},{24,20},{28,24},{5,1},{9,5},{13... | collective-permute-start | bytes 331784 | tf_op jit(solution)/shard_map/ppermute | solution.py:724
  135.5 27.4 %collective-permute-start.21 = (bf16[144,384]{1,0:T(8,128)(2,1)S(1)}, bf16[144,384]{1,0:T(8,128)(2,1)S(1)}, u32[]{:S(2)}, u32[]{:S(2)}) collective-permute-start(bf16[144,384]{1,0:T(8,128)(2,1)S(1)} %get-tuple-element.141.rest_3_), channel_id=1, source_target_pairs={{8,0},{12,4},{16,8},{20,12},{24,16},{28,20},{9,1},{13,5},{17,9},{2... | collective-permute-start | bytes 331784 | tf_op jit(solution)/shard_map/ppermute | solution.py:724
  136.8 27.4 %collective-permute-start.22 = (bf16[144,384]{1,0:T(8,128)(2,1)S(1)}, bf16[144,384]{1,0:T(8,128)(2,1)S(1)}, u32[]{:S(2)}, u32[]{:S(2)}) collective-permute-start(bf16[144,384]{1,0:T(8,128)(2,1)S(1)} %get-tuple-element.141.rest_3_), channel_id=1, source_target_pairs={{12,0},{16,4},{20,8},{24,12},{28,16},{13,1},{17,5},{21,9},{25,13},... | collective-permute-start | bytes 331784 | tf_op jit(solution)/shard_map/ppermute | solution.py:724
  156.6 26.4 %collective-permute-start.17 = (bf16[144,384]{1,0:T(8,128)(2,1)S(1)}, bf16[144,384]{1,0:T(8,128)(2,1)S(1)}, u32[]{:S(2)}, u32[]{:S(2)}) collective-permute-start(bf16[144,384]{1,0:T(8,128)(2,1)S(1)} %get-tuple-element.143.rest_3_), channel_id=1, source_target_pairs={{4,0},{8,4},{12,8},{16,12},{20,16},{24,20},{28,24},{5,1},{9,5},{13... | collective-permute-start | bytes 331784 | tf_op jit(solution)/shard_map/ppermute | solution.py:724
  159.6 18.6 %collective-permute-start.23 = (bf16[1024,768]{1,0:T(8,128)(2,1)S(1)}, bf16[1024,768]{1,0:T(8,128)(2,1)S(1)}, u32[]{:S(2)}, u32[]{:S(2)}) collective-permute-start(bf16[1024,768]{1,0:T(8,128)(2,1)S(1)} %constant_dynamic-slice_fusion.10), channel_id=1, source_target_pairs={{0,1},{1,0},{2,3},{3,2},{4,5},{5,4},{6,7},{7,6},{8,9},{9,8},{10,11... | collective-permute-start | bytes 4718600 | tf_op jit(solution)/shard_map/ppermute | solution.py:718
  161.6 22.8 %collective-permute-start.18 = (bf16[144,384]{1,0:T(8,128)(2,1)S(1)}, bf16[144,384]{1,0:T(8,128)(2,1)S(1)}, u32[]{:S(2)}, u32[]{:S(2)}) collective-permute-start(bf16[144,384]{1,0:T(8,128)(2,1)S(1)} %get-tuple-element.143.rest_3_), channel_id=1, source_target_pairs={{8,0},{12,4},{16,8},{20,12},{24,16},{28,20},{9,1},{13,5},{17,9},{2... | collective-permute-start | bytes 331784 | tf_op jit(solution)/shard_map/ppermute | solution.py:724
  162.8 21.5 %collective-permute-start.19 = (bf16[144,384]{1,0:T(8,128)(2,1)S(1)}, bf16[144,384]{1,0:T(8,128)(2,1)S(1)}, u32[]{:S(2)}, u32[]{:S(2)}) collective-permute-start(bf16[144,384]{1,0:T(8,128)(2,1)S(1)} %get-tuple-element.143.rest_3_), channel_id=1, source_target_pairs={{12,0},{16,4},{20,8},{24,12},{28,16},{13,1},{17,5},{21,9},{25,13},... | collective-permute-start | bytes 331784 | tf_op jit(solution)/shard_map/ppermute | solution.py:724
  164.2 36.9 %collective-permute-start.28 = (bf16[1024,768]{1,0:T(8,128)(2,1)}, bf16[1024,768]{1,0:T(8,128)(2,1)S(1)}, u32[]{:S(2)}, u32[]{:S(2)}) collective-permute-start(bf16[1024,768]{1,0:T(8,128)(2,1)} %constant_dynamic-slice_fusion.9), channel_id=1, source_target_pairs={{0,1},{1,0},{2,3},{3,2},{4,5},{5,4},{6,7},{7,6},{8,9},{9,8},{10,11... | collective-permute-start | bytes 4718600 | tf_op jit(solution)/shard_map/ppermute | solution.py:718
  179.3 26.4 %collective-permute-start.26 = (bf16[144,384]{1,0:T(8,128)(2,1)S(1)}, bf16[144,384]{1,0:T(8,128)(2,1)S(1)}, u32[]{:S(2)}, u32[]{:S(2)}) collective-permute-start(bf16[144,384]{1,0:T(8,128)(2,1)S(1)} %get-tuple-element.162), channel_id=1, source_target_pairs={{12,0},{16,4},{20,8},{24,12},{28,16},{13,1},{17,5},{21,9},{25,13},... | collective-permute-start | bytes 331784 | tf_op jit(solution)/shard_map/ppermute | solution.py:724
  183.0 23.2 %collective-permute-start.27 = (bf16[144,384]{1,0:T(8,128)(2,1)S(1)}, bf16[144,384]{1,0:T(8,128)(2,1)S(1)}, u32[]{:S(2)}, u32[]{:S(2)}) collective-permute-start(bf16[144,384]{1,0:T(8,128)(2,1)S(1)} %get-tuple-element.162), channel_id=1, source_target_pairs={{24,0},{28,4},{25,1},{29,5},{26,2},{30,6},{27,3},{31,7}} | collective-permute-start | bytes 331784 | tf_op jit(solution)/shard_map/ppermute | solution.py:724
  197.8 42.7 %collective-permute-start.24 = (bf16[144,384]{1,0:T(8,128)(2,1)S(1)}, bf16[144,384]{1,0:T(8,128)(2,1)S(1)}, u32[]{:S(2)}, u32[]{:S(2)}) collective-permute-start(bf16[144,384]{1,0:T(8,128)(2,1)S(1)} %get-tuple-element.153), channel_id=1, source_target_pairs={{12,0},{16,4},{20,8},{24,12},{28,16},{13,1},{17,5},{21,9},{25,13},... | collective-permute-start | bytes 331784 | tf_op jit(solution)/shard_map/ppermute | solution.py:724
  199.3 41.1 %collective-permute-start.25 = (bf16[144,384]{1,0:T(8,128)(2,1)S(1)}, bf16[144,384]{1,0:T(8,128)(2,1)S(1)}, u32[]{:S(2)}, u32[]{:S(2)}) collective-permute-start(bf16[144,384]{1,0:T(8,128)(2,1)S(1)} %get-tuple-element.153), channel_id=1, source_target_pairs={{24,0},{28,4},{25,1},{29,5},{26,2},{30,6},{27,3},{31,7}} | collective-permute-start | bytes 331784 | tf_op jit(solution)/shard_map/ppermute | solution.py:724
  201.1 37.3 %collective-permute-start.30 = (bf16[1024,768]{1,0:T(8,128)(2,1)S(1)}, bf16[1024,768]{1,0:T(8,128)(2,1)S(1)}, u32[]{:S(2)}, u32[]{:S(2)}) collective-permute-start(bf16[1024,768]{1,0:T(8,128)(2,1)S(1)} %add_convert_fusion.2.rest_4_), channel_id=1, source_target_pairs={{0,2},{1,3},{2,0},{3,1},{4,6},{5,7},{6,4},{7,5},{8,10},{9,11},{10,... | collective-permute-start | bytes 4718600 | tf_op jit(solution)/shard_map/ppermute | solution.py:718
  205.7 65.6 %collective-permute-start.32 = (bf16[1024,768]{1,0:T(8,128)(2,1)}, bf16[1024,768]{1,0:T(8,128)(2,1)}, u32[]{:S(2)}, u32[]{:S(2)}) collective-permute-start(bf16[1024,768]{1,0:T(8,128)(2,1)} %add_convert_fusion.1.rest_4_), channel_id=1, source_target_pairs={{0,2},{1,3},{2,0},{3,1},{4,6},{5,7},{6,4},{7,5},{8,10},{9,11},{10,... | collective-permute-start | bytes 4718600 | tf_op jit(solution)/shard_map/ppermute | solution.py:718
  235.5 10.9 %collective-permute-start.29 = (f32[16,640]{1,0:T(8,128)S(1)}, f32[16,640]{1,0:T(8,128)S(1)}, u32[]{:S(2)}, u32[]{:S(2)}) collective-permute-start(f32[16,640]{1,0:T(8,128)S(1)} %get-tuple-element.170), channel_id=1, source_target_pairs={{4,0},{8,4},{12,8},{16,12},{20,16},{24,20},{28,24},{5,1},{9,5},{13... | collective-permute-start | bytes 122888 | tf_op jit(solution)/shard_map/ppermute | solution.py:724
  254.5 28.3 %collective-permute-start.31 = (bf16[1024,768]{1,0:T(8,128)(2,1)}, bf16[1024,768]{1,0:T(8,128)(2,1)}, u32[]{:S(2)}, u32[]{:S(2)}) collective-permute-start(bf16[1024,768]{1,0:T(8,128)(2,1)} %constant_dynamic-slice_fusion.8), channel_id=1, source_target_pairs={{0,1},{1,0},{2,3},{3,2},{4,5},{5,4},{6,7},{7,6},{8,9},{9,8},{10,11... | collective-permute-start | bytes 4718600 | tf_op jit(solution)/shard_map/ppermute | solution.py:718
  284.7 35.7 %collective-permute-start.34 = (bf16[1024,768]{1,0:T(8,128)(2,1)S(1)}, bf16[1024,768]{1,0:T(8,128)(2,1)}, u32[]{:S(2)}, u32[]{:S(2)}) collective-permute-start(bf16[1024,768]{1,0:T(8,128)(2,1)S(1)} %add_convert_fusion.rest_5_), channel_id=1, source_target_pairs={{0,2},{1,3},{2,0},{3,1},{4,6},{5,7},{6,4},{7,5},{8,10},{9,11},{10,... | collective-permute-start | bytes 4718600 | tf_op jit(solution)/shard_map/ppermute | solution.py:718
  315.5 14.0 %collective-permute-start.33 = (f32[16,640]{1,0:T(8,128)S(1)}, f32[16,640]{1,0:T(8,128)S(1)}, u32[]{:S(2)}, u32[]{:S(2)}) collective-permute-start(f32[16,640]{1,0:T(8,128)S(1)} %get-tuple-element.179), channel_id=1, source_target_pairs={{4,0},{8,4},{12,8},{16,12},{20,16},{24,20},{28,24},{5,1},{9,5},{13... | collective-permute-start | bytes 122888 | tf_op jit(solution)/shard_map/ppermute | solution.py:724
  345.5 48.4 %collective-permute-start.41 = (bf16[1024,768]{1,0:T(8,128)(2,1)}, bf16[1024,768]{1,0:T(8,128)(2,1)}, u32[]{:S(2)}, u32[]{:S(2)}) collective-permute-start(bf16[1024,768]{1,0:T(8,128)(2,1)} %get-tuple-element.247.mine), channel_id=1, source_target_pairs={{0,1},{1,0},{2,3},{3,2},{4,5},{5,4},{6,7},{7,6},{8,9},{9,8},{10,11... | collective-permute-start | bytes 4718600 | tf_op jit(solution)/shard_map/ppermute | solution.py:718
  345.6 35.0 %collective-permute-start.42 = (bf16[1024,768]{1,0:T(8,128)(2,1)S(1)}, bf16[1024,768]{1,0:T(8,128)(2,1)}, u32[]{:S(2)}, u32[]{:S(2)}) collective-permute-start(bf16[1024,768]{1,0:T(8,128)(2,1)S(1)} %get-tuple-element.245.mine), channel_id=1, source_target_pairs={{0,1},{1,0},{2,3},{3,2},{4,5},{5,4},{6,7},{7,6},{8,9},{9,8},{10,11... | collective-permute-start | bytes 4718600 | tf_op jit(solution)/shard_map/ppermute | solution.py:718
  347.1 17.5 %collective-permute-start.35 = (bf16[384,640]{1,0:T(8,128)(2,1)}, bf16[384,640]{1,0:T(8,128)(2,1)S(1)}, u32[]{:S(2)}, u32[]{:S(2)}) collective-permute-start(bf16[384,640]{1,0:T(8,128)(2,1)} %get-tuple-element.255), channel_id=1, source_target_pairs={{0,4},{4,0},{8,12},{12,8},{16,20},{20,16},{24,28},{28,24},{1,5},{5... | collective-permute-start | bytes 1474568 | tf_op jit(solution)/shard_map/ppermute | solution.py:718
  350.6 19.3 %collective-permute-start.43 = (bf16[512,768]{1,0:T(8,128)(2,1)S(1)}, bf16[512,768]{1,0:T(8,128)(2,1)}, u32[]{:S(2)}, u32[]{:S(2)}) collective-permute-start(bf16[512,768]{1,0:T(8,128)(2,1)S(1)} %add_convert_fusion.4.rest_3_), channel_id=1, source_target_pairs={{0,2},{1,3},{2,0},{3,1},{4,6},{5,7},{6,4},{7,5},{8,10},{9,11},{10,... | collective-permute-start | bytes 2359304 | tf_op jit(solution)/shard_map/ppermute | solution.py:718
  352.3 63.0 %collective-permute-start.50 = (bf16[1024,768]{1,0:T(8,128)(2,1)}, bf16[1024,768]{1,0:T(8,128)(2,1)}, u32[]{:S(2)}, u32[]{:S(2)}) collective-permute-start(bf16[1024,768]{1,0:T(8,128)(2,1)} %get-tuple-element.243.mine), channel_id=1, source_target_pairs={{0,1},{1,0},{2,3},{3,2},{4,5},{5,4},{6,7},{7,6},{8,9},{9,8},{10,11... | collective-permute-start | bytes 4718600 | tf_op jit(solution)/shard_map/ppermute | solution.py:718
  367.2 36.9 %collective-permute-start.38 = (bf16[96,640]{1,0:T(8,128)(2,1)}, bf16[96,640]{1,0:T(8,128)(2,1)S(1)}, u32[]{:S(2)}, u32[]{:S(2)}) collective-permute-start(bf16[96,640]{1,0:T(8,128)(2,1)} %get-tuple-element.261), channel_id=1, source_target_pairs={{0,8},{4,12},{8,0},{12,4},{16,24},{20,28},{24,16},{28,20},{1,9},{5... | collective-permute-start | bytes 368648 | tf_op jit(solution)/shard_map/ppermute | solution.py:718
  374.4 29.9 %collective-permute-start.39 = (bf16[96,640]{1,0:T(8,128)(2,1)S(1)}, bf16[96,640]{1,0:T(8,128)(2,1)}, u32[]{:S(2)}, u32[]{:S(2)}) collective-permute-start(bf16[96,640]{1,0:T(8,128)(2,1)S(1)} %get-tuple-element.260), channel_id=1, source_target_pairs={{0,16},{4,20},{8,24},{12,28},{16,0},{20,4},{24,8},{28,12},{1,17},{... | collective-permute-start | bytes 368648 | tf_op jit(solution)/shard_map/ppermute | solution.py:718
  380.6 11.8 %collective-permute-start.52 = (f32[72,128]{1,0:T(8,128)S(1)}, f32[72,128]{1,0:T(8,128)S(1)}, u32[]{:S(2)}, u32[]{:S(2)}) collective-permute-start(f32[72,128]{1,0:T(8,128)S(1)} %fusion.8), channel_id=1, source_target_pairs={{0,8},{4,12},{8,0},{12,4},{16,24},{20,28},{24,16},{28,20},{1,9},{5... | collective-permute-start | bytes 110600 | tf_op jit(solution)/shard_map/ppermute | solution.py:718
  392.4 19.2 %collective-permute-start.44 = (bf16[512,768]{1,0:T(8,128)(2,1)}, bf16[512,768]{1,0:T(8,128)(2,1)}, u32[]{:S(2)}, u32[]{:S(2)}) collective-permute-start(bf16[512,768]{1,0:T(8,128)(2,1)} %add_convert_fusion.3), channel_id=1, source_target_pairs={{0,2},{1,3},{2,0},{3,1},{4,6},{5,7},{6,4},{7,5},{8,10},{9,11},{10,... | collective-permute-start | bytes 2359304 | tf_op jit(solution)/shard_map/ppermute | solution.py:718
  404.1 36.0 %collective-permute-start.46 = (bf16[512,768]{1,0:T(8,128)(2,1)}, bf16[512,768]{1,0:T(8,128)(2,1)}, u32[]{:S(2)}, u32[]{:S(2)}) collective-permute-start(bf16[512,768]{1,0:T(8,128)(2,1)} %get-tuple-element.251.mine), channel_id=1, source_target_pairs={{0,1},{1,0},{2,3},{3,2},{4,5},{5,4},{6,7},{7,6},{8,9},{9,8},{10,11... | collective-permute-start | bytes 2359304 | tf_op jit(solution)/shard_map/ppermute | solution.py:718
  410.3 11.9 %collective-permute-start.47 = (f32[96,256]{1,0:T(8,128)S(1)}, f32[96,256]{1,0:T(8,128)S(1)}, u32[]{:S(2)}, u32[]{:S(2)}) collective-permute-start(f32[96,256]{1,0:T(8,128)S(1)} %slice.144), channel_id=1, source_target_pairs={{0,1},{1,0},{2,3},{3,2},{4,5},{5,4},{6,7},{7,6},{8,9},{9,8},{10,11... | collective-permute-start | bytes 294920 | tf_op jit(solution)/shard_map/ppermute | solution.py:718
  410.4 11.8 %collective-permute-start.48 = (f32[96,256]{1,0:T(8,128)S(1)}, f32[96,256]{1,0:T(8,128)S(1)}, u32[]{:S(2)}, u32[]{:S(2)}) collective-permute-start(f32[96,256]{1,0:T(8,128)S(1)} %slice.144), channel_id=1, source_target_pairs={{0,2},{1,3},{2,0},{3,1},{4,6},{5,7},{6,4},{7,5},{8,10},{9,11},{10,... | collective-permute-start | bytes 294920 | tf_op jit(solution)/shard_map/ppermute | solution.py:718
  430.1 24.8 %collective-permute-start.45 = (bf16[512,768]{1,0:T(8,128)(2,1)}, bf16[512,768]{1,0:T(8,128)(2,1)}, u32[]{:S(2)}, u32[]{:S(2)}) collective-permute-start(bf16[512,768]{1,0:T(8,128)(2,1)} %get-tuple-element.250.mine), channel_id=1, source_target_pairs={{0,1},{1,0},{2,3},{3,2},{4,5},{5,4},{6,7},{7,6},{8,9},{9,8},{10,11... | collective-permute-start | bytes 2359304 | tf_op jit(solution)/shard_map/ppermute | solution.py:718
  (78 other events, 828.7 us)
Sparse Core Ops, SparseCore 0:
  254.6 117.9 all-reduce.12

commit v3 on v2

--- a/solution.py
+++ b/solution.py
@@ -107,6 +107,12 @@
             hit = hit | (places == start)
         return hit
 
+    def none_near(self, first, rows):
+        near = (self.starts[0] >= first - 2) & (self.starts[0] <= first + rows + 2)
+        for start in self.starts[1:]:
+            near = near | ((start >= first - 2) & (start <= first + rows + 2))
+        return jnp.logical_not(near)
+
     def tap_masks(self, first, rows):
         places = first + iota((rows, 128), 0)
         masks = []
@@ -195,14 +201,33 @@
     deltas = softplus(dot(normed, weights[:, channels + width + 256 :]) + dt_bias)
     deltas_o[...] = deltas
     first = docs.anchor + step * tile
-    masks = docs.tap_masks(first, tile)
-    for slab in range(width // 128):
-        lanes = slice(128 * slab, 128 * slab + 128)
-        pre = shift[:, lanes] + taps[3:4, lanes] * ext[8 : 8 + tile, lanes]
-        for back in range(1, 4):
-            pre = pre + taps[3 - back : 4 - back, lanes] * ext[8 - back : 8 - back + tile, lanes] * masks[back - 1]
-        pre_o[:, lanes] = pre.astype(BF)
-        conv_o[:, lanes] = (pre * sigmoid(pre)).astype(BF)
+    plain = docs.none_near(first, tile)
+
+    def convolve(masks):
+        for slab in range(width // 128):
+            lanes = slice(128 * slab, 128 * slab + 128)
+            if masks is None:
+                source = ext[:, lanes]
+                pre = shift[:, lanes] + taps[3:4, lanes] * source[8:]
+            else:
+                pre = shift[:, lanes] + taps[3:4, lanes] * ext[8 : 8 + tile, lanes]
+            for back in range(1, 4):
+                if masks is None:
+                    moved = pltpu.roll(source, back, 0)[8:]
+                else:
+                    moved = ext[8 - back : 8 - back + tile, lanes] * masks[back - 1]
+                pre = pre + taps[3 - back : 4 - back, lanes] * moved
+            pre_o[:, lanes] = pre.astype(BF)
+            conv_o[:, lanes] = (pre * sigmoid(pre)).astype(BF)
+
+    @pl.when(plain)
+    def _():
+        convolve(None)
+
+    @pl.when(jnp.logical_not(plain))
+    def _():
+        convolve(docs.tap_masks(first, tile))
+
     parts = Tile(docs, first, deltas, rate, wedge[...])
     count = len(parts.parts)
     wide = spread_heads(
@@ -298,13 +323,15 @@
 
 
 def third_kernel(
-    tile, channels, full, chained,
-    meta, mixed, gate, conv, deltas, normed, cotangent, out_weight, table, spread, wedge,
+    tile, channels, full, chained, final,
+    side, meta, mixed, gate, conv, deltas, normed, cotangent, out_weight, table, spread, wedge,
     stats_a, stats_b, stats_c, stats_d, *rest, m,
 ):
     if chained:
         grad_out_i, grad_gate_i, rows_i, *rest = rest
-    branch_o, gate_back_o, ssd_back_o, held_o, sums_o, leaving_o, grad_out, grad_gate, rows_o, state, total = rest[-11:]
+    grad_out, grad_gate, state, total = rest[-4:]
+    *grads_o, rows_o = rest[: -4][-2 if final else -3 :]
+    mine_o, other_o, gate_back_o, ssd_back_o, held_o, sums_o, leaving_o = rest[: -4 - len(grads_o) - 1][-7:]
     step = pl.program_id(0)
     gate_gain = table[GATE : GATE + 1, :channels]
     rate = table[RATE : RATE + 1, :128]
@@ -362,12 +389,31 @@
         entered = stacked(ssd_back.astype(F32) * wide[c], 0)
         state[...] = state[...] * wide[count + c][0:1] + dot_tn(twice(reads, 0), entered)
     branch = jnp.concatenate(branches[::-1], axis=0)
-    branch_o[...] = dot(branch, out_weight[...]).astype(BF)
+    part = dot(branch, out_weight[...]).astype(BF)
+    here = place // (pl.num_programs(0) // 2) == side[0]
+
+    @pl.when(here)
+    def _():
+        mine_o[...] = part
+
+    @pl.when(jnp.logical_not(here))
+    def _():
+        other_o[...] = part
+
     grad_out[...] += dot_tn(branch, cotangent[...])
     grad_gate[...] += dot_tn(normed[...], gate_back_o[...])
 
     @pl.when(step == pl.num_programs(0) - 1)
     def _():
+        if final:
+            depth = grad_gate.shape[0]
+            grads_o[0][:depth, :] = grad_gate[...].astype(BF)
+            for block in range(grad_out.shape[1] // channels):
+                lanes = slice(channels * block, channels * block + channels)
+                grads_o[0][depth + channels * block : depth + channels * (block + 1), :] = grad_out[:, lanes].astype(BF)
+        else:
+            grads_o[0][...] = grad_out[...]
+            grads_o[1][...] = grad_gate[...]
         end = docs.anchor + pl.num_programs(0) * tile - 1
         through = jnp.where(docs.counts(end) == docs.counts(docs.anchor - 1), 0.0, NEVER)
         leaving_o[...] = packed(state[...], spread_heads([jnp.exp(total[...] + through)], spread[...])[0][0:1])
@@ -513,29 +559,47 @@
         heads_o[0:8, :] += jnp.sum(dt_back.reshape(Q // 8, 8, 128), axis=0)
         heads_o[8:16, :] += jnp.sum((grad_run * part_deltas).reshape(Q // 8, 8, 128), axis=0)
 
-    masks = docs.tap_masks(first, tile)
-    for slab in range(width // 128):
-        lanes = slice(128 * slab, 128 * slab + 128)
-        pre_rows = pre[:, lanes].astype(F32)
-        sigma = sigmoid(pre_rows)
-        grad_pre = grads[:, lanes] * (sigma * (1.0 + pre_rows * (1.0 - sigma)))
-        source = xbc[:, lanes].astype(F32)
-        result = taps[3:4, lanes] * grad_pre
-        taps_o[24:32, lanes] += jnp.sum((grad_pre * source).reshape(tile // 8, 8, 128), axis=0)
-        taps_o[32:40, lanes] += jnp.sum(grad_pre.reshape(tile // 8, 8, 128), axis=0)
-        for back in range(1, 4):
-            ext[back - 1, 16 : 16 + tile, lanes] = grad_pre * masks[back - 1]
-            moved = ext[back - 1, 16 + back : 16 + back + tile, lanes]
-            result = result + taps[3 - back : 4 - back, lanes] * moved
-            taps_o[8 * (3 - back) : 8 * (4 - back), lanes] += jnp.sum((moved * source).reshape(tile // 8, 8, 128), axis=0)
-        high = result.astype(BF)
-        in_back_o[:, lanes] = high
-        if 128 * slab >= channels:
-            in_back_o[:, slice(256 + 128 * slab, 384 + 128 * slab)] = (result - high.astype(F32)).astype(BF)
-
-        @pl.when(step == 0)
-        def _():
-            tail_o[:, lanes] = result[tile - RIM :]
+    plain = docs.none_near(first, tile)
+
+    def convolve_back(masks):
+        for slab in range(width // 128):
+            lanes = slice(128 * slab, 128 * slab + 128)
+            pre_rows = pre[:, lanes].astype(F32)
+            sigma = sigmoid(pre_rows)
+            grad_pre = grads[:, lanes] * (sigma * (1.0 + pre_rows * (1.0 - sigma)))
+            source = xbc[:, lanes].astype(F32)
+            result = taps[3:4, lanes] * grad_pre
+            taps_o[24:32, lanes] += jnp.sum((grad_pre * source).reshape(tile // 8, 8, 128), axis=0)
+            taps_o[32:40, lanes] += jnp.sum(grad_pre.reshape(tile // 8, 8, 128), axis=0)
+            if masks is None:
+                longer = jnp.concatenate([grad_pre, ext[0, 16 + tile :, lanes]], axis=0)
+            for back in range(1, 4):
+                if masks is None:
+                    ext[back - 1, 16:24, lanes] = grad_pre[0:8]
+                    moved = pltpu.roll(longer, tile + 8 - back, 0)[:tile]
+                else:
+                    ext[back - 1, 16 : 16 + tile, lanes] = grad_pre * masks[back - 1]
+                    moved = ext[back - 1, 16 + back : 16 + back + tile, lanes]
+                result = result + taps[3 - back : 4 - back, lanes] * moved
+                taps_o[8 * (3 - back) : 8 * (4 - back), lanes] += jnp.sum(
+                    (moved * source).reshape(tile // 8, 8, 128), axis=0
+                )
+            high = result.astype(BF)
+            in_back_o[:, lanes] = high
+            if 128 * slab >= channels:
+                in_back_o[:, slice(256 + 128 * slab, 384 + 128 * slab)] = (result - high.astype(F32)).astype(BF)
+
+            @pl.when(step == 0)
+            def _():
+                tail_o[:, lanes] = result[tile - RIM :]
+
+    @pl.when(plain)
+    def _():
+        convolve_back(None)
+
+    @pl.when(jnp.logical_not(plain))
+    def _():
+        convolve_back(docs.tap_masks(first, tile))
 
     @pl.when(place == 0)
     def _():
@@ -659,7 +723,7 @@
     def whole(self, *arrays):
         for array in arrays:
             self.args.append(array)
-            self.in_specs.append(pl.BlockSpec(array.shape, lambda i, rank=array.ndim: (0,) * rank))
+            self.in_specs.append(pl.BlockSpec(array.shape, lambda i, *s, rank=array.ndim: (0,) * rank))
         return self
 
     def scalars(self, array):
@@ -675,7 +739,7 @@
 
     def out(self, shape, dtype, spec=None):
         self.outs.append(jax.ShapeDtypeStruct(shape, dtype))
-        self.out_specs.append(spec or pl.BlockSpec(shape, lambda i, rank=len(shape): (0,) * rank))
+        self.out_specs.append(spec or pl.BlockSpec(shape, lambda i, *s, rank=len(shape): (0,) * rank))
         return self
 
     def after(self, *arrays):
@@ -770,22 +834,56 @@
     return total
 
 
+def pair_sum(mine, other):
+    return (mine.astype(F32) + swap(other, "head", 1).astype(F32)).astype(BF)
+
+
 def head_pair(part):
     rows = part.shape[0] // 2
     side = lax.axis_index("head") % 2
     mine = lax.dynamic_slice_in_dim(part, side * rows, rows, 0)
-    other = lax.dynamic_slice_in_dim(part, (1 - side) * rows, rows, 0)
-    return (mine.astype(F32) + swap(other, "head", 1).astype(F32)).astype(BF)
+    return pair_sum(mine, lax.dynamic_slice_in_dim(part, (1 - side) * rows, rows, 0))
 
 
 def head_rest(low):
-    total = low.astype(F32)
     bit = 2
     while bit < lax.axis_size("head"):
-        low = total.astype(BF)
-        total = low.astype(F32) + swap(low, "head", bit).astype(F32)
+        low = (low.astype(F32) + swap(low, "head", bit).astype(F32)).astype(BF)
         bit *= 2
-    return total
+    return low
+
+
+class Reduction:
+    def __init__(self, value, axis):
+        self.value, self.axis, self.bits, self.out = value, axis, 1, True
+        self.count, self.me = lax.axis_size(axis), lax.axis_index(axis)
+        self.start()
+
+    def start(self):
+        if self.out:
+            rows, half = self.value.shape[0] // 2, self.me // self.bits % 2
+            sent = lax.dynamic_slice_in_dim(self.value, (1 - half) * rows, rows, 0)
+            self.value = lax.dynamic_slice_in_dim(self.value, half * rows, rows, 0)
+        else:
+            sent = self.value
+        self.other = swap(sent, self.axis, self.bits)
+
+    def done(self):
+        return not self.out and self.bits == 0
+
+    def step(self, after):
+        other, _ = lax.optimization_barrier((self.other, after))
+        if self.out:
+            self.value = (self.value.astype(F32) + other.astype(F32)).astype(BF)
+            self.out = self.bits * 2 < self.count
+            self.bits = self.bits * 2 if self.out else self.bits
+        else:
+            first = self.me // self.bits % 2 == 0
+            pieces = [jnp.where(first, self.value, other), jnp.where(first, other, self.value)]
+            self.value = jnp.concatenate(pieces, axis=0)
+            self.bits //= 2
+        if not self.done():
+            self.start()
 
 
 def pair_parts(value, axis):
@@ -823,6 +921,10 @@
     other = swap(half, axis, 1)
     first = lax.axis_index(axis) % 2 == 0
     return jnp.concatenate([jnp.where(first, half, other), jnp.where(first, other, half)], axis=0)
+
+
+def add_swaps(value, axis):
+    return sum_rows([value] + [swap(value, axis, bits) for bits in range(1, lax.axis_size(axis))])
 
 
 def all_sum(value, axis):
@@ -902,25 +1004,26 @@
         [jnp.where(doc_starts >= 1, doc_starts, 2**30), jnp.full((micro, 1), anchor)], axis=1
     ).astype(jnp.int32)
 
+    side = (lax.axis_index("head") % 2).astype(jnp.int32)[None]
     ahead = lambda i: i
     astern = lambda i: steps - 1 - i
 
     def rows_of(cols, turn, rows=tile):
-        return pl.BlockSpec((rows, cols), lambda i: (turn(i), 0))
+        return pl.BlockSpec((rows, cols), lambda i, *s: (turn(i), 0))
 
     def rows_in(m, cols, turn):
-        return pl.BlockSpec((None, tile, cols), lambda i: (m, turn(i), 0))
+        return pl.BlockSpec((None, tile, cols), lambda i, *s: (m, turn(i), 0))
 
     def chunks_of(turn, rows, cols):
-        return pl.BlockSpec((per, rows, cols), lambda i: (turn(i), 0, 0))
+        return pl.BlockSpec((per, rows, cols), lambda i, *s: (turn(i), 0, 0))
 
     def stat_spec(turn):
-        return pl.BlockSpec((8, tile), lambda i: (0, turn(i)))
+        return pl.BlockSpec((8, tile), lambda i, *s: (0, turn(i)))
 
     def project(m, *waits):
         call = Call(partial(first_kernel, tile, channels, m=m), steps, f"project_{m}")
         call.scalars(meta)
-        call.blocks((rim_tokens, pl.BlockSpec((None, RIM, model), lambda i: (m, 0, 0))))
+        call.blocks((rim_tokens, pl.BlockSpec((None, RIM, model), lambda i, *s: (m, 0, 0))))
         call.blocks((tokens, rows_in(m, model, ahead)))
         call.whole(weights, table, spread, wedge).after(*waits)
         call.out((length, model), BF, rows_of(model, ahead))
@@ -967,7 +1070,8 @@
 
     def norm(m, kept, mixed, stats, chain, *waits):
         normed, gate, xbc, pre, conv, deltas = kept[:6]
-        call = Call(partial(third_kernel, tile, channels, float(full), bool(chain), m=m), steps, f"gate_{m}")
+        final = m + 1 == micro
+        call = Call(partial(third_kernel, tile, channels, float(full), bool(chain), final, m=m), steps, f"gate_{m}")
         call.scalars(meta)
         call.blocks(
             (mixed, rows_of(channels, astern)),
@@ -980,17 +1084,29 @@
         call.whole(out_weight, table, spread, wedge)
         call.blocks(*[(part, stat_spec(astern)) for part in stats])
         call.whole(*chain).after(*waits)
-        call.out((length, model), BF, rows_of(model, astern))
+        half = steps // 2
+
+        def spot(flip):
+            return pl.BlockSpec(
+                (tile, model),
+                lambda i, s: (jnp.clip(astern(i) - (s[0] if flip == 0 else 1 - s[0]) * half, 0, half - 1), 0),
+            )
+
+        call.out((length // 2, model), BF, spot(0)).out((length // 2, model), BF, spot(1))
         call.out((length, channels), BF, rows_of(channels, astern))
         call.out((length, channels), BF, rows_of(channels, astern))
         call.out((blocks, 128, channels), F32, chunks_of(astern, 128, channels))
         call.out((blocks, 8, 128), F32, chunks_of(astern, 8, 128))
         call.out((STATES + 16, channels), BF)
-        call.out((channels, model), F32)
-        call.out((model, channels), F32)
+        if final:
+            call.out((2 * model, channels), BF)
+        else:
+            call.out((channels, model), F32)
+            call.out((model, channels), F32)
         call.out((16, channels), F32)
+        call.temp((channels, model), F32).temp((model, channels), F32)
         call.temp((128, channels), F32).temp((8, 128), F32)
-        return call.run(19)
+        return call.run(17, side)
 
     def within(m, kept, ssd_back, parts, *waits):
         conv, deltas = kept[4:6]
@@ -1011,14 +1127,14 @@
         call.whole(edge)
         call.blocks(
             (deltas, rows_of(128, astern)),
-            (third[2], rows_of(channels, astern)),
+            (third[3], rows_of(channels, astern)),
             (inner[0], rows_of(width, astern)),
             (inner[1], rows_of(128, astern)),
             (held, chunks_of(astern, 128, channels)),
             (sums, chunks_of(astern, 8, 128)),
         )
         call.whole(carry)
-        call.blocks((third[3], chunks_of(astern, 128, channels)), (third[4], chunks_of(astern, 8, 128)))
+        call.blocks((third[4], chunks_of(astern, 128, channels)), (third[5], chunks_of(astern, 8, 128)))
         call.whole(table, spread, gather, wedge, wedge_up, wedge_below, *parts, *chain).after(*waits)
         call.out((length, width + 256), BF, rows_of(width + 256, astern))
         call.out((length, 128), BF, rows_of(128, astern))
@@ -1063,11 +1179,7 @@
         call.temp((tile, width + 256), BF).temp((model, width), F32).temp((128, model), F32)
         return call.run(8)
 
-    side = (lax.axis_index("head") % 2).astype(jnp.int32)[None]
-
-    def place(m, begin, totals, token, earlier, *waits):
-        low = totals.astype(BF)
-        other = swap(low, "head", 1)
+    def place(m, begin, low, other, token, earlier, *waits):
         big = min(512, low.shape[0])
         half = low.shape[0] // big
         call = Call(partial(place_kernel, token), 2 * half, f"place_{m}_{begin}_{token:d}")
@@ -1103,76 +1215,55 @@
     for m in every:
         stats = [mixes[m][1]] + [swap(mixes[m][1], "head", bits) for bits in range(1, lax.axis_size("head"))]
         thirds.append(norm(m, kept[m], mixes[m][0], stats, chain, *order_by))
-        chain = thirds[m][6:9]
-        order_by = [thirds[m][5]]
-    grad_out, grad_gate, gate_rows = chain
-    grad_out, grad_gate = lax.psum((grad_out, grad_gate), "seq")
-    mixed_pair = [head_pair(thirds[m][0]) for m in every]
+        chain = thirds[m][7:]
+        order_by = [thirds[m][6]]
+    packed_grads, gate_rows = chain
+    reduction = Reduction(packed_grads, "seq")
+    mixed_pair = [pair_sum(thirds[m][0], thirds[m][1]) for m in every]
     mixed_all = [head_rest(mixed_pair[m]) for m in every]
     inner_b, fourths, chain = [], [], ()
     for m in every:
-        inner_b.append(within(m, kept[m], thirds[m][2], near_parts(thirds[m][5], "seq", -1), *order_by))
-        order_by = [inner_b[m][2], mixed_pair[m]]
+        near = near_parts(thirds[m][6], "seq", -1)
+        inner_b.append(within(m, kept[m], thirds[m][3], near, mixed_pair[m], *order_by))
+        order_by = [inner_b[m][2]]
+        reduction.step(inner_b[m][2])
     far = [far_parts(inner_b[m][2], inner_b[m][3], "seq", -1) for m in every]
+    order_by.append(mixed_all[0])
+    mixed_other = [swap(mixed_all[m], "head", 1) for m in every]
+    token_other = []
     gain_rows, grads, token_all, half_steps = (), (), [], steps // 2
     for m in every:
         final = m + 1 == micro
         fourths.append(across(m, kept[m], mixes[m][2], thirds[m], inner_b[m], far[m], chain, *order_by))
         chain = fourths[m][4:6]
+        if not reduction.done():
+            reduction.step(fourths[m][4])
         rim = from_behind(fourths[m][2], "seq", -1)
-        gate_back = thirds[m][1]
+        gate_back = thirds[m][2]
         if not final:
             both = (0, steps)
-            first = part_of(m, gate_back, fourths[m], (0, half_steps), both, None, gain_rows, None, 6, mixed_all[m], *far[m + 1])
+            first = part_of(m, gate_back, fourths[m], (0, half_steps), both, None, gain_rows, None, 6, mixed_all[m + 1], *far[m + 1])
             second = part_of(m, gate_back, fourths[m], (half_steps, steps), both, rim, first[1:], first[0], 6)
             grads = weight_back(m, kept[m], fourths[m], rim, grads, F32, second[1])
+            reduction.step(second[1])
+            reduction.step(grads[1])
             pair = head_pair(second[0])
             token_all.append(head_rest(pair))
+            token_other.append(swap(token_all[m], "head", 1))
             gain_rows = second[1:]
-            order_by = [pair, grads[1], mixed_all[m + 1]]
+            order_by = [pair, grads[1]]
         else:
-            first = part_of(m, gate_back, fourths[m], (0, half_steps), (0, half_steps), None, gain_rows, None, 6, token_all[-1])
-            grads = weight_back(m, kept[m], fourths[m], rim, grads, BF, first[1])
+            first = part_of(m, gate_back, fourths[m], (0, half_steps), (0, half_steps), None, gain_rows, None, 6, token_all[-1], *mixed_other)
             pair = head_pair(first[0])
             second = part_of(
-                m, gate_back, fourths[m], (half_steps, steps), (half_steps, half_steps), rim, first[1:], None, 6,
-                pair, grads[1],
+                m, gate_back, fourths[m], (half_steps, steps), (half_steps, half_steps), rim, first[1:], None, 6
             )
+            grads = weight_back(m, kept[m], fourths[m], rim, grads, BF, second[1], pair, *token_other)
             gain_rows = second[1:]
             last_pair = [pair, head_pair(second[0])]
     tap_rows, head_rows = chain
     grads, dt_rows = grads
     gain_rows = gain_rows[0]
-    halved = pair_parts(grads, "seq")
-    last_all = [head_rest(last_pair[0])]
-    halved, last_pair, dt_rows = lax.optimization_barrier((halved, last_pair, dt_rows))
-    last_all.append(head_rest(last_pair[1]))
-    halved = sum_rows(halved).astype(BF)
-    pieces = scatter_parts(halved, "seq")
-    mixed_out = token_grad = None
-    for m in every:
-        mixed_out = place(m, 0, mixed_all[m], False, mixed_out, halved, last_all[0], grad_out, grad_gate)
-    pieces, mixed_out = lax.optimization_barrier((pieces, mixed_out))
-    part = sum_rows(pieces)
-    share = 2 * states // lax.axis_size("head")
-    bc_parts = [part[:, channels:width]]
-    bc_parts += [swap(bc_parts[0], "head", bits) for bits in range(1, lax.axis_size("head"))]
-    for m in range(micro - 1):
-        token_grad = place(m, 0, token_all[m], True, token_grad, part, last_all[1])
-    bc_parts, token_grad = lax.optimization_barrier((bc_parts, token_grad))
-    bc_mine = lax.dynamic_slice_in_dim(sum_rows(bc_parts), lax.axis_index("head") * share, share, 1)
-    gathered = gather_half(
-        jnp.concatenate(
-            [part[:, :channels], bc_mine, jnp.zeros((part.shape[0], -share % 128), F32)], axis=1
-        ).astype(BF),
-        "seq",
-    )
-    gathered = gather_pair(gathered, "seq")
-    grad_x = gathered[:, :channels].astype(F32)
-    grad_bc = gathered[:, channels : channels + share].astype(F32)
-
-    token_grad = place(micro - 1, 0, last_all[0], True, token_grad)
-    token_grad = place(micro - 1, length // 2, last_all[1], True, token_grad)
 
     def folded(rows):
         return jnp.sum(rows.reshape(-1, 8, rows.shape[1]), axis=1)
@@ -1181,26 +1272,64 @@
     by_row = folded(gate_rows)
     by_head = folded(head_rows)[:, :heads]
     skip_sum = jnp.sum(by_row[1].reshape(heads, dim), axis=1)
-    gain_sum = jnp.sum(gain_rows, axis=0)
     small = jnp.concatenate(
-        [by_tap[:, channels:].reshape(-1), gain_sum,
-         dt_rows[:heads].reshape(-1), by_tap[:, :channels].reshape(-1), by_row[0], by_head.reshape(-1), skip_sum]
+        [by_tap[:, channels:].reshape(-1), jnp.sum(gain_rows, axis=0), dt_rows[:heads].reshape(-1),
+         by_tap[:, :channels].reshape(-1), by_row[0], by_head.reshape(-1), skip_sum]
     )
+    small = jnp.pad(small, (0, -small.size % 1024)).reshape(-1, 128)
     shared_size = by_tap[:, channels:].size + model
-    small = jnp.pad(small, (0, -small.size % 1024)).reshape(-1, 128)
-    small = all_sum(small, "seq")
-    shared_rows = shared_size // 128
-    shared = all_sum(small[:shared_rows], "head").reshape(-1)
-    rest = small[shared_rows:].reshape(-1)
+    halved = pair_parts(grads, "seq")
+    last_all = [head_rest(last_pair[0])]
+    halved, last_pair = lax.optimization_barrier((halved, last_pair))
+    last_all.append(head_rest(last_pair[1]))
+    halved = sum_rows(halved).astype(BF)
+    pieces = scatter_parts(halved, "seq")
+    small = all_sum(lax.optimization_barrier((small, halved))[0], "seq")
+    mixed_out = place(0, 0, mixed_all[0], mixed_other[0], False, None, halved, last_all[0])
+    pieces, mixed_out = lax.optimization_barrier((pieces, mixed_out))
+    part = sum_rows(pieces)
+    while not reduction.done():
+        reduction.step(part)
+    packed_grads = reduction.value
+    share = 2 * states // lax.axis_size("head")
+    bc_parts = [part[:, channels:width]]
+    bc_parts += [swap(bc_parts[0], "head", bits) for bits in range(1, lax.axis_size("head"))]
+    for m in range(1, micro):
+        mixed_out = place(m, 0, mixed_all[m], mixed_other[m], False, mixed_out, part, last_all[1])
+    bc_parts, mixed_out = lax.optimization_barrier((bc_parts, mixed_out))
+    bc_mine = lax.dynamic_slice_in_dim(sum_rows(bc_parts), lax.axis_index("head") * share, share, 1)
+    payload = jnp.concatenate(
+        [part[:, :channels], bc_mine, jnp.zeros((part.shape[0], -share % 128), F32)], axis=1
+    ).astype(BF)
+    gathered = gather_half(payload, "seq")
+    token_grad = None
+    for m in range(micro - 1):
+        token_grad = place(m, 0, token_all[m], token_other[m], True, token_grad, payload)
+    gathered, token_grad = lax.optimization_barrier((gathered, token_grad))
+    gathered = gather_pair(gathered, "seq")
+    grad_x = gathered[:, :channels].astype(F32)
+    grad_bc = gathered[:, channels : channels + share].astype(F32)
+
+    token_grad = place(micro - 1, 0, last_all[0], swap(last_all[0], "head", 1), True, token_grad)
+    last_other = swap(last_all[1], "head", 1)
+    token_grad = place(micro - 1, length // 2, last_all[1], last_other, True, token_grad)
+
     tap_count = conv_x_weight.shape[0]
+    shared, _ = lax.optimization_barrier((small[: shared_size // 128], payload))
+    shared = add_swaps(shared, "head").reshape(-1)
+    rest = small[shared_size // 128 :].reshape(-1)
     bc_taps = shared[: (tap_count + 1) * 2 * states].reshape(tap_count + 1, 2 * states)
-    grad_norm_gain = shared[(tap_count + 1) * 2 * states : shared_size]
+    grad_norm_gain = shared[(tap_count + 1) * 2 * states :]
     grad_dt = rest[: heads * model].reshape(heads, model).T
     rest = rest[heads * model :]
     cut = (tap_count + 1) * channels
     x_taps = rest[:cut].reshape(tap_count + 1, channels)
     grad_gate_gain = rest[cut : cut + channels]
     tails = rest[cut + channels : cut + channels + 3 * heads].reshape(3, heads)
+    grad_gate = packed_grads[:model].astype(F32)
+    grad_out = jnp.concatenate(
+        [packed_grads[row : row + channels] for row in range(model, 2 * model, channels)], axis=1
+    ).astype(F32)
     return (
         mixed_out,
         token_grad,

time: 477 us -> 450 us (0.943)
  Pallas kernels: 250 us -> 235 us
  between operations: 15.9 us -> 2.72 us
  starting transfers between devices: 86.4 us -> 99.2 us
  waiting for transfers between devices: 48 us -> 43 us
    pallas_call x23, Pallas kernels: 250 us -> 235 us  [run(): pl.pallas_call(self.kernel, grid_spec=pltpu.PrefetchScalarGridSpec(num_sc...]
    ppermute x37 -> x44, starting transfers between devices: 40.6 us -> 52.8 us  [swap(): return lax.ppermute(value, axis, [(i, i ^ bits) for i in range(count)])]
    ppermute x37 -> x44, waiting for transfers between devices: 47.9 us -> 42.9 us  [swap(): return lax.ppermute(value, axis, [(i, i ^ bits) for i in range(count)])]
    convert_element_type x9 -> x14, other arithmetic: 23.7 us -> 21.6 us  [the longest x5 10.5 us: pair_sum(): return (mine.astype(F32) + swap(other, 'head', 1).astype(F32)).astype(BF)]
    unnamed x138 -> x165, local copies, waits for them, and re-layouts: 15 us -> 14.8 us
  transfers between devices with their start and end apart: 61 -> 67, of which waited for: 7 -> 10; matrix products, arithmetic and copies ran while one was open for 12% -> 12% of each run, Pallas kernels for 48% -> 49%
where the time goes in v3:
time: 450 us; the launch traced here: 442 us
  Pallas kernels  235 us (52%)
  starting transfers between devices  99.2 us (22%)
  waiting for transfers between devices  43 us (10%)
  other arithmetic  32.1 us (7%)
  local copies, waits for them, and re-layouts  30.4 us (7%)
    pallas_call x23, Pallas kernels, run(): pl.pallas_call(self.kernel, grid_spec=pltpu.PrefetchScalarGridSpec(num_sc...  235 us
    ppermute x44, starting transfers between devices, swap(): return lax.ppermute(value, axis, [(i, i ^ bits) for i in range(count)])  52.8 us
    ppermute x23, starting transfers between devices, from_behind(): return lax.ppermute(value, axis, [(i, i + steps) for i in sources])  46.3 us
    ppermute x44, waiting for transfers between devices, swap(): return lax.ppermute(value, axis, [(i, i ^ bits) for i in range(count)])  42.9 us
    unnamed x165, local copies, waits for them, and re-layouts  14.8 us
    convert_element_type x5, other arithmetic, pair_sum(): return (mine.astype(F32) + swap(other, 'head', 1).astype(F32)).astype(BF)  10.5 us
    convert_element_type x5, other arithmetic, head_rest(): low = (low.astype(F32) + swap(low, 'head', bit).astype(F32)).astype(BF)  9.74 us
  transfers between devices with their start and end apart: 67, of which 10 were waited for; matrix products, arithmetic and copies ran while one was open for 12% of the time, Pallas kernels for 49%

profile of v3, /device:TPU:0, one launch (start us, length us, event | category | flops | bytes accessed | tf_op | source)
XLA Modules:
  0.0 441.9 jit_solution(17785113533795632711)
XLA Ops:
  1.5 4.9 %collective-permute-start = (bf16[2,16,768]{2,1,0:T(8,128)(2,1)S(1)}, bf16[2,16,768]{2,1,0:T(8,128)(2,1)S(1)}, u32[]{:S(2)}, u32[]{:S(2)}) collective-permute-start(bf16[2,16,768]{2,1,0:T(8,128)(2,1)S(1)} %slice.120), channel_id=1, source_target_pairs={{0,4},{4,8},{8,12},{12,16},{16,20},{20,24},{24,28},{1,5},{5,9},{9,... | collective-permute-start | bytes 147464 | tf_op jit(solution)/shard_map/ppermute | solution.py:788
  7.7 3.7 fusion.7
  14.2 16.5 %project_0.1 = (bf16[2048,768]{1,0:T(8,128)(2,1)}, f32[2048,384]{1,0:T(8,128)}, bf16[2048,640]{1,0:T(8,128)(2,1)}, bf16[2048,640]{1,0:T(8,128)(2,1)}, bf16[2048,...) custom-call(s32[2,9]{1,0:T(2,128)S(1)} %concatenate.37.meta, ...), custom_call_target="tpu_custom_call" | custom-call | flops 25300000768 | tf_op jit(solution)/shard_map/project_0/pallas_call | solution.py:761
  31.3 4.4 %collective-permute-start.4 = (bf16[144,384]{1,0:T(8,128)(2,1)S(1)}, bf16[144,384]{1,0:T(8,128)(2,1)S(1)}, u32[]{:S(2)}, u32[]{:S(2)}) collective-permute-start(bf16[144,384]{1,0:T(8,128)(2,1)S(1)} %get-tuple-element.121.rest_0_), channel_id=1, source_target_pairs={{0,4},{4,8},{8,12},{12,16},{16,20},{20,24},{24,28},{1,5},{5,9},{9,... | collective-permute-start | bytes 331784 | tf_op jit(solution)/shard_map/ppermute | solution.py:788
  35.8 2.7 collective-permute-start.5
  38.5 6.2 %collective-permute-start.6 = (bf16[144,384]{1,0:T(8,128)(2,1)S(1)}, bf16[144,384]{1,0:T(8,128)(2,1)S(1)}, u32[]{:S(2)}, u32[]{:S(2)}) collective-permute-start(bf16[144,384]{1,0:T(8,128)(2,1)S(1)} %get-tuple-element.121.rest_0_), channel_id=1, source_target_pairs={{0,12},{4,16},{8,20},{12,24},{16,28},{1,13},{5,17},{9,21},{13,25},... | collective-permute-start | bytes 331784 | tf_op jit(solution)/shard_map/ppermute | solution.py:788
  44.7 16.5 %project_1.1 = (bf16[2048,768]{1,0:T(8,128)(2,1)}, f32[2048,384]{1,0:T(8,128)}, bf16[2048,640]{1,0:T(8,128)(2,1)}, bf16[2048,640]{1,0:T(8,128)(2,1)}, bf16[2048,...) custom-call(s32[2,9]{1,0:T(2,128)S(1)} %concatenate.37.meta, ...), custom_call_target="tpu_custom_call" | custom-call | flops 25300000768 | tf_op jit(solution)/shard_map/project_1/pallas_call | solution.py:761
  63.1 2.5 collective-permute-start.2
  67.0 6.1 %inside_0.1 = (f32[2048,384]{1,0:T(8,128)}, f32[136,384]{1,0:T(8,128)S(1)}, bf16[144,384]{1,0:T(8,128)(2,1)S(1)}) custom-call(s32[2,9]{1,0:T(2,128)S(1)} %concatenate.37.meta, bf16[2048,640]{1,0:T(8,128)(2,1)S(1)} %copy-done.26, f32[2048,128]{1,0:T(8,128)S(1)} %get-tuple-element.130.deltas, f32[16,768]{1,0:T(8,128)S(1)} %concatenate.42.table.rest_1_, ...), custom_call_target="tpu_custom_call" | custom-call | flops 12650000384 | tf_op jit(solution)/shard_map/inside_0/pallas_call | solution.py:761
  75.8 6.0 %inside_1.1 = (f32[2048,384]{1,0:T(8,128)}, f32[136,384]{1,0:T(8,128)S(1)}, bf16[144,384]{1,0:T(8,128)(2,1)S(1)}) custom-call(s32[2,9]{1,0:T(2,128)S(1)} %concatenate.37.meta, bf16[2048,640]{1,0:T(8,128)(2,1)S(1)} %copy-done.27, f32[2048,128]{1,0:T(8,128)S(1)} %get-tuple-element.127.deltas, f32[16,768]{1,0:T(8,128)S(1)} %concatenate.42.table.rest_1_, ...), custom_call_target="tpu_custom_call" | custom-call | flops 12650000384 | tf_op jit(solution)/shard_map/inside_1/pallas_call | solution.py:761
  85.5 9.6 %mix_0.1 = (f32[2048,384]{1,0:T(8,128)}, f32[8,2048]{1,0:T(8,128)S(1)}, f32[128,384]{1,0:T(8,128)S(1)}) custom-call(s32[2,9]{1,0:T(2,128)S(1)} %concatenate.37.meta, f32[2048,384]{1,0:T(8,128)} %get-tuple-element.138.inside, bf16[2048,640]{1,0:T(8,128)(2,1)S(1)} %copy-done.26, f32[2048,128]{1,0:T(8,128)S(1)} %get-tuple-element.130.deltas, ...), custom_call_target="tpu_custom_call" | custom-call | flops 13799999488 | tf_op jit(solution)/shard_map/mix_0/pallas_call | solution.py:761
  96.9 9.6 %mix_1.1 = (f32[2048,384]{1,0:T(8,128)}, f32[8,2048]{1,0:T(8,128)S(1)}, f32[128,384]{1,0:T(8,128)S(1)}) custom-call(s32[2,9]{1,0:T(2,128)S(1)} %concatenate.37.meta, f32[2048,384]{1,0:T(8,128)} %get-tuple-element.132.inside, bf16[2048,640]{1,0:T(8,128)(2,1)S(1)} %copy-done.27, f32[2048,128]{1,0:T(8,128)S(1)} %get-tuple-element.127.deltas, ...), custom_call_target="tpu_custom_call" | custom-call | flops 13799999488 | tf_op jit(solution)/shard_map/mix_1/pallas_call | solution.py:761
  108.5 18.7 %gate_0.1 = (bf16[1024,768]{1,0:T(8,128)(2,1)}, bf16[1024,768]{1,0:T(8,128)(2,1)}, bf16[2048,384]{1,0:T(8,128)(2,1)}, bf16[2048,384]{1,0:T(8,128)(2,1)}, f32[16,...) custom-call(s32[1]{0:T(128)} %bitcast.4.side, ...), custom_call_target="tpu_custom_call" | custom-call | flops 19549999104 | tf_op jit(solution)/shard_map/gate_0/pallas_call | solution.py:761
  131.8 18.5 %gate_1.1 = (bf16[1024,768]{1,0:T(8,128)(2,1)}, bf16[1024,768]{1,0:T(8,128)(2,1)}, bf16[2048,384]{1,0:T(8,128)(2,1)}, bf16[2048,384]{1,0:T(8,128)(2,1)}, f32[16,...) custom-call(s32[1]{0:T(128)} %bitcast.4.side, ...), custom_call_target="tpu_custom_call" | custom-call | flops 19549999104 | tf_op jit(solution)/shard_map/gate_1/pallas_call | solution.py:761
  155.0 2.4 add_convert_fusion.4.rest_3_
  158.9 3.1 collective-permute-start.60
  162.0 13.4 %within_0.1 = (f32[2048,640]{1,0:T(8,128)}, f32[2048,128]{1,0:T(8,128)S(1)}, f32[136,384]{1,0:T(8,128)S(1)}, bf16[144,384]{1,0:T(8,128)(2,1)S(1)}) custom-call(s32[2,9]{1,0:T(2,128)S(1)} %concatenate.37.meta, bf16[2048,640]{1,0:T(8,128)(2,1)} %get-tuple-element.129.conv, f32[2048,128]{1,0:T(8,128)S(1)} %copy-done.29, bf16[2048,384]{1,0:T(8,128)(2,1)S(1)} %copy-done.36, ...), custom_call_target="tpu_custom_call" | custom-call | flops 16099999744 | tf_op jit(solution)/shard_map/within_0/pallas_call | solution.py:761
  175.4 2.6 collective-permute-done.60
  184.4 4.0 collective-permute-start.61
  188.9 13.4 %within_1.1 = (f32[2048,640]{1,0:T(8,128)}, f32[2048,128]{1,0:T(8,128)S(1)}, f32[136,384]{1,0:T(8,128)S(1)}, bf16[144,384]{1,0:T(8,128)(2,1)S(1)}) custom-call(s32[2,9]{1,0:T(2,128)S(1)} %concatenate.37.meta, bf16[2048,640]{1,0:T(8,128)(2,1)} %get-tuple-element.123.conv, f32[2048,128]{1,0:T(8,128)S(1)} %copy-done.32, bf16[2048,384]{1,0:T(8,128)(2,1)S(1)} %copy-done.34, ...), custom_call_target="tpu_custom_call" | custom-call | flops 16099999744 | tf_op jit(solution)/shard_map/within_1/pallas_call | solution.py:761
  203.8 11.6 %collective-permute-done.29 = bf16[1024,768]{1,0:T(8,128)(2,1)} collective-permute-done((bf16[1024,768]{1,0:T(8,128)(2,1)S(1)}, bf16[1024,768]{1,0:T(8,128)(2,1)}, u32[]{:S(2)}, u32[]{:S(2)}) %collective-permute-start.29) | collective-permute-done | bytes 1572896 | tf_op jit(solution)/shard_map/ppermute | solution.py:782
  218.5 6.3 %collective-permute-start.62 = (bf16[192,384]{1,0:T(8,128)(2,1)S(1)}, bf16[192,384]{1,0:T(8,128)(2,1)S(1)}, u32[]{:S(2)}, u32[]{:S(2)}) collective-permute-start(bf16[192,384]{1,0:T(8,128)(2,1)S(1)} %constant_dynamic-slice_fusion), channel_id=1, source_target_pairs={{0,16},{4,20},{8,24},{12,28},{16,0},{20,4},{24,8},{28,12},{1,17},{... | collective-permute-start | bytes 442376 | tf_op jit(solution)/shard_map/ppermute | solution.py:782
  225.0 23.8 %across_0.1 = (bf16[2048,896]{1,0:T(8,128)(2,1)}, bf16[2048,128]{1,0:T(8,128)(2,1)S(1)}, f32[16,640]{1,0:T(8,128)S(1)}, f32[16,640]{1,0:T(8,128)S(1)}, f32[40,640]{1,0:T(8,128)S(1)}, /*index=5*/f32[16,128]{1,0:T(8,128)S(1)}) custom-call(s32[2,9]{1,0:T(2,128)S(1)} %concatenate.37.meta, bf16[2048,640]{1,0:T(8,128)(2,1)} %get-tuple-element.129.conv, ...), custom_call_target="tpu_custom_call" | custom-call | flops 36800000000 | tf_op jit(solution)/shard_map/across_0/pallas_call | solution.py:761
  248.8 3.3 collective-permute-start.63
  255.9 6.1 %input_0_0.1 = (bf16[2048,768]{1,0:T(8,128)(2,1)}, f32[8,768]{1,0:T(8,128)S(1)}) custom-call(bf16[2,2048,768]{2,1,0:T(8,128)(2,1)} %tokens.21, bf16[2048,384]{1,0:T(8,128)(2,1)S(1)} %copy-done.20, bf16[2048,896]{1,0:T(8,128)(2,1)} %get-tuple-element.179.in_back, bf16[2048,128]{1,0:T(8,128)(2,1)S(1)} %get-tuple-element.180.dt_back, ...), custom_call_target="tpu_custom_call" | custom-call | flops 6899999744 | tf_op jit(solution)/shard_map/input_0_0/pallas_call | solution.py:761
  261.9 5.5 %input_0_2.1 = (bf16[2048,768]{1,0:T(8,128)(2,1)}, f32[8,768]{1,0:T(8,128)S(1)}) custom-call(bf16[2,2048,768]{2,1,0:T(8,128)(2,1)} %tokens.21, bf16[2048,384]{1,0:T(8,128)(2,1)S(1)} %copy-done.20, bf16[2048,896]{1,0:T(8,128)(2,1)} %get-tuple-element.179.in_back, bf16[2048,128]{1,0:T(8,128)(2,1)S(1)} %get-tuple-element.180.dt_back, ...), custom_call_target="tpu_custom_call", output_to_operand_aliasing={{0}: (8, {})} | custom-call | flops 6899999744 | tf_op jit(solution)/shard_map/input_0_2/pallas_call | solution.py:761
  269.7 2.5 collective-permute-start.64
  272.2 6.8 %weigh_0.1 = (f32[768,640]{1,0:T(8,128)S(1)}, f32[8,768]{1,0:T(8,128)S(1)}) custom-call(bf16[2048,768]{1,0:T(8,128)(2,1)S(1)} %copy-done.23, bf16[2048,896]{1,0:T(8,128)(2,1)} %get-tuple-element.179.in_back, bf16[2048,128]{1,0:T(8,128)(2,1)S(1)} %get-tuple-element.180.dt_back, f32[16,640]{1,0:T(8,128)S(1)} %get-tuple-element.181.rest_0_.tail, ...), custom_call_target="tpu_custom_call" | custom-call | flops 9200000000 | tf_op jit(solution)/shard_map/weigh_0/pallas_call | solution.py:761
  283.8 2.3 add_convert_fusion.1.rest_5_
  287.7 23.7 %across_1.1 = (bf16[2048,896]{1,0:T(8,128)(2,1)}, bf16[2048,128]{1,0:T(8,128)(2,1)S(1)}, f32[16,640]{1,0:T(8,128)S(1)}, f32[16,640]{1,0:T(8,128)S(1)}, f32[40,640]{1,0:T(8,128)S(1)}, /*index=5*/f32[16,128]{1,0:T(8,128)S(1)}) custom-call(s32[2,9]{1,0:T(2,128)S(1)} %concatenate.37.meta, bf16[2048,640]{1,0:T(8,128)(2,1)} %get-tuple-element.123.conv, ...), custom_call_target="tpu_custom_call" | custom-call | flops 36800000000 | tf_op jit(solution)/shard_map/across_1/pallas_call | solution.py:761
  315.8 5.8 %collective-permute-done.34 = bf16[1024,768]{1,0:T(8,128)(2,1)} collective-permute-done((bf16[1024,768]{1,0:T(8,128)(2,1)S(1)}, bf16[1024,768]{1,0:T(8,128)(2,1)}, u32[]{:S(2)}, u32[]{:S(2)}) %collective-permute-start.34) | collective-permute-done | bytes 1572896 | tf_op jit(solution)/shard_map/ppermute | solution.py:782
  321.6 3.0 add_convert_fusion.rest_1_.mine
  326.3 5.2 %input_1_0.1 = (bf16[1024,768]{1,0:T(8,128)(2,1)S(1)}, f32[8,768]{1,0:T(8,128)S(1)}) custom-call(bf16[2,2048,768]{2,1,0:T(8,128)(2,1)} %tokens.21, bf16[2048,384]{1,0:T(8,128)(2,1)S(1)} %copy-done.18, bf16[2048,896]{1,0:T(8,128)(2,1)} %get-tuple-element.188.in_back, bf16[2048,128]{1,0:T(8,128)(2,1)S(1)} %get-tuple-element.189.dt_back, ...), custom_call_target="tpu_custom_call" | custom-call | flops 6899999744 | tf_op jit(solution)/shard_map/input_1_0/pallas_call | solution.py:761
  337.3 4.7 %input_1_2.1 = (bf16[1024,768]{1,0:T(8,128)(2,1)S(1)}, f32[8,768]{1,0:T(8,128)S(1)}) custom-call(bf16[2,2048,768]{2,1,0:T(8,128)(2,1)} %tokens.21, bf16[2048,384]{1,0:T(8,128)(2,1)S(1)} %copy-done.19, bf16[2048,896]{1,0:T(8,128)(2,1)} %get-tuple-element.188.in_back, bf16[2048,128]{1,0:T(8,128)(2,1)S(1)} %get-tuple-element.189.dt_back, ...), custom_call_target="tpu_custom_call" | custom-call | flops 6899999744 | tf_op jit(solution)/shard_map/input_1_2/pallas_call | solution.py:761
  347.2 7.1 %weigh_1.1 = (bf16[768,640]{1,0:T(8,128)(2,1)S(1)}, f32[8,768]{1,0:T(8,128)S(1)}) custom-call(bf16[2048,768]{1,0:T(8,128)(2,1)} %get-tuple-element.122.normed, bf16[2048,896]{1,0:T(8,128)(2,1)} %get-tuple-element.188.in_back, bf16[2048,128]{1,0:T(8,128)(2,1)S(1)} %copy-done.22, f32[16,640]{1,0:T(8,128)S(1)} %get-tuple-element.190.rest_0_.tail, ...), custom_call_target="tpu_custom_call" | custom-call | flops 9200000000 | tf_op jit(solution)/shard_map/weigh_1/pallas_call | solution.py:761
  356.7 2.4 add_convert_fusion.8
  359.3 9.0 %collective-permute-done.39 = bf16[384,640]{1,0:T(8,128)(2,1)} collective-permute-done((bf16[384,640]{1,0:T(8,128)(2,1)}, bf16[384,640]{1,0:T(8,128)(2,1)}, u32[]{:S(2)}, u32[]{:S(2)}) %collective-permute-start.39) | collective-permute-done | bytes 491552 | tf_op jit(solution)/shard_map/ppermute | solution.py:782
  375.7 2.6 collective-permute-start.42
  380.4 4.4 %place_0_0_0.1.rest_0_ = bf16[2,2048,768]{2,1,0:T(8,128)(2,1)} custom-call(s32[1]{0:T(128)} %bitcast.4.side, bf16[1024,768]{1,0:T(8,128)(2,1)S(1)} %copy-done.6, bf16[1024,768]{1,0:T(8,128)(2,1)S(1)} %copy-done.11, bf16[2,2048,768]{2,1,0:T(8,128)(2,1)} %tokens.21, bf16[384,640]{1,0:T(8,128)(2,1)S(1)} %add_convert_fusion.11.rest_0_, ...), custom_call_target="tpu_custom_call" | custom-call | flops 4600000000 | tf_op jit(solution)/shard_map/place_0_0_0/pallas_call | solution.py:761
  385.7 2.6 collective-permute-start.43
  396.0 4.5 %place_1_0_0.1 = bf16[2,2048,768]{2,1,0:T(8,128)(2,1)} custom-call(s32[1]{0:T(128)} %bitcast.4.side, bf16[1024,768]{1,0:T(8,128)(2,1)S(1)} %add_convert_fusion.2.rest_0_.mine, bf16[1024,768]{1,0:T(8,128)(2,1)S(1)} %copy-done.1, bf16[2,2048,768]{2,1,0:T(8,128)(2,1)} %tokens.21, ...), custom_call_target="tpu_custom_call", output_to_operand_aliasing={{}: (4, {})} | custom-call | flops 4600000000 | tf_op jit(solution)/shard_map/place_1_0_0/pallas_call | solution.py:761
  403.0 6.9 %place_0_0_1.1.rest_2_ = bf16[2,2048,768]{2,1,0:T(8,128)(2,1)} custom-call(s32[1]{0:T(128)} %bitcast.4.side, bf16[1024,768]{1,0:T(8,128)(2,1)} %add_convert_fusion.rest_1_.mine, bf16[1024,768]{1,0:T(8,128)(2,1)} %collective-permute-done.38.rest_4_.other, bf16[2,2048,768]{2,1,0:T(8,128)(2,1)} %tokens.21, bf16[2,2048,768]{2,1,0:T(8,128)(2,1)} %rest_0_.5, ...), custom_call_target="tpu_custom_call" | custom-call | flops 4600000000 | tf_op jit(solution)/shard_map/place_0_0_1/pallas_call | solution.py:761
  409.9 2.7 collective-permute-start.52
  415.7 4.9 %collective-permute-done.52 = bf16[96,512]{1,0:T(8,128)(2,1)S(1)} collective-permute-done((bf16[96,512]{1,0:T(8,128)(2,1)S(1)}, bf16[96,512]{1,0:T(8,128)(2,1)S(1)}, u32[]{:S(2)}, u32[]{:S(2)}) %collective-permute-start.52) | collective-permute-done | bytes 98336 | tf_op jit(solution)/shard_map/ppermute | solution.py:782
  422.3 4.1 place_1_0_1.1.rest_2_
  426.3 4.6 %collective-permute-done.66 = bf16[384,512]{1,0:T(8,128)(2,1)S(1)} collective-permute-done((bf16[384,512]{1,0:T(8,128)(2,1)S(1)}, bf16[384,512]{1,0:T(8,128)(2,1)S(1)}, u32[]{:S(2)}, u32[]{:S(2)}) %collective-permute-start.66) | collective-permute-done | bytes 393248 | tf_op jit(solution)/shard_map/ppermute | solution.py:782
  434.8 3.2 copy.48
  438.1 3.6 place_1_1024_1.1
  (370 shorter events, 101.4 us)
Async XLA Ops:
  1.5 12.7 %collective-permute-start = (bf16[2,16,768]{2,1,0:T(8,128)(2,1)S(1)}, bf16[2,16,768]{2,1,0:T(8,128)(2,1)S(1)}, u32[]{:S(2)}, u32[]{:S(2)}) collective-permute-start(bf16[2,16,768]{2,1,0:T(8,128)(2,1)S(1)} %slice.120), channel_id=1, source_target_pairs={{0,4},{4,8},{8,12},{12,16},{16,20},{20,24},{24,28},{1,5},{5,9},{9,... | collective-permute-start | bytes 147464 | tf_op jit(solution)/shard_map/ppermute | solution.py:788
  31.3 34.3 %collective-permute-start.4 = (bf16[144,384]{1,0:T(8,128)(2,1)S(1)}, bf16[144,384]{1,0:T(8,128)(2,1)S(1)}, u32[]{:S(2)}, u32[]{:S(2)}) collective-permute-start(bf16[144,384]{1,0:T(8,128)(2,1)S(1)} %get-tuple-element.121.rest_0_), channel_id=1, source_target_pairs={{0,4},{4,8},{8,12},{12,16},{16,20},{20,24},{24,28},{1,5},{5,9},{9,... | collective-permute-start | bytes 331784 | tf_op jit(solution)/shard_map/ppermute | solution.py:788
  35.8 31.2 %collective-permute-start.5 = (bf16[144,384]{1,0:T(8,128)(2,1)S(1)}, bf16[144,384]{1,0:T(8,128)(2,1)S(1)}, u32[]{:S(2)}, u32[]{:S(2)}) collective-permute-start(bf16[144,384]{1,0:T(8,128)(2,1)S(1)} %get-tuple-element.121.rest_0_), channel_id=1, source_target_pairs={{0,8},{4,12},{8,16},{12,20},{16,24},{20,28},{1,9},{5,13},{9,17},{1... | collective-permute-start | bytes 331784 | tf_op jit(solution)/shard_map/ppermute | solution.py:788
  38.5 28.5 %collective-permute-start.6 = (bf16[144,384]{1,0:T(8,128)(2,1)S(1)}, bf16[144,384]{1,0:T(8,128)(2,1)S(1)}, u32[]{:S(2)}, u32[]{:S(2)}) collective-permute-start(bf16[144,384]{1,0:T(8,128)(2,1)S(1)} %get-tuple-element.121.rest_0_), channel_id=1, source_target_pairs={{0,12},{4,16},{8,20},{12,24},{16,28},{1,13},{5,17},{9,21},{13,25},... | collective-permute-start | bytes 331784 | tf_op jit(solution)/shard_map/ppermute | solution.py:788
  61.2 14.5 %collective-permute-start.1 = (bf16[144,384]{1,0:T(8,128)(2,1)S(1)}, bf16[144,384]{1,0:T(8,128)(2,1)S(1)}, u32[]{:S(2)}, u32[]{:S(2)}) collective-permute-start(bf16[144,384]{1,0:T(8,128)(2,1)S(1)} %get-tuple-element.128.rest_3_), channel_id=1, source_target_pairs={{0,4},{4,8},{8,12},{12,16},{16,20},{20,24},{24,28},{1,5},{5,9},{9,... | collective-permute-start | bytes 331784 | tf_op jit(solution)/shard_map/ppermute | solution.py:788
  63.1 12.6 %collective-permute-start.2 = (bf16[144,384]{1,0:T(8,128)(2,1)S(1)}, bf16[144,384]{1,0:T(8,128)(2,1)S(1)}, u32[]{:S(2)}, u32[]{:S(2)}) collective-permute-start(bf16[144,384]{1,0:T(8,128)(2,1)S(1)} %get-tuple-element.128.rest_3_), channel_id=1, source_target_pairs={{0,8},{4,12},{8,16},{12,20},{16,24},{20,28},{1,9},{5,13},{9,17},{1... | collective-permute-start | bytes 331784 | tf_op jit(solution)/shard_map/ppermute | solution.py:788
  73.1 12.3 %collective-permute-start.10 = (bf16[144,384]{1,0:T(8,128)(2,1)S(1)}, bf16[144,384]{1,0:T(8,128)(2,1)S(1)}, u32[]{:S(2)}, u32[]{:S(2)}) collective-permute-start(bf16[144,384]{1,0:T(8,128)(2,1)S(1)} %get-tuple-element.142), channel_id=1, source_target_pairs={{0,24},{4,28},{1,25},{5,29},{2,26},{6,30},{3,27},{7,31}} | collective-permute-start | bytes 331784 | tf_op jit(solution)/shard_map/ppermute | solution.py:788
  81.8 15.1 %collective-permute-start.7 = (bf16[144,384]{1,0:T(8,128)(2,1)S(1)}, bf16[144,384]{1,0:T(8,128)(2,1)S(1)}, u32[]{:S(2)}, u32[]{:S(2)}) collective-permute-start(bf16[144,384]{1,0:T(8,128)(2,1)S(1)} %get-tuple-element.137), channel_id=1, source_target_pairs={{0,12},{4,16},{8,20},{12,24},{16,28},{1,13},{5,17},{9,21},{13,25},... | collective-permute-start | bytes 331784 | tf_op jit(solution)/shard_map/ppermute | solution.py:788
  83.7 13.2 %collective-permute-start.8 = (bf16[144,384]{1,0:T(8,128)(2,1)S(1)}, bf16[144,384]{1,0:T(8,128)(2,1)S(1)}, u32[]{:S(2)}, u32[]{:S(2)}) collective-permute-start(bf16[144,384]{1,0:T(8,128)(2,1)S(1)} %get-tuple-element.137), channel_id=1, source_target_pairs={{0,24},{4,28},{1,25},{5,29},{2,26},{6,30},{3,27},{7,31}} | collective-permute-start | bytes 331784 | tf_op jit(solution)/shard_map/ppermute | solution.py:788
  95.0 13.4 %collective-permute-start.14 = (f32[8,2048]{1,0:T(8,128)S(1)}, f32[8,2048]{1,0:T(8,128)S(1)}, u32[]{:S(2)}, u32[]{:S(2)}) collective-permute-start(f32[8,2048]{1,0:T(8,128)S(1)} %get-tuple-element.143.rest_3_.stats_a), channel_id=1, source_target_pairs={{0,1},{1,0},{2,3},{3,2},{4,5},{5,4},{6,7},{7,6},{8,9},{9,8},{10,11... | collective-permute-start | bytes 196616 | tf_op jit(solution)/shard_map/ppermute | solution.py:782
  95.1 13.4 %collective-permute-start.15 = (f32[8,2048]{1,0:T(8,128)S(1)}, f32[8,2048]{1,0:T(8,128)S(1)}, u32[]{:S(2)}, u32[]{:S(2)}) collective-permute-start(f32[8,2048]{1,0:T(8,128)S(1)} %get-tuple-element.143.rest_3_.stats_a), channel_id=1, source_target_pairs={{0,2},{1,3},{2,0},{3,1},{4,6},{5,7},{6,4},{7,5},{8,10},{9,11},{10,... | collective-permute-start | bytes 196616 | tf_op jit(solution)/shard_map/ppermute | solution.py:782
  106.5 23.3 %collective-permute-start.11 = (f32[8,2048]{1,0:T(8,128)S(1)}, f32[8,2048]{1,0:T(8,128)S(1)}, u32[]{:S(2)}, u32[]{:S(2)}) collective-permute-start(f32[8,2048]{1,0:T(8,128)S(1)} %get-tuple-element.145.rest_0_.stats_a), channel_id=1, source_target_pairs={{0,1},{1,0},{2,3},{3,2},{4,5},{5,4},{6,7},{7,6},{8,9},{9,8},{10,11... | collective-permute-start | bytes 196616 | tf_op jit(solution)/shard_map/ppermute | solution.py:782
  107.0 24.1 %collective-permute-start.12 = (f32[8,2048]{1,0:T(8,128)S(1)}, f32[8,2048]{1,0:T(8,128)S(1)}, u32[]{:S(2)}, u32[]{:S(2)}) collective-permute-start(f32[8,2048]{1,0:T(8,128)S(1)} %get-tuple-element.145.rest_0_.stats_a), channel_id=1, source_target_pairs={{0,2},{1,3},{2,0},{3,1},{4,6},{5,7},{6,4},{7,5},{8,10},{9,11},{10,... | collective-permute-start | bytes 196616 | tf_op jit(solution)/shard_map/ppermute | solution.py:782
  108.5 23.4 %collective-permute-start.13 = (f32[8,2048]{1,0:T(8,128)S(1)}, f32[8,2048]{1,0:T(8,128)S(1)}, u32[]{:S(2)}, u32[]{:S(2)}) collective-permute-start(f32[8,2048]{1,0:T(8,128)S(1)} %get-tuple-element.145.rest_0_.stats_a), channel_id=1, source_target_pairs={{0,3},{1,2},{2,1},{3,0},{4,7},{5,6},{6,5},{7,4},{8,11},{9,10},{10,... | collective-permute-start | bytes 196616 | tf_op jit(solution)/shard_map/ppermute | solution.py:782
  127.2 30.2 %collective-permute-start.21 = (bf16[144,384]{1,0:T(8,128)(2,1)S(1)}, bf16[144,384]{1,0:T(8,128)(2,1)S(1)}, u32[]{:S(2)}, u32[]{:S(2)}) collective-permute-start(bf16[144,384]{1,0:T(8,128)(2,1)S(1)} %get-tuple-element.151.rest_3_), channel_id=1, source_target_pairs={{4,0},{8,4},{12,8},{16,12},{20,16},{24,20},{28,24},{5,1},{9,5},{13... | collective-permute-start | bytes 331784 | tf_op jit(solution)/shard_map/ppermute | solution.py:788
  128.5 30.4 %collective-permute-start.22 = (bf16[144,384]{1,0:T(8,128)(2,1)S(1)}, bf16[144,384]{1,0:T(8,128)(2,1)S(1)}, u32[]{:S(2)}, u32[]{:S(2)}) collective-permute-start(bf16[144,384]{1,0:T(8,128)(2,1)S(1)} %get-tuple-element.151.rest_3_), channel_id=1, source_target_pairs={{8,0},{12,4},{16,8},{20,12},{24,16},{28,20},{9,1},{13,5},{17,9},{2... | collective-permute-start | bytes 331784 | tf_op jit(solution)/shard_map/ppermute | solution.py:788
  129.8 32.2 %collective-permute-start.23 = (bf16[144,384]{1,0:T(8,128)(2,1)S(1)}, bf16[144,384]{1,0:T(8,128)(2,1)S(1)}, u32[]{:S(2)}, u32[]{:S(2)}) collective-permute-start(bf16[144,384]{1,0:T(8,128)(2,1)S(1)} %get-tuple-element.151.rest_3_), channel_id=1, source_target_pairs={{12,0},{16,4},{20,8},{24,12},{28,16},{13,1},{17,5},{21,9},{25,13},... | collective-permute-start | bytes 331784 | tf_op jit(solution)/shard_map/ppermute | solution.py:788
  131.1 22.6 %collective-permute-start.24 = (bf16[1024,768]{1,0:T(8,128)(2,1)}, bf16[1024,768]{1,0:T(8,128)(2,1)}, u32[]{:S(2)}, u32[]{:S(2)}) collective-permute-start(bf16[1024,768]{1,0:T(8,128)(2,1)} %get-tuple-element.158), channel_id=1, source_target_pairs={{0,1},{1,0},{2,3},{3,2},{4,5},{5,4},{6,7},{7,6},{8,9},{9,8},{10,11... | collective-permute-start | bytes 4718600 | tf_op jit(solution)/shard_map/ppermute | solution.py:782
  151.0 32.1 %collective-permute-start.17 = (bf16[144,384]{1,0:T(8,128)(2,1)S(1)}, bf16[144,384]{1,0:T(8,128)(2,1)S(1)}, u32[]{:S(2)}, u32[]{:S(2)}) collective-permute-start(bf16[144,384]{1,0:T(8,128)(2,1)S(1)} %get-tuple-element.153.rest_4_), channel_id=1, source_target_pairs={{4,0},{8,4},{12,8},{16,12},{20,16},{24,20},{28,24},{5,1},{9,5},{13... | collective-permute-start | bytes 331784 | tf_op jit(solution)/shard_map/ppermute | solution.py:788
  153.7 30.7 %collective-permute-start.18 = (bf16[144,384]{1,0:T(8,128)(2,1)S(1)}, bf16[144,384]{1,0:T(8,128)(2,1)S(1)}, u32[]{:S(2)}, u32[]{:S(2)}) collective-permute-start(bf16[144,384]{1,0:T(8,128)(2,1)S(1)} %get-tuple-element.153.rest_4_), channel_id=1, source_target_pairs={{8,0},{12,4},{16,8},{20,12},{24,16},{28,20},{9,1},{13,5},{17,9},{2... | collective-permute-start | bytes 331784 | tf_op jit(solution)/shard_map/ppermute | solution.py:788
  157.4 31.0 %collective-permute-start.19 = (bf16[144,384]{1,0:T(8,128)(2,1)S(1)}, bf16[144,384]{1,0:T(8,128)(2,1)S(1)}, u32[]{:S(2)}, u32[]{:S(2)}) collective-permute-start(bf16[144,384]{1,0:T(8,128)(2,1)S(1)} %get-tuple-element.153.rest_4_), channel_id=1, source_target_pairs={{12,0},{16,4},{20,8},{24,12},{28,16},{13,1},{17,5},{21,9},{25,13},... | collective-permute-start | bytes 331784 | tf_op jit(solution)/shard_map/ppermute | solution.py:788
  158.9 19.1 %collective-permute-start.60 = (bf16[768,384]{1,0:T(8,128)(2,1)S(1)}, bf16[768,384]{1,0:T(8,128)(2,1)S(1)}, u32[]{:S(2)}, u32[]{:S(2)}) collective-permute-start(bf16[768,384]{1,0:T(8,128)(2,1)S(1)} %constant_dynamic-slice_fusion.2), channel_id=1, source_target_pairs={{0,4},{4,0},{8,12},{12,8},{16,20},{20,16},{24,28},{28,24},{1,5},{5... | collective-permute-start | bytes 1769480 | tf_op jit(solution)/shard_map/ppermute | solution.py:782
  162.0 17.6 %collective-permute-start.20 = (bf16[1024,768]{1,0:T(8,128)(2,1)S(1)}, bf16[1024,768]{1,0:T(8,128)(2,1)S(1)}, u32[]{:S(2)}, u32[]{:S(2)}) collective-permute-start(bf16[1024,768]{1,0:T(8,128)(2,1)S(1)} %copy-done.77), channel_id=1, source_target_pairs={{0,1},{1,0},{2,3},{3,2},{4,5},{5,4},{6,7},{7,6},{8,9},{9,8},{10,11... | collective-permute-start | bytes 4718600 | tf_op jit(solution)/shard_map/ppermute | solution.py:782
  178.0 37.4 %collective-permute-start.29 = (bf16[1024,768]{1,0:T(8,128)(2,1)S(1)}, bf16[1024,768]{1,0:T(8,128)(2,1)}, u32[]{:S(2)}, u32[]{:S(2)}) collective-permute-start(bf16[1024,768]{1,0:T(8,128)(2,1)S(1)} %add_convert_fusion.4.rest_3_), channel_id=1, source_target_pairs={{0,2},{1,3},{2,0},{3,1},{4,6},{5,7},{6,4},{7,5},{8,10},{9,11},{10,... | collective-permute-start | bytes 4718600 | tf_op jit(solution)/shard_map/ppermute | solution.py:782
  179.7 38.9 %collective-permute-start.27 = (bf16[144,384]{1,0:T(8,128)(2,1)S(1)}, bf16[144,384]{1,0:T(8,128)(2,1)S(1)}, u32[]{:S(2)}, u32[]{:S(2)}) collective-permute-start(bf16[144,384]{1,0:T(8,128)(2,1)S(1)} %get-tuple-element.175), channel_id=1, source_target_pairs={{12,0},{16,4},{20,8},{24,12},{28,16},{13,1},{17,5},{21,9},{25,13},... | collective-permute-start | bytes 331784 | tf_op jit(solution)/shard_map/ppermute | solution.py:788
  183.1 41.8 %collective-permute-start.28 = (bf16[144,384]{1,0:T(8,128)(2,1)S(1)}, bf16[144,384]{1,0:T(8,128)(2,1)S(1)}, u32[]{:S(2)}, u32[]{:S(2)}) collective-permute-start(bf16[144,384]{1,0:T(8,128)(2,1)S(1)} %get-tuple-element.175), channel_id=1, source_target_pairs={{24,0},{28,4},{25,1},{29,5},{26,2},{30,6},{27,3},{31,7}} | collective-permute-start | bytes 331784 | tf_op jit(solution)/shard_map/ppermute | solution.py:788
  184.4 17.9 %collective-permute-start.61 = (bf16[384,384]{1,0:T(8,128)(2,1)S(1)}, bf16[384,384]{1,0:T(8,128)(2,1)S(1)}, u32[]{:S(2)}, u32[]{:S(2)}) collective-permute-start(bf16[384,384]{1,0:T(8,128)(2,1)S(1)} %constant_dynamic-slice_fusion.1), channel_id=1, source_target_pairs={{0,8},{4,12},{8,0},{12,4},{16,24},{20,28},{24,16},{28,20},{1,9},{5... | collective-permute-start | bytes 884744 | tf_op jit(solution)/shard_map/ppermute | solution.py:782
  188.4 63.7 %collective-permute-start.31 = (bf16[1024,768]{1,0:T(8,128)(2,1)S(1)}, bf16[1024,768]{1,0:T(8,128)(2,1)}, u32[]{:S(2)}, u32[]{:S(2)}) collective-permute-start(bf16[1024,768]{1,0:T(8,128)(2,1)S(1)} %add_convert_fusion.5.rest_3_), channel_id=1, source_target_pairs={{0,2},{1,3},{2,0},{3,1},{4,6},{5,7},{6,4},{7,5},{8,10},{9,11},{10,... | collective-permute-start | bytes 4718600 | tf_op jit(solution)/shard_map/ppermute | solution.py:782
  202.3 53.4 %collective-permute-start.25 = (bf16[144,384]{1,0:T(8,128)(2,1)S(1)}, bf16[144,384]{1,0:T(8,128)(2,1)S(1)}, u32[]{:S(2)}, u32[]{:S(2)}) collective-permute-start(bf16[144,384]{1,0:T(8,128)(2,1)S(1)} %get-tuple-element.166), channel_id=1, source_target_pairs={{12,0},{16,4},{20,8},{24,12},{28,16},{13,1},{17,5},{21,9},{25,13},... | collective-permute-start | bytes 331784 | tf_op jit(solution)/shard_map/ppermute | solution.py:788
  215.4 40.4 %collective-permute-start.26 = (bf16[144,384]{1,0:T(8,128)(2,1)S(1)}, bf16[144,384]{1,0:T(8,128)(2,1)S(1)}, u32[]{:S(2)}, u32[]{:S(2)}) collective-permute-start(bf16[144,384]{1,0:T(8,128)(2,1)S(1)} %get-tuple-element.166), channel_id=1, source_target_pairs={{24,0},{28,4},{25,1},{29,5},{26,2},{30,6},{27,3},{31,7}} | collective-permute-start | bytes 331784 | tf_op jit(solution)/shard_map/ppermute | solution.py:788
  218.5 30.2 %collective-permute-start.62 = (bf16[192,384]{1,0:T(8,128)(2,1)S(1)}, bf16[192,384]{1,0:T(8,128)(2,1)S(1)}, u32[]{:S(2)}, u32[]{:S(2)}) collective-permute-start(bf16[192,384]{1,0:T(8,128)(2,1)S(1)} %constant_dynamic-slice_fusion), channel_id=1, source_target_pairs={{0,16},{4,20},{8,24},{12,28},{16,0},{20,4},{24,8},{28,12},{1,17},{... | collective-permute-start | bytes 442376 | tf_op jit(solution)/shard_map/ppermute | solution.py:782
  224.9 99.8 %collective-permute-start.35 = (bf16[1024,768]{1,0:T(8,128)(2,1)S(1)}, bf16[1024,768]{1,0:T(8,128)(2,1)S(1)}, u32[]{:S(2)}, u32[]{:S(2)}) collective-permute-start(bf16[1024,768]{1,0:T(8,128)(2,1)S(1)} %add_convert_fusion.3.rest_4_.mine), channel_id=1, source_target_pairs={{0,1},{1,0},{2,3},{3,2},{4,5},{5,4},{6,7},{7,6},{8,9},{9,8},{10,11... | collective-permute-start | bytes 4718600 | tf_op jit(solution)/shard_map/ppermute | solution.py:782
  248.8 20.8 %collective-permute-start.63 = (bf16[192,384]{1,0:T(8,128)(2,1)S(1)}, bf16[192,384]{1,0:T(8,128)(2,1)S(1)}, u32[]{:S(2)}, u32[]{:S(2)}) collective-permute-start(bf16[192,384]{1,0:T(8,128)(2,1)S(1)} %add_convert_fusion.13), channel_id=1, source_target_pairs={{0,16},{4,20},{8,24},{12,28},{16,0},{20,4},{24,8},{28,12},{1,17},{... | collective-permute-start | bytes 442376 | tf_op jit(solution)/shard_map/ppermute | solution.py:782
  255.7 68.9 %collective-permute-start.36 = (bf16[1024,768]{1,0:T(8,128)(2,1)S(1)}, bf16[1024,768]{1,0:T(8,128)(2,1)S(1)}, u32[]{:S(2)}, u32[]{:S(2)}) collective-permute-start(bf16[1024,768]{1,0:T(8,128)(2,1)S(1)} %add_convert_fusion.2.rest_0_.mine), channel_id=1, source_target_pairs={{0,1},{1,0},{2,3},{3,2},{4,5},{5,4},{6,7},{7,6},{8,9},{9,8},{10,11... | collective-permute-start | bytes 4718600 | tf_op jit(solution)/shard_map/ppermute | solution.py:782
  269.1 14.7 %collective-permute-start.32 = (bf16[1024,768]{1,0:T(8,128)(2,1)S(1)}, bf16[1024,768]{1,0:T(8,128)(2,1)}, u32[]{:S(2)}, u32[]{:S(2)}) collective-permute-start(bf16[1024,768]{1,0:T(8,128)(2,1)S(1)} %constant_dynamic-slice_fusion.11), channel_id=1, source_target_pairs={{0,1},{1,0},{2,3},{3,2},{4,5},{5,4},{6,7},{7,6},{8,9},{9,8},{10,11... | collective-permute-start | bytes 4718600 | tf_op jit(solution)/shard_map/ppermute | solution.py:782
  281.7 29.7 %collective-permute-start.65 = (bf16[768,384]{1,0:T(8,128)(2,1)}, bf16[768,384]{1,0:T(8,128)(2,1)}, u32[]{:S(2)}, u32[]{:S(2)}) collective-permute-start(bf16[768,384]{1,0:T(8,128)(2,1)} %pad_maximum_fusion), channel_id=1, source_target_pairs={{0,4},{4,0},{8,12},{12,8},{16,20},{20,16},{24,28},{28,24},{1,5},{5... | collective-permute-start | bytes 1769480 | tf_op jit(solution)/shard_map/ppermute | solution.py:782
  286.1 35.6 %collective-permute-start.34 = (bf16[1024,768]{1,0:T(8,128)(2,1)S(1)}, bf16[1024,768]{1,0:T(8,128)(2,1)}, u32[]{:S(2)}, u32[]{:S(2)}) collective-permute-start(bf16[1024,768]{1,0:T(8,128)(2,1)S(1)} %add_convert_fusion.1.rest_5_), channel_id=1, source_target_pairs={{0,2},{1,3},{2,0},{3,1},{4,6},{5,7},{6,4},{7,5},{8,10},{9,11},{10,... | collective-permute-start | bytes 4718600 | tf_op jit(solution)/shard_map/ppermute | solution.py:782
  311.4 22.9 %collective-permute-start.33 = (f32[16,640]{1,0:T(8,128)S(1)}, f32[16,640]{1,0:T(8,128)S(1)}, u32[]{:S(2)}, u32[]{:S(2)}) collective-permute-start(f32[16,640]{1,0:T(8,128)S(1)} %get-tuple-element.191), channel_id=1, source_target_pairs={{4,0},{8,4},{12,8},{16,12},{20,16},{24,20},{28,24},{5,1},{9,5},{13... | collective-permute-start | bytes 122888 | tf_op jit(solution)/shard_map/ppermute | solution.py:788
  324.6 22.5 %collective-permute-start.38 = (bf16[1024,768]{1,0:T(8,128)(2,1)}, bf16[1024,768]{1,0:T(8,128)(2,1)}, u32[]{:S(2)}, u32[]{:S(2)}) collective-permute-start(bf16[1024,768]{1,0:T(8,128)(2,1)} %add_convert_fusion.rest_1_.mine), channel_id=1, source_target_pairs={{0,1},{1,0},{2,3},{3,2},{4,5},{5,4},{6,7},{7,6},{8,9},{9,8},{10,11... | collective-permute-start | bytes 4718600 | tf_op jit(solution)/shard_map/ppermute | solution.py:782
  343.0 13.7 %collective-permute-start.40 = (bf16[512,768]{1,0:T(8,128)(2,1)}, bf16[512,768]{1,0:T(8,128)(2,1)}, u32[]{:S(2)}, u32[]{:S(2)}) collective-permute-start(bf16[512,768]{1,0:T(8,128)(2,1)} %constant_dynamic-slice_fusion.7), channel_id=1, source_target_pairs={{0,1},{1,0},{2,3},{3,2},{4,5},{5,4},{6,7},{7,6},{8,9},{9,8},{10,11... | collective-permute-start | bytes 2359304 | tf_op jit(solution)/shard_map/ppermute | solution.py:782
  345.6 24.4 %collective-permute-start.44 = (bf16[512,768]{1,0:T(8,128)(2,1)S(1)}, bf16[512,768]{1,0:T(8,128)(2,1)}, u32[]{:S(2)}, u32[]{:S(2)}) collective-permute-start(bf16[512,768]{1,0:T(8,128)(2,1)S(1)} %add_convert_fusion.9.rest_3_), channel_id=1, source_target_pairs={{0,2},{1,3},{2,0},{3,1},{4,6},{5,7},{6,4},{7,5},{8,10},{9,11},{10,... | collective-permute-start | bytes 2359304 | tf_op jit(solution)/shard_map/ppermute | solution.py:782
  355.2 13.2 %collective-permute-start.39 = (bf16[384,640]{1,0:T(8,128)(2,1)}, bf16[384,640]{1,0:T(8,128)(2,1)}, u32[]{:S(2)}, u32[]{:S(2)}) collective-permute-start(bf16[384,640]{1,0:T(8,128)(2,1)} %get-tuple-element.265), channel_id=1, source_target_pairs={{0,4},{4,0},{8,12},{12,8},{16,20},{20,16},{24,28},{28,24},{1,5},{5... | collective-permute-start | bytes 1474568 | tf_op jit(solution)/shard_map/ppermute | solution.py:782
  371.6 50.6 %collective-permute-start.50 = (bf16[512,768]{1,0:T(8,128)(2,1)S(1)}, bf16[512,768]{1,0:T(8,128)(2,1)}, u32[]{:S(2)}, u32[]{:S(2)}) collective-permute-start(bf16[512,768]{1,0:T(8,128)(2,1)S(1)} %add_convert_fusion.7.rest_1_.mine), channel_id=1, source_target_pairs={{0,1},{1,0},{2,3},{3,2},{4,5},{5,4},{6,7},{7,6},{8,9},{9,8},{10,11... | collective-permute-start | bytes 2359304 | tf_op jit(solution)/shard_map/ppermute | solution.py:782
  371.7 22.7 %collective-permute-start.48 = (bf16[512,768]{1,0:T(8,128)(2,1)}, bf16[512,768]{1,0:T(8,128)(2,1)}, u32[]{:S(2)}, u32[]{:S(2)}) collective-permute-start(bf16[512,768]{1,0:T(8,128)(2,1)} %add_convert_fusion.8), channel_id=1, source_target_pairs={{0,2},{1,3},{2,0},{3,1},{4,6},{5,7},{6,4},{7,5},{8,10},{9,11},{10,... | collective-permute-start | bytes 2359304 | tf_op jit(solution)/shard_map/ppermute | solution.py:782
  375.0 15.6 %collective-permute-start.41 = (bf16[96,640]{1,0:T(8,128)(2,1)S(1)}, bf16[96,640]{1,0:T(8,128)(2,1)S(1)}, u32[]{:S(2)}, u32[]{:S(2)}) collective-permute-start(bf16[96,640]{1,0:T(8,128)(2,1)S(1)} %get-tuple-element.275), channel_id=1, source_target_pairs={{0,8},{4,12},{8,0},{12,4},{16,24},{20,28},{24,16},{28,20},{1,9},{5... | collective-permute-start | bytes 368648 | tf_op jit(solution)/shard_map/ppermute | solution.py:782
  375.7 15.0 %collective-permute-start.42 = (bf16[96,640]{1,0:T(8,128)(2,1)S(1)}, bf16[96,640]{1,0:T(8,128)(2,1)S(1)}, u32[]{:S(2)}, u32[]{:S(2)}) collective-permute-start(bf16[96,640]{1,0:T(8,128)(2,1)S(1)} %get-tuple-element.274), channel_id=1, source_target_pairs={{0,16},{4,20},{8,24},{12,28},{16,0},{20,4},{24,8},{28,12},{1,17},{... | collective-permute-start | bytes 368648 | tf_op jit(solution)/shard_map/ppermute | solution.py:782
  400.7 15.0 %collective-permute-start.51 = (bf16[96,512]{1,0:T(8,128)(2,1)S(1)}, bf16[96,512]{1,0:T(8,128)(2,1)S(1)}, u32[]{:S(2)}, u32[]{:S(2)}) collective-permute-start(bf16[96,512]{1,0:T(8,128)(2,1)S(1)} %get-tuple-element.260.rest_2_), channel_id=1, source_target_pairs={{0,8},{4,12},{8,0},{12,4},{16,24},{20,28},{24,16},{28,20},{1,9},{5... | collective-permute-start | bytes 294920 | tf_op jit(solution)/shard_map/ppermute | solution.py:782
  413.9 24.2 %collective-permute-start.49 = (bf16[512,768]{1,0:T(8,128)(2,1)S(1)}, bf16[512,768]{1,0:T(8,128)(2,1)S(1)}, u32[]{:S(2)}, u32[]{:S(2)}) collective-permute-start(bf16[512,768]{1,0:T(8,128)(2,1)S(1)} %add_convert_fusion.6.rest_2_.mine), channel_id=1, source_target_pairs={{0,1},{1,0},{2,3},{3,2},{4,5},{5,4},{6,7},{7,6},{8,9},{9,8},{10,11... | collective-permute-start | bytes 2359304 | tf_op jit(solution)/shard_map/ppermute | solution.py:782
  (98 other events, 961.8 us)

commit v4 on v3

--- a/solution.py
+++ b/solution.py
@@ -1117,7 +1117,7 @@
         call.out((length, width), F32, rows_of(width, ahead, small))
         call.out((length, 128), F32, rows_of(128, ahead, small))
         call.out((STATES + 8, channels), F32).out((STATES + 16, channels), BF)
-        return call.run(14)
+        return call.run(3)
 
     def across(m, kept, carry, third, inner, parts, chain, *waits):
         normed, gate, xbc, pre, conv, deltas, held, sums, leaving, edge = kept
@@ -1143,7 +1143,7 @@
         call.out((40, width), F32)
         call.out((16, 128), F32)
         call.temp((3, tile + 24, width), F32).temp((tile, width), F32).temp((STATES, channels), F32)
-        return call.run(32)
+        return call.run(10)
 
     def part_of(m, gate_back, fourth, span, rows, rim, chain, earlier, micros, *waits):
         count = span[1] - span[0]

time: 450 us -> 438 us (0.973)
  waiting for transfers between devices: 43 us -> 32.6 us
    ppermute x44, waiting for transfers between devices: 42.9 us -> 30.6 us  [swap(): return lax.ppermute(value, axis, [(i, i ^ bits) for i in range(count)])]
    unnamed x165 -> x131, local copies, waits for them, and re-layouts: 14.8 us -> 16.2 us
  transfers between devices with their start and end apart: 67 -> 67, of which waited for: 10 -> 10; matrix products, arithmetic and copies ran while one was open for 12% -> 12% of each run, Pallas kernels for 49% -> 51%
where the time goes in v4:
time: 438 us; the launch traced here: 430 us
  Pallas kernels  237 us (54%)
  starting transfers between devices  96 us (22%)
  waiting for transfers between devices  32.6 us (7%)
  local copies, waits for them, and re-layouts  30.8 us (7%)
  other arithmetic  30.4 us (7%)
    pallas_call x23, Pallas kernels, run(): pl.pallas_call(self.kernel, grid_spec=pltpu.PrefetchScalarGridSpec(num_sc...  237 us
    ppermute x44, starting transfers between devices, swap(): return lax.ppermute(value, axis, [(i, i ^ bits) for i in range(count)])  51.3 us
    ppermute x23, starting transfers between devices, from_behind(): return lax.ppermute(value, axis, [(i, i + steps) for i in sources])  44.7 us
    ppermute x44, waiting for transfers between devices, swap(): return lax.ppermute(value, axis, [(i, i ^ bits) for i in range(count)])  30.6 us
    unnamed x131, local copies, waits for them, and re-layouts  16.2 us
    convert_element_type x5, other arithmetic, pair_sum(): return (mine.astype(F32) + swap(other, 'head', 1).astype(F32)).astype(BF)  11.6 us
    convert_element_type x5, other arithmetic, head_rest(): low = (low.astype(F32) + swap(low, 'head', bit).astype(F32)).astype(BF)  9.73 us
  transfers between devices with their start and end apart: 67, of which 10 were waited for; matrix products, arithmetic and copies ran while one was open for 12% of the time, Pallas kernels for 51%

profile of v4, /device:TPU:0, one launch (start us, length us, event | category | flops | bytes accessed | tf_op | source)
XLA Modules:
  0.0 429.5 jit_solution(16811006365596971709)
XLA Ops:
  1.5 4.9 %collective-permute-start = (bf16[2,16,768]{2,1,0:T(8,128)(2,1)S(1)}, bf16[2,16,768]{2,1,0:T(8,128)(2,1)S(1)}, u32[]{:S(2)}, u32[]{:S(2)}) collective-permute-start(bf16[2,16,768]{2,1,0:T(8,128)(2,1)S(1)} %slice.120), channel_id=1, source_target_pairs={{0,4},{4,8},{8,12},{12,16},{16,20},{20,24},{24,28},{1,5},{5,9},{9,... | collective-permute-start | bytes 147464 | tf_op jit(solution)/shard_map/ppermute | solution.py:788
  7.7 3.7 fusion.7
  13.3 16.7 %project_0.1 = (bf16[2048,768]{1,0:T(8,128)(2,1)}, f32[2048,384]{1,0:T(8,128)}, bf16[2048,640]{1,0:T(8,128)(2,1)}, bf16[2048,640]{1,0:T(8,128)(2,1)}, bf16[2048,...) custom-call(s32[2,9]{1,0:T(2,128)S(1)} %concatenate.37.meta, ...), custom_call_target="tpu_custom_call" | custom-call | flops 25300000768 | tf_op jit(solution)/shard_map/project_0/pallas_call | solution.py:761
  30.0 3.7 collective-permute-start.4
  33.7 3.5 collective-permute-start.5
  37.2 4.6 %collective-permute-start.6 = (bf16[144,384]{1,0:T(8,128)(2,1)S(1)}, bf16[144,384]{1,0:T(8,128)(2,1)S(1)}, u32[]{:S(2)}, u32[]{:S(2)}) collective-permute-start(bf16[144,384]{1,0:T(8,128)(2,1)S(1)} %get-tuple-element.121.rest_0_), channel_id=1, source_target_pairs={{0,12},{4,16},{8,20},{12,24},{16,28},{1,13},{5,17},{9,21},{13,25},... | collective-permute-start | bytes 331784 | tf_op jit(solution)/shard_map/ppermute | solution.py:788
  41.9 17.3 %project_1.1 = (bf16[2048,768]{1,0:T(8,128)(2,1)}, f32[2048,384]{1,0:T(8,128)}, bf16[2048,640]{1,0:T(8,128)(2,1)}, bf16[2048,640]{1,0:T(8,128)(2,1)}, bf16[2048,...) custom-call(s32[2,9]{1,0:T(2,128)S(1)} %concatenate.37.meta, ...), custom_call_target="tpu_custom_call" | custom-call | flops 25300000768 | tf_op jit(solution)/shard_map/project_1/pallas_call | solution.py:761
  59.2 2.7 collective-permute-start.1
  64.5 6.0 %inside_0.1 = (f32[2048,384]{1,0:T(8,128)}, f32[136,384]{1,0:T(8,128)S(1)}, bf16[144,384]{1,0:T(8,128)(2,1)S(1)}) custom-call(s32[2,9]{1,0:T(2,128)S(1)} %concatenate.37.meta, bf16[2048,640]{1,0:T(8,128)(2,1)S(1)} %copy-done.19, f32[2048,128]{1,0:T(8,128)S(1)} %get-tuple-element.130.deltas, f32[16,768]{1,0:T(8,128)S(1)} %concatenate.42.table.rest_1_, ...), custom_call_target="tpu_custom_call" | custom-call | flops 12650000384 | tf_op jit(solution)/shard_map/inside_0/pallas_call | solution.py:761
  73.2 6.0 %inside_1.1 = (f32[2048,384]{1,0:T(8,128)}, f32[136,384]{1,0:T(8,128)S(1)}, bf16[144,384]{1,0:T(8,128)(2,1)S(1)}) custom-call(s32[2,9]{1,0:T(2,128)S(1)} %concatenate.37.meta, bf16[2048,640]{1,0:T(8,128)(2,1)S(1)} %copy-done.18, f32[2048,128]{1,0:T(8,128)S(1)} %get-tuple-element.127.deltas, f32[16,768]{1,0:T(8,128)S(1)} %concatenate.42.table.rest_1_, ...), custom_call_target="tpu_custom_call" | custom-call | flops 12650000384 | tf_op jit(solution)/shard_map/inside_1/pallas_call | solution.py:761
  79.2 1.9 collective-permute-start.7
  82.8 9.6 %mix_0.1 = (f32[2048,384]{1,0:T(8,128)}, f32[8,2048]{1,0:T(8,128)S(1)}, f32[128,384]{1,0:T(8,128)S(1)}) custom-call(s32[2,9]{1,0:T(2,128)S(1)} %concatenate.37.meta, f32[2048,384]{1,0:T(8,128)} %get-tuple-element.138.inside, bf16[2048,640]{1,0:T(8,128)(2,1)S(1)} %copy-done.19, f32[2048,128]{1,0:T(8,128)S(1)} %get-tuple-element.130.deltas, ...), custom_call_target="tpu_custom_call" | custom-call | flops 13799999488 | tf_op jit(solution)/shard_map/mix_0/pallas_call | solution.py:761
  94.2 9.6 %mix_1.1 = (f32[2048,384]{1,0:T(8,128)}, f32[8,2048]{1,0:T(8,128)S(1)}, f32[128,384]{1,0:T(8,128)S(1)}) custom-call(s32[2,9]{1,0:T(2,128)S(1)} %concatenate.37.meta, f32[2048,384]{1,0:T(8,128)} %get-tuple-element.132.inside, bf16[2048,640]{1,0:T(8,128)(2,1)S(1)} %copy-done.18, f32[2048,128]{1,0:T(8,128)S(1)} %get-tuple-element.127.deltas, ...), custom_call_target="tpu_custom_call" | custom-call | flops 13799999488 | tf_op jit(solution)/shard_map/mix_1/pallas_call | solution.py:761
  105.8 18.6 %gate_0.1 = (bf16[1024,768]{1,0:T(8,128)(2,1)}, bf16[1024,768]{1,0:T(8,128)(2,1)}, bf16[2048,384]{1,0:T(8,128)(2,1)}, bf16[2048,384]{1,0:T(8,128)(2,1)}, f32[16,...) custom-call(s32[1]{0:T(128)} %bitcast.4.side, ...), custom_call_target="tpu_custom_call" | custom-call | flops 19549999104 | tf_op jit(solution)/shard_map/gate_0/pallas_call | solution.py:761
  125.0 18.7 %gate_1.1 = (bf16[1024,768]{1,0:T(8,128)(2,1)}, bf16[1024,768]{1,0:T(8,128)(2,1)}, bf16[2048,384]{1,0:T(8,128)(2,1)}, bf16[2048,384]{1,0:T(8,128)(2,1)}, f32[16,...) custom-call(s32[1]{0:T(128)} %bitcast.4.side, ...), custom_call_target="tpu_custom_call" | custom-call | flops 19549999104 | tf_op jit(solution)/shard_map/gate_1/pallas_call | solution.py:761
  148.2 2.7 collective-permute-start.60
  150.9 2.4 add_convert_fusion.4.rest_3_
  158.2 13.4 %within_0.1 = (f32[2048,640]{1,0:T(8,128)}, f32[2048,128]{1,0:T(8,128)S(1)}, f32[136,384]{1,0:T(8,128)S(1)}, bf16[144,384]{1,0:T(8,128)(2,1)S(1)}) custom-call(s32[2,9]{1,0:T(2,128)S(1)} %concatenate.37.meta, bf16[2048,640]{1,0:T(8,128)(2,1)} %get-tuple-element.129.conv, f32[2048,128]{1,0:T(8,128)S(1)} %copy-done.32, bf16[2048,384]{1,0:T(8,128)(2,1)S(1)} %copy-done.22, ...), custom_call_target="tpu_custom_call" | custom-call | flops 3449999872 | tf_op jit(solution)/shard_map/within_0/pallas_call | solution.py:761
  174.7 1.9 add_convert_fusion.5.rest_3_
  178.0 3.4 collective-permute-start.61
  183.4 13.4 %within_1.1 = (f32[2048,640]{1,0:T(8,128)}, f32[2048,128]{1,0:T(8,128)S(1)}, f32[136,384]{1,0:T(8,128)S(1)}, bf16[144,384]{1,0:T(8,128)(2,1)S(1)}) custom-call(s32[2,9]{1,0:T(2,128)S(1)} %concatenate.37.meta, bf16[2048,640]{1,0:T(8,128)(2,1)} %get-tuple-element.123.conv, f32[2048,128]{1,0:T(8,128)S(1)} %copy-done.24, bf16[2048,384]{1,0:T(8,128)(2,1)S(1)} %copy-done.20, ...), custom_call_target="tpu_custom_call" | custom-call | flops 3449999872 | tf_op jit(solution)/shard_map/within_1/pallas_call | solution.py:761
  201.5 11.7 %collective-permute-start.62 = (bf16[192,384]{1,0:T(8,128)(2,1)S(1)}, bf16[192,384]{1,0:T(8,128)(2,1)S(1)}, u32[]{:S(2)}, u32[]{:S(2)}) collective-permute-start(bf16[192,384]{1,0:T(8,128)(2,1)S(1)} %constant_dynamic-slice_fusion), channel_id=1, source_target_pairs={{0,16},{4,20},{8,24},{12,28},{16,0},{20,4},{24,8},{28,12},{1,17},{... | collective-permute-start | bytes 442376 | tf_op jit(solution)/shard_map/ppermute | solution.py:782
  213.2 23.6 %across_0.1 = (bf16[2048,896]{1,0:T(8,128)(2,1)}, bf16[2048,128]{1,0:T(8,128)(2,1)S(1)}, f32[16,640]{1,0:T(8,128)S(1)}, f32[16,640]{1,0:T(8,128)S(1)}, f32[40,640]{1,0:T(8,128)S(1)}, /*index=5*/f32[16,128]{1,0:T(8,128)S(1)}) custom-call(s32[2,9]{1,0:T(2,128)S(1)} %concatenate.37.meta, bf16[2048,640]{1,0:T(8,128)(2,1)} %get-tuple-element.129.conv, ...), custom_call_target="tpu_custom_call" | custom-call | flops 11500000256 | tf_op jit(solution)/shard_map/across_0/pallas_call | solution.py:761
  242.9 6.1 %input_0_0.1 = (bf16[2048,768]{1,0:T(8,128)(2,1)}, f32[8,768]{1,0:T(8,128)S(1)}) custom-call(bf16[2,2048,768]{2,1,0:T(8,128)(2,1)} %tokens.21, bf16[2048,384]{1,0:T(8,128)(2,1)S(1)} %copy-done.36, bf16[2048,896]{1,0:T(8,128)(2,1)} %get-tuple-element.179.in_back, bf16[2048,128]{1,0:T(8,128)(2,1)S(1)} %get-tuple-element.180.dt_back, ...), custom_call_target="tpu_custom_call" | custom-call | flops 6899999744 | tf_op jit(solution)/shard_map/input_0_0/pallas_call | solution.py:761
  249.0 5.5 %input_0_2.1 = (bf16[2048,768]{1,0:T(8,128)(2,1)}, f32[8,768]{1,0:T(8,128)S(1)}) custom-call(bf16[2,2048,768]{2,1,0:T(8,128)(2,1)} %tokens.21, bf16[2048,384]{1,0:T(8,128)(2,1)S(1)} %copy-done.36, bf16[2048,896]{1,0:T(8,128)(2,1)} %get-tuple-element.179.in_back, bf16[2048,128]{1,0:T(8,128)(2,1)S(1)} %get-tuple-element.180.dt_back, ...), custom_call_target="tpu_custom_call", output_to_operand_aliasing={{0}: (8, {})} | custom-call | flops 6899999744 | tf_op jit(solution)/shard_map/input_0_2/pallas_call | solution.py:761
  254.5 2.9 constant_dynamic-slice_fusion.11
  259.6 6.7 %weigh_0.1 = (f32[768,640]{1,0:T(8,128)S(1)}, f32[8,768]{1,0:T(8,128)S(1)}) custom-call(bf16[2048,768]{1,0:T(8,128)(2,1)S(1)} %copy-done.41, bf16[2048,896]{1,0:T(8,128)(2,1)} %get-tuple-element.179.in_back, bf16[2048,128]{1,0:T(8,128)(2,1)S(1)} %copy-done.40, f32[16,640]{1,0:T(8,128)S(1)} %get-tuple-element.181.rest_0_.tail, ...), custom_call_target="tpu_custom_call" | custom-call | flops 9200000000 | tf_op jit(solution)/shard_map/weigh_0/pallas_call | solution.py:761
  268.7 1.9 collective-permute-start.65
  270.7 3.4 add_convert_fusion.1.rest_5_
  275.6 25.9 %across_1.1 = (bf16[2048,896]{1,0:T(8,128)(2,1)}, bf16[2048,128]{1,0:T(8,128)(2,1)S(1)}, f32[16,640]{1,0:T(8,128)S(1)}, f32[16,640]{1,0:T(8,128)S(1)}, f32[40,640]{1,0:T(8,128)S(1)}, /*index=5*/f32[16,128]{1,0:T(8,128)S(1)}) custom-call(s32[2,9]{1,0:T(2,128)S(1)} %concatenate.37.meta, bf16[2048,640]{1,0:T(8,128)(2,1)} %get-tuple-element.123.conv, ...), custom_call_target="tpu_custom_call" | custom-call | flops 11500000256 | tf_op jit(solution)/shard_map/across_1/pallas_call | solution.py:761
  304.7 5.2 %collective-permute-done.34 = bf16[1024,768]{1,0:T(8,128)(2,1)S(1)} collective-permute-done((bf16[1024,768]{1,0:T(8,128)(2,1)}, bf16[1024,768]{1,0:T(8,128)(2,1)S(1)}, u32[]{:S(2)}, u32[]{:S(2)}) %collective-permute-start.34) | collective-permute-done | bytes 1572896 | tf_op jit(solution)/shard_map/ppermute | solution.py:782
  309.9 3.0 add_convert_fusion.rest_1_.mine
  314.5 5.2 %input_1_0.1 = (bf16[1024,768]{1,0:T(8,128)(2,1)S(1)}, f32[8,768]{1,0:T(8,128)S(1)}) custom-call(bf16[2,2048,768]{2,1,0:T(8,128)(2,1)} %tokens.21, bf16[2048,384]{1,0:T(8,128)(2,1)S(1)} %copy-done.28, bf16[2048,896]{1,0:T(8,128)(2,1)} %get-tuple-element.188.in_back, bf16[2048,128]{1,0:T(8,128)(2,1)S(1)} %get-tuple-element.189.dt_back, ...), custom_call_target="tpu_custom_call" | custom-call | flops 6899999744 | tf_op jit(solution)/shard_map/input_1_0/pallas_call | solution.py:761
  324.8 4.6 %input_1_2.1 = (bf16[1024,768]{1,0:T(8,128)(2,1)S(1)}, f32[8,768]{1,0:T(8,128)S(1)}) custom-call(bf16[2,2048,768]{2,1,0:T(8,128)(2,1)} %tokens.21, bf16[2048,384]{1,0:T(8,128)(2,1)S(1)} %copy-done.29, bf16[2048,896]{1,0:T(8,128)(2,1)} %get-tuple-element.188.in_back, bf16[2048,128]{1,0:T(8,128)(2,1)S(1)} %copy-done.38, bf16[768,1408]{1,0:T(8,128)(2,1)S(1)} %copy-done.9, ...), custom_call_target="tpu_custom_call" | custom-call | flops 6899999744 | tf_op jit(solution)/shard_map/input_1_2/pallas_call | solution.py:761
  334.5 7.1 %weigh_1.1 = (bf16[768,640]{1,0:T(8,128)(2,1)S(1)}, f32[8,768]{1,0:T(8,128)S(1)}) custom-call(bf16[2048,768]{1,0:T(8,128)(2,1)} %get-tuple-element.122.normed, bf16[2048,896]{1,0:T(8,128)(2,1)} %get-tuple-element.188.in_back, bf16[2048,128]{1,0:T(8,128)(2,1)S(1)} %copy-done.38, f32[16,640]{1,0:T(8,128)S(1)} %get-tuple-element.190.rest_0_.tail, ...), custom_call_target="tpu_custom_call" | custom-call | flops 9200000000 | tf_op jit(solution)/shard_map/weigh_1/pallas_call | solution.py:761
  344.1 2.4 add_convert_fusion.8
  346.7 9.0 %collective-permute-done.39 = bf16[384,640]{1,0:T(8,128)(2,1)} collective-permute-done((bf16[384,640]{1,0:T(8,128)(2,1)}, bf16[384,640]{1,0:T(8,128)(2,1)}, u32[]{:S(2)}, u32[]{:S(2)}) %collective-permute-start.39) | collective-permute-done | bytes 491552 | tf_op jit(solution)/shard_map/ppermute | solution.py:782
  366.7 4.4 %place_0_0_0.1.rest_0_ = bf16[2,2048,768]{2,1,0:T(8,128)(2,1)} custom-call(s32[1]{0:T(128)} %bitcast.4.side, bf16[1024,768]{1,0:T(8,128)(2,1)S(1)} %copy-done.6, bf16[1024,768]{1,0:T(8,128)(2,1)S(1)} %copy-done.11, bf16[2,2048,768]{2,1,0:T(8,128)(2,1)} %tokens.21, bf16[384,640]{1,0:T(8,128)(2,1)S(1)} %add_convert_fusion.11.rest_0_, ...), custom_call_target="tpu_custom_call" | custom-call | flops 4600000000 | tf_op jit(solution)/shard_map/place_0_0_0/pallas_call | solution.py:761
  372.9 2.9 collective-permute-start.43
  383.2 4.5 %place_1_0_0.1 = bf16[2,2048,768]{2,1,0:T(8,128)(2,1)} custom-call(s32[1]{0:T(128)} %bitcast.4.side, bf16[1024,768]{1,0:T(8,128)(2,1)S(1)} %add_convert_fusion.2.rest_0_.mine, bf16[1024,768]{1,0:T(8,128)(2,1)S(1)} %copy-done.1, bf16[2,2048,768]{2,1,0:T(8,128)(2,1)} %tokens.21, ...), custom_call_target="tpu_custom_call", output_to_operand_aliasing={{}: (4, {})} | custom-call | flops 4600000000 | tf_op jit(solution)/shard_map/place_1_0_0/pallas_call | solution.py:761
  390.2 6.9 %place_0_0_1.1.rest_2_ = bf16[2,2048,768]{2,1,0:T(8,128)(2,1)} custom-call(s32[1]{0:T(128)} %bitcast.4.side, bf16[1024,768]{1,0:T(8,128)(2,1)} %add_convert_fusion.rest_1_.mine, bf16[1024,768]{1,0:T(8,128)(2,1)} %collective-permute-done.38.rest_4_.other, bf16[2,2048,768]{2,1,0:T(8,128)(2,1)} %tokens.21, bf16[2,2048,768]{2,1,0:T(8,128)(2,1)} %rest_0_.5, ...), custom_call_target="tpu_custom_call" | custom-call | flops 4600000000 | tf_op jit(solution)/shard_map/place_0_0_1/pallas_call | solution.py:761
  397.0 3.1 collective-permute-start.52
  402.8 5.1 %collective-permute-done.52 = bf16[96,512]{1,0:T(8,128)(2,1)S(1)} collective-permute-done((bf16[96,512]{1,0:T(8,128)(2,1)S(1)}, bf16[96,512]{1,0:T(8,128)(2,1)S(1)}, u32[]{:S(2)}, u32[]{:S(2)}) %collective-permute-start.52) | collective-permute-done | bytes 98336 | tf_op jit(solution)/shard_map/ppermute | solution.py:782
  409.2 4.1 place_1_0_1.1.rest_2_
  413.3 5.2 %collective-permute-done.66 = bf16[384,512]{1,0:T(8,128)(2,1)S(1)} collective-permute-done((bf16[384,512]{1,0:T(8,128)(2,1)S(1)}, bf16[384,512]{1,0:T(8,128)(2,1)S(1)}, u32[]{:S(2)}, u32[]{:S(2)}) %collective-permute-start.66) | collective-permute-done | bytes 393248 | tf_op jit(solution)/shard_map/ppermute | solution.py:782
  420.4 1.8 copy.49
  422.4 3.2 copy.48
  425.6 3.6 place_1_1024_1.1
  (336 shorter events, 93.5 us)
Async XLA Ops:
  1.5 11.7 %collective-permute-start = (bf16[2,16,768]{2,1,0:T(8,128)(2,1)S(1)}, bf16[2,16,768]{2,1,0:T(8,128)(2,1)S(1)}, u32[]{:S(2)}, u32[]{:S(2)}) collective-permute-start(bf16[2,16,768]{2,1,0:T(8,128)(2,1)S(1)} %slice.120), channel_id=1, source_target_pairs={{0,4},{4,8},{8,12},{12,16},{16,20},{20,24},{24,28},{1,5},{5,9},{9,... | collective-permute-start | bytes 147464 | tf_op jit(solution)/shard_map/ppermute | solution.py:788
  30.0 33.2 %collective-permute-start.4 = (bf16[144,384]{1,0:T(8,128)(2,1)S(1)}, bf16[144,384]{1,0:T(8,128)(2,1)S(1)}, u32[]{:S(2)}, u32[]{:S(2)}) collective-permute-start(bf16[144,384]{1,0:T(8,128)(2,1)S(1)} %get-tuple-element.121.rest_0_), channel_id=1, source_target_pairs={{0,4},{4,8},{8,12},{12,16},{16,20},{20,24},{24,28},{1,5},{5,9},{9,... | collective-permute-start | bytes 331784 | tf_op jit(solution)/shard_map/ppermute | solution.py:788
  33.7 30.8 %collective-permute-start.5 = (bf16[144,384]{1,0:T(8,128)(2,1)S(1)}, bf16[144,384]{1,0:T(8,128)(2,1)S(1)}, u32[]{:S(2)}, u32[]{:S(2)}) collective-permute-start(bf16[144,384]{1,0:T(8,128)(2,1)S(1)} %get-tuple-element.121.rest_0_), channel_id=1, source_target_pairs={{0,8},{4,12},{8,16},{12,20},{16,24},{20,28},{1,9},{5,13},{9,17},{1... | collective-permute-start | bytes 331784 | tf_op jit(solution)/shard_map/ppermute | solution.py:788
  37.2 27.3 %collective-permute-start.6 = (bf16[144,384]{1,0:T(8,128)(2,1)S(1)}, bf16[144,384]{1,0:T(8,128)(2,1)S(1)}, u32[]{:S(2)}, u32[]{:S(2)}) collective-permute-start(bf16[144,384]{1,0:T(8,128)(2,1)S(1)} %get-tuple-element.121.rest_0_), channel_id=1, source_target_pairs={{0,12},{4,16},{8,20},{12,24},{16,28},{1,13},{5,17},{9,21},{13,25},... | collective-permute-start | bytes 331784 | tf_op jit(solution)/shard_map/ppermute | solution.py:788
  59.2 13.9 %collective-permute-start.1 = (bf16[144,384]{1,0:T(8,128)(2,1)S(1)}, bf16[144,384]{1,0:T(8,128)(2,1)S(1)}, u32[]{:S(2)}, u32[]{:S(2)}) collective-permute-start(bf16[144,384]{1,0:T(8,128)(2,1)S(1)} %get-tuple-element.128.rest_3_), channel_id=1, source_target_pairs={{0,4},{4,8},{8,12},{12,16},{16,20},{20,24},{24,28},{1,5},{5,9},{9,... | collective-permute-start | bytes 331784 | tf_op jit(solution)/shard_map/ppermute | solution.py:788
  61.9 11.3 %collective-permute-start.2 = (bf16[144,384]{1,0:T(8,128)(2,1)S(1)}, bf16[144,384]{1,0:T(8,128)(2,1)S(1)}, u32[]{:S(2)}, u32[]{:S(2)}) collective-permute-start(bf16[144,384]{1,0:T(8,128)(2,1)S(1)} %get-tuple-element.128.rest_3_), channel_id=1, source_target_pairs={{0,8},{4,12},{8,16},{12,20},{16,24},{20,28},{1,9},{5,13},{9,17},{1... | collective-permute-start | bytes 331784 | tf_op jit(solution)/shard_map/ppermute | solution.py:788
  70.5 12.2 %collective-permute-start.10 = (bf16[144,384]{1,0:T(8,128)(2,1)S(1)}, bf16[144,384]{1,0:T(8,128)(2,1)S(1)}, u32[]{:S(2)}, u32[]{:S(2)}) collective-permute-start(bf16[144,384]{1,0:T(8,128)(2,1)S(1)} %get-tuple-element.142), channel_id=1, source_target_pairs={{0,24},{4,28},{1,25},{5,29},{2,26},{6,30},{3,27},{7,31}} | collective-permute-start | bytes 331784 | tf_op jit(solution)/shard_map/ppermute | solution.py:788
  79.2 15.1 %collective-permute-start.7 = (bf16[144,384]{1,0:T(8,128)(2,1)S(1)}, bf16[144,384]{1,0:T(8,128)(2,1)S(1)}, u32[]{:S(2)}, u32[]{:S(2)}) collective-permute-start(bf16[144,384]{1,0:T(8,128)(2,1)S(1)} %get-tuple-element.137), channel_id=1, source_target_pairs={{0,12},{4,16},{8,20},{12,24},{16,28},{1,13},{5,17},{9,21},{13,25},... | collective-permute-start | bytes 331784 | tf_op jit(solution)/shard_map/ppermute | solution.py:788
  81.1 13.2 %collective-permute-start.8 = (bf16[144,384]{1,0:T(8,128)(2,1)S(1)}, bf16[144,384]{1,0:T(8,128)(2,1)S(1)}, u32[]{:S(2)}, u32[]{:S(2)}) collective-permute-start(bf16[144,384]{1,0:T(8,128)(2,1)S(1)} %get-tuple-element.137), channel_id=1, source_target_pairs={{0,24},{4,28},{1,25},{5,29},{2,26},{6,30},{3,27},{7,31}} | collective-permute-start | bytes 331784 | tf_op jit(solution)/shard_map/ppermute | solution.py:788
  92.4 13.3 %collective-permute-start.14 = (f32[8,2048]{1,0:T(8,128)S(1)}, f32[8,2048]{1,0:T(8,128)S(1)}, u32[]{:S(2)}, u32[]{:S(2)}) collective-permute-start(f32[8,2048]{1,0:T(8,128)S(1)} %get-tuple-element.143.rest_3_.stats_a), channel_id=1, source_target_pairs={{0,1},{1,0},{2,3},{3,2},{4,5},{5,4},{6,7},{7,6},{8,9},{9,8},{10,11... | collective-permute-start | bytes 196616 | tf_op jit(solution)/shard_map/ppermute | solution.py:782
  92.4 13.4 %collective-permute-start.15 = (f32[8,2048]{1,0:T(8,128)S(1)}, f32[8,2048]{1,0:T(8,128)S(1)}, u32[]{:S(2)}, u32[]{:S(2)}) collective-permute-start(f32[8,2048]{1,0:T(8,128)S(1)} %get-tuple-element.143.rest_3_.stats_a), channel_id=1, source_target_pairs={{0,2},{1,3},{2,0},{3,1},{4,6},{5,7},{6,4},{7,5},{8,10},{9,11},{10,... | collective-permute-start | bytes 196616 | tf_op jit(solution)/shard_map/ppermute | solution.py:782
  93.9 11.9 %collective-permute-start.16 = (f32[8,2048]{1,0:T(8,128)S(1)}, f32[8,2048]{1,0:T(8,128)S(1)}, u32[]{:S(2)}, u32[]{:S(2)}) collective-permute-start(f32[8,2048]{1,0:T(8,128)S(1)} %get-tuple-element.143.rest_3_.stats_a), channel_id=1, source_target_pairs={{0,3},{1,2},{2,1},{3,0},{4,7},{5,6},{6,5},{7,4},{8,11},{9,10},{10,... | collective-permute-start | bytes 196616 | tf_op jit(solution)/shard_map/ppermute | solution.py:782
  103.9 21.2 %collective-permute-start.11 = (f32[8,2048]{1,0:T(8,128)S(1)}, f32[8,2048]{1,0:T(8,128)S(1)}, u32[]{:S(2)}, u32[]{:S(2)}) collective-permute-start(f32[8,2048]{1,0:T(8,128)S(1)} %get-tuple-element.145.rest_0_.stats_a), channel_id=1, source_target_pairs={{0,1},{1,0},{2,3},{3,2},{4,5},{5,4},{6,7},{7,6},{8,9},{9,8},{10,11... | collective-permute-start | bytes 196616 | tf_op jit(solution)/shard_map/ppermute | solution.py:782
  104.2 20.9 %collective-permute-start.12 = (f32[8,2048]{1,0:T(8,128)S(1)}, f32[8,2048]{1,0:T(8,128)S(1)}, u32[]{:S(2)}, u32[]{:S(2)}) collective-permute-start(f32[8,2048]{1,0:T(8,128)S(1)} %get-tuple-element.145.rest_0_.stats_a), channel_id=1, source_target_pairs={{0,2},{1,3},{2,0},{3,1},{4,6},{5,7},{6,4},{7,5},{8,10},{9,11},{10,... | collective-permute-start | bytes 196616 | tf_op jit(solution)/shard_map/ppermute | solution.py:782
  105.7 19.4 %collective-permute-start.13 = (f32[8,2048]{1,0:T(8,128)S(1)}, f32[8,2048]{1,0:T(8,128)S(1)}, u32[]{:S(2)}, u32[]{:S(2)}) collective-permute-start(f32[8,2048]{1,0:T(8,128)S(1)} %get-tuple-element.145.rest_0_.stats_a), channel_id=1, source_target_pairs={{0,3},{1,2},{2,1},{3,0},{4,7},{5,6},{6,5},{7,4},{8,11},{9,10},{10,... | collective-permute-start | bytes 196616 | tf_op jit(solution)/shard_map/ppermute | solution.py:782
  124.4 23.8 %collective-permute-start.24 = (bf16[1024,768]{1,0:T(8,128)(2,1)}, bf16[1024,768]{1,0:T(8,128)(2,1)}, u32[]{:S(2)}, u32[]{:S(2)}) collective-permute-start(bf16[1024,768]{1,0:T(8,128)(2,1)} %get-tuple-element.158), channel_id=1, source_target_pairs={{0,1},{1,0},{2,3},{3,2},{4,5},{5,4},{6,7},{7,6},{8,9},{9,8},{10,11... | collective-permute-start | bytes 4718600 | tf_op jit(solution)/shard_map/ppermute | solution.py:782
  143.7 29.6 %collective-permute-start.20 = (bf16[1024,768]{1,0:T(8,128)(2,1)}, bf16[1024,768]{1,0:T(8,128)(2,1)}, u32[]{:S(2)}, u32[]{:S(2)}) collective-permute-start(bf16[1024,768]{1,0:T(8,128)(2,1)} %get-tuple-element.155), channel_id=1, source_target_pairs={{0,1},{1,0},{2,3},{3,2},{4,5},{5,4},{6,7},{7,6},{8,9},{9,8},{10,11... | collective-permute-start | bytes 4718600 | tf_op jit(solution)/shard_map/ppermute | solution.py:782
  148.2 23.4 %collective-permute-start.60 = (bf16[768,384]{1,0:T(8,128)(2,1)S(1)}, bf16[768,384]{1,0:T(8,128)(2,1)S(1)}, u32[]{:S(2)}, u32[]{:S(2)}) collective-permute-start(bf16[768,384]{1,0:T(8,128)(2,1)S(1)} %constant_dynamic-slice_fusion.2), channel_id=1, source_target_pairs={{0,4},{4,0},{8,12},{12,8},{16,20},{20,16},{24,28},{28,24},{1,5},{5... | collective-permute-start | bytes 1769480 | tf_op jit(solution)/shard_map/ppermute | solution.py:782
  153.3 23.4 %collective-permute-start.17 = (bf16[144,384]{1,0:T(8,128)(2,1)S(1)}, bf16[144,384]{1,0:T(8,128)(2,1)S(1)}, u32[]{:S(2)}, u32[]{:S(2)}) collective-permute-start(bf16[144,384]{1,0:T(8,128)(2,1)S(1)} %get-tuple-element.153.rest_4_), channel_id=1, source_target_pairs={{4,0},{8,4},{12,8},{16,12},{20,16},{24,20},{28,24},{5,1},{9,5},{13... | collective-permute-start | bytes 331784 | tf_op jit(solution)/shard_map/ppermute | solution.py:788
  154.6 23.4 %collective-permute-start.18 = (bf16[144,384]{1,0:T(8,128)(2,1)S(1)}, bf16[144,384]{1,0:T(8,128)(2,1)S(1)}, u32[]{:S(2)}, u32[]{:S(2)}) collective-permute-start(bf16[144,384]{1,0:T(8,128)(2,1)S(1)} %get-tuple-element.153.rest_4_), channel_id=1, source_target_pairs={{8,0},{12,4},{16,8},{20,12},{24,16},{28,20},{9,1},{13,5},{17,9},{2... | collective-permute-start | bytes 331784 | tf_op jit(solution)/shard_map/ppermute | solution.py:788
  156.7 41.5 %collective-permute-start.29 = (bf16[1024,768]{1,0:T(8,128)(2,1)S(1)}, bf16[1024,768]{1,0:T(8,128)(2,1)}, u32[]{:S(2)}, u32[]{:S(2)}) collective-permute-start(bf16[1024,768]{1,0:T(8,128)(2,1)S(1)} %add_convert_fusion.4.rest_3_), channel_id=1, source_target_pairs={{0,2},{1,3},{2,0},{3,1},{4,6},{5,7},{6,4},{7,5},{8,10},{9,11},{10,... | collective-permute-start | bytes 4718600 | tf_op jit(solution)/shard_map/ppermute | solution.py:782
  171.6 11.2 %collective-permute-start.19 = (bf16[144,384]{1,0:T(8,128)(2,1)S(1)}, bf16[144,384]{1,0:T(8,128)(2,1)S(1)}, u32[]{:S(2)}, u32[]{:S(2)}) collective-permute-start(bf16[144,384]{1,0:T(8,128)(2,1)S(1)} %get-tuple-element.153.rest_4_), channel_id=1, source_target_pairs={{12,0},{16,4},{20,8},{24,12},{28,16},{13,1},{17,5},{21,9},{25,13},... | collective-permute-start | bytes 331784 | tf_op jit(solution)/shard_map/ppermute | solution.py:788
  173.3 28.1 %collective-permute-start.27 = (bf16[144,384]{1,0:T(8,128)(2,1)S(1)}, bf16[144,384]{1,0:T(8,128)(2,1)S(1)}, u32[]{:S(2)}, u32[]{:S(2)}) collective-permute-start(bf16[144,384]{1,0:T(8,128)(2,1)S(1)} %get-tuple-element.175), channel_id=1, source_target_pairs={{12,0},{16,4},{20,8},{24,12},{28,16},{13,1},{17,5},{21,9},{25,13},... | collective-permute-start | bytes 331784 | tf_op jit(solution)/shard_map/ppermute | solution.py:788
  176.7 36.5 %collective-permute-start.28 = (bf16[144,384]{1,0:T(8,128)(2,1)S(1)}, bf16[144,384]{1,0:T(8,128)(2,1)S(1)}, u32[]{:S(2)}, u32[]{:S(2)}) collective-permute-start(bf16[144,384]{1,0:T(8,128)(2,1)S(1)} %get-tuple-element.175), channel_id=1, source_target_pairs={{24,0},{28,4},{25,1},{29,5},{26,2},{30,6},{27,3},{31,7}} | collective-permute-start | bytes 331784 | tf_op jit(solution)/shard_map/ppermute | solution.py:788
  178.0 18.8 %collective-permute-start.61 = (bf16[384,384]{1,0:T(8,128)(2,1)S(1)}, bf16[384,384]{1,0:T(8,128)(2,1)S(1)}, u32[]{:S(2)}, u32[]{:S(2)}) collective-permute-start(bf16[384,384]{1,0:T(8,128)(2,1)S(1)} %constant_dynamic-slice_fusion.1), channel_id=1, source_target_pairs={{0,8},{4,12},{8,0},{12,4},{16,24},{20,28},{24,16},{28,20},{1,9},{5... | collective-permute-start | bytes 884744 | tf_op jit(solution)/shard_map/ppermute | solution.py:782
  182.8 55.2 %collective-permute-start.31 = (bf16[1024,768]{1,0:T(8,128)(2,1)S(1)}, bf16[1024,768]{1,0:T(8,128)(2,1)S(1)}, u32[]{:S(2)}, u32[]{:S(2)}) collective-permute-start(bf16[1024,768]{1,0:T(8,128)(2,1)S(1)} %add_convert_fusion.5.rest_3_), channel_id=1, source_target_pairs={{0,2},{1,3},{2,0},{3,1},{4,6},{5,7},{6,4},{7,5},{8,10},{9,11},{10,... | collective-permute-start | bytes 4718600 | tf_op jit(solution)/shard_map/ppermute | solution.py:782
  196.8 46.0 %collective-permute-start.25 = (bf16[144,384]{1,0:T(8,128)(2,1)S(1)}, bf16[144,384]{1,0:T(8,128)(2,1)S(1)}, u32[]{:S(2)}, u32[]{:S(2)}) collective-permute-start(bf16[144,384]{1,0:T(8,128)(2,1)S(1)} %get-tuple-element.166), channel_id=1, source_target_pairs={{12,0},{16,4},{20,8},{24,12},{28,16},{13,1},{17,5},{21,9},{25,13},... | collective-permute-start | bytes 331784 | tf_op jit(solution)/shard_map/ppermute | solution.py:788
  198.2 44.6 %collective-permute-start.26 = (bf16[144,384]{1,0:T(8,128)(2,1)S(1)}, bf16[144,384]{1,0:T(8,128)(2,1)S(1)}, u32[]{:S(2)}, u32[]{:S(2)}) collective-permute-start(bf16[144,384]{1,0:T(8,128)(2,1)S(1)} %get-tuple-element.166), channel_id=1, source_target_pairs={{24,0},{28,4},{25,1},{29,5},{26,2},{30,6},{27,3},{31,7}} | collective-permute-start | bytes 331784 | tf_op jit(solution)/shard_map/ppermute | solution.py:788
  201.5 35.4 %collective-permute-start.62 = (bf16[192,384]{1,0:T(8,128)(2,1)S(1)}, bf16[192,384]{1,0:T(8,128)(2,1)S(1)}, u32[]{:S(2)}, u32[]{:S(2)}) collective-permute-start(bf16[192,384]{1,0:T(8,128)(2,1)S(1)} %constant_dynamic-slice_fusion), channel_id=1, source_target_pairs={{0,16},{4,20},{8,24},{12,28},{16,0},{20,4},{24,8},{28,12},{1,17},{... | collective-permute-start | bytes 442376 | tf_op jit(solution)/shard_map/ppermute | solution.py:782
  213.2 99.7 %collective-permute-start.35 = (bf16[1024,768]{1,0:T(8,128)(2,1)S(1)}, bf16[1024,768]{1,0:T(8,128)(2,1)S(1)}, u32[]{:S(2)}, u32[]{:S(2)}) collective-permute-start(bf16[1024,768]{1,0:T(8,128)(2,1)S(1)} %add_convert_fusion.3.rest_4_.mine), channel_id=1, source_target_pairs={{0,1},{1,0},{2,3},{3,2},{4,5},{5,4},{6,7},{7,6},{8,9},{9,8},{10,11... | collective-permute-start | bytes 4718600 | tf_op jit(solution)/shard_map/ppermute | solution.py:782
  236.9 20.9 %collective-permute-start.63 = (bf16[192,384]{1,0:T(8,128)(2,1)S(1)}, bf16[192,384]{1,0:T(8,128)(2,1)S(1)}, u32[]{:S(2)}, u32[]{:S(2)}) collective-permute-start(bf16[192,384]{1,0:T(8,128)(2,1)S(1)} %add_convert_fusion.13), channel_id=1, source_target_pairs={{0,16},{4,20},{8,24},{12,28},{16,0},{20,4},{24,8},{28,12},{1,17},{... | collective-permute-start | bytes 442376 | tf_op jit(solution)/shard_map/ppermute | solution.py:782
  242.8 70.1 %collective-permute-start.36 = (bf16[1024,768]{1,0:T(8,128)(2,1)S(1)}, bf16[1024,768]{1,0:T(8,128)(2,1)S(1)}, u32[]{:S(2)}, u32[]{:S(2)}) collective-permute-start(bf16[1024,768]{1,0:T(8,128)(2,1)S(1)} %add_convert_fusion.2.rest_0_.mine), channel_id=1, source_target_pairs={{0,1},{1,0},{2,3},{3,2},{4,5},{5,4},{6,7},{7,6},{8,9},{9,8},{10,11... | collective-permute-start | bytes 4718600 | tf_op jit(solution)/shard_map/ppermute | solution.py:782
  257.4 13.3 %collective-permute-start.32 = (bf16[1024,768]{1,0:T(8,128)(2,1)}, bf16[1024,768]{1,0:T(8,128)(2,1)}, u32[]{:S(2)}, u32[]{:S(2)}) collective-permute-start(bf16[1024,768]{1,0:T(8,128)(2,1)} %constant_dynamic-slice_fusion.11), channel_id=1, source_target_pairs={{0,1},{1,0},{2,3},{3,2},{4,5},{5,4},{6,7},{7,6},{8,9},{9,8},{10,11... | collective-permute-start | bytes 4718600 | tf_op jit(solution)/shard_map/ppermute | solution.py:782
  268.7 32.7 %collective-permute-start.65 = (bf16[768,384]{1,0:T(8,128)(2,1)}, bf16[768,384]{1,0:T(8,128)(2,1)S(1)}, u32[]{:S(2)}, u32[]{:S(2)}) collective-permute-start(bf16[768,384]{1,0:T(8,128)(2,1)} %pad_maximum_fusion), channel_id=1, source_target_pairs={{0,4},{4,0},{8,12},{12,8},{16,20},{20,16},{24,28},{28,24},{1,5},{5... | collective-permute-start | bytes 1769480 | tf_op jit(solution)/shard_map/ppermute | solution.py:782
  274.1 35.8 %collective-permute-start.34 = (bf16[1024,768]{1,0:T(8,128)(2,1)}, bf16[1024,768]{1,0:T(8,128)(2,1)S(1)}, u32[]{:S(2)}, u32[]{:S(2)}) collective-permute-start(bf16[1024,768]{1,0:T(8,128)(2,1)} %add_convert_fusion.1.rest_5_), channel_id=1, source_target_pairs={{0,2},{1,3},{2,0},{3,1},{4,6},{5,7},{6,4},{7,5},{8,10},{9,11},{10,... | collective-permute-start | bytes 4718600 | tf_op jit(solution)/shard_map/ppermute | solution.py:782
  301.5 20.3 %collective-permute-start.33 = (f32[16,640]{1,0:T(8,128)S(1)}, f32[16,640]{1,0:T(8,128)S(1)}, u32[]{:S(2)}, u32[]{:S(2)}) collective-permute-start(f32[16,640]{1,0:T(8,128)S(1)} %get-tuple-element.191), channel_id=1, source_target_pairs={{4,0},{8,4},{12,8},{16,12},{20,16},{24,20},{28,24},{5,1},{9,5},{13... | collective-permute-start | bytes 122888 | tf_op jit(solution)/shard_map/ppermute | solution.py:788
  312.9 21.6 %collective-permute-start.38 = (bf16[1024,768]{1,0:T(8,128)(2,1)}, bf16[1024,768]{1,0:T(8,128)(2,1)}, u32[]{:S(2)}, u32[]{:S(2)}) collective-permute-start(bf16[1024,768]{1,0:T(8,128)(2,1)} %add_convert_fusion.rest_1_.mine), channel_id=1, source_target_pairs={{0,1},{1,0},{2,3},{3,2},{4,5},{5,4},{6,7},{7,6},{8,9},{9,8},{10,11... | collective-permute-start | bytes 4718600 | tf_op jit(solution)/shard_map/ppermute | solution.py:782
  330.3 13.8 %collective-permute-start.40 = (bf16[512,768]{1,0:T(8,128)(2,1)}, bf16[512,768]{1,0:T(8,128)(2,1)}, u32[]{:S(2)}, u32[]{:S(2)}) collective-permute-start(bf16[512,768]{1,0:T(8,128)(2,1)} %constant_dynamic-slice_fusion.7), channel_id=1, source_target_pairs={{0,1},{1,0},{2,3},{3,2},{4,5},{5,4},{6,7},{7,6},{8,9},{9,8},{10,11... | collective-permute-start | bytes 2359304 | tf_op jit(solution)/shard_map/ppermute | solution.py:782
  333.0 24.5 %collective-permute-start.44 = (bf16[512,768]{1,0:T(8,128)(2,1)S(1)}, bf16[512,768]{1,0:T(8,128)(2,1)}, u32[]{:S(2)}, u32[]{:S(2)}) collective-permute-start(bf16[512,768]{1,0:T(8,128)(2,1)S(1)} %add_convert_fusion.9.rest_3_), channel_id=1, source_target_pairs={{0,2},{1,3},{2,0},{3,1},{4,6},{5,7},{6,4},{7,5},{8,10},{9,11},{10,... | collective-permute-start | bytes 2359304 | tf_op jit(solution)/shard_map/ppermute | solution.py:782
  342.5 13.2 %collective-permute-start.39 = (bf16[384,640]{1,0:T(8,128)(2,1)}, bf16[384,640]{1,0:T(8,128)(2,1)}, u32[]{:S(2)}, u32[]{:S(2)}) collective-permute-start(bf16[384,640]{1,0:T(8,128)(2,1)} %get-tuple-element.265), channel_id=1, source_target_pairs={{0,4},{4,0},{8,12},{12,8},{16,20},{20,16},{24,28},{28,24},{1,5},{5... | collective-permute-start | bytes 1474568 | tf_op jit(solution)/shard_map/ppermute | solution.py:782
  359.1 50.1 %collective-permute-start.50 = (bf16[512,768]{1,0:T(8,128)(2,1)S(1)}, bf16[512,768]{1,0:T(8,128)(2,1)}, u32[]{:S(2)}, u32[]{:S(2)}) collective-permute-start(bf16[512,768]{1,0:T(8,128)(2,1)S(1)} %add_convert_fusion.7.rest_1_.mine), channel_id=1, source_target_pairs={{0,1},{1,0},{2,3},{3,2},{4,5},{5,4},{6,7},{7,6},{8,9},{9,8},{10,11... | collective-permute-start | bytes 2359304 | tf_op jit(solution)/shard_map/ppermute | solution.py:782
  359.2 22.4 %collective-permute-start.48 = (bf16[512,768]{1,0:T(8,128)(2,1)}, bf16[512,768]{1,0:T(8,128)(2,1)}, u32[]{:S(2)}, u32[]{:S(2)}) collective-permute-start(bf16[512,768]{1,0:T(8,128)(2,1)} %add_convert_fusion.8), channel_id=1, source_target_pairs={{0,2},{1,3},{2,0},{3,1},{4,6},{5,7},{6,4},{7,5},{8,10},{9,11},{10,... | collective-permute-start | bytes 2359304 | tf_op jit(solution)/shard_map/ppermute | solution.py:782
  362.4 15.8 %collective-permute-start.41 = (bf16[96,640]{1,0:T(8,128)(2,1)S(1)}, bf16[96,640]{1,0:T(8,128)(2,1)S(1)}, u32[]{:S(2)}, u32[]{:S(2)}) collective-permute-start(bf16[96,640]{1,0:T(8,128)(2,1)S(1)} %get-tuple-element.275), channel_id=1, source_target_pairs={{0,8},{4,12},{8,0},{12,4},{16,24},{20,28},{24,16},{28,20},{1,9},{5... | collective-permute-start | bytes 368648 | tf_op jit(solution)/shard_map/ppermute | solution.py:782
  363.1 15.1 %collective-permute-start.42 = (bf16[96,640]{1,0:T(8,128)(2,1)S(1)}, bf16[96,640]{1,0:T(8,128)(2,1)S(1)}, u32[]{:S(2)}, u32[]{:S(2)}) collective-permute-start(bf16[96,640]{1,0:T(8,128)(2,1)S(1)} %get-tuple-element.274), channel_id=1, source_target_pairs={{0,16},{4,20},{8,24},{12,28},{16,0},{20,4},{24,8},{28,12},{1,17},{... | collective-permute-start | bytes 368648 | tf_op jit(solution)/shard_map/ppermute | solution.py:782
  387.8 15.0 %collective-permute-start.51 = (bf16[96,512]{1,0:T(8,128)(2,1)S(1)}, bf16[96,512]{1,0:T(8,128)(2,1)S(1)}, u32[]{:S(2)}, u32[]{:S(2)}) collective-permute-start(bf16[96,512]{1,0:T(8,128)(2,1)S(1)} %get-tuple-element.260.rest_2_), channel_id=1, source_target_pairs={{0,8},{4,12},{8,0},{12,4},{16,24},{20,28},{24,16},{28,20},{1,9},{5... | collective-permute-start | bytes 294920 | tf_op jit(solution)/shard_map/ppermute | solution.py:782
  388.3 11.8 %collective-permute-start.58 = (f32[16,128]{1,0:T(8,128)S(1)}, f32[16,128]{1,0:T(8,128)S(1)}, u32[]{:S(2)}, u32[]{:S(2)}) collective-permute-start(f32[16,128]{1,0:T(8,128)S(1)} %slice.158), channel_id=1, source_target_pairs={{0,2},{1,3},{2,0},{3,1},{4,6},{5,7},{6,4},{7,5},{8,10},{9,11},{10,... | collective-permute-start | bytes 24584 | tf_op jit(solution)/shard_map/ppermute | solution.py:782
  390.1 11.0 %collective-permute-start.59 = (f32[16,128]{1,0:T(8,128)S(1)}, f32[16,128]{1,0:T(8,128)S(1)}, u32[]{:S(2)}, u32[]{:S(2)}) collective-permute-start(f32[16,128]{1,0:T(8,128)S(1)} %slice.158), channel_id=1, source_target_pairs={{0,3},{1,2},{2,1},{3,0},{4,7},{5,6},{6,5},{7,4},{8,11},{9,10},{10,... | collective-permute-start | bytes 24584 | tf_op jit(solution)/shard_map/ppermute | solution.py:782
  401.0 24.6 %collective-permute-start.49 = (bf16[512,768]{1,0:T(8,128)(2,1)S(1)}, bf16[512,768]{1,0:T(8,128)(2,1)S(1)}, u32[]{:S(2)}, u32[]{:S(2)}) collective-permute-start(bf16[512,768]{1,0:T(8,128)(2,1)S(1)} %add_convert_fusion.6.rest_2_.mine), channel_id=1, source_target_pairs={{0,1},{1,0},{2,3},{3,2},{4,5},{5,4},{6,7},{7,6},{8,9},{9,8},{10,11... | collective-permute-start | bytes 2359304 | tf_op jit(solution)/shard_map/ppermute | solution.py:782
  (81 other events, 683.8 us)
